TPU v7x, 32 devices: a whole 2x2x4 slice. The times are simulated.
32 devices in a mesh: chain: 2 (over x), blk: 16 (over z, y, core).
Axes of the slice: x: 2, y: 2, z: 4, core: 2. Of those that a mesh axis runs over, the one named last changes fastest.
Arguments:
- ratings: bfloat16 [3, 65536, 768], P(None, ('chain', 'blk')), parts along dimension 1, may hold values from -4 to 4
- tile_mask: int32 [3, 512, 6], P(None, ('chain', 'blk')), parts along dimension 1, may hold values 0 or 1
- user_factors: float32 [65536, 256], P(('chain', 'blk')), parts along dimension 0, may hold values from -1.5 to 1.5
- user_momentum: float32 [65536, 256], P(('chain', 'blk')), parts along dimension 0, may hold values from -6 to 6
- item_factors: float32 [24576, 256], P(('chain', 'blk')), parts along dimension 0, may hold values from -1.5 to 1.5
- item_momentum: float32 [24576, 256], P(('chain', 'blk')), parts along dimension 0, may hold values from -6 to 6
- user_noise: bfloat16 [3, 65536, 256], P(None, ('chain', 'blk')), parts along dimension 1, may hold values from -6 to 6
- item_noise: bfloat16 [3, 24576, 256], P(None, ('chain', 'blk')), parts along dimension 1, may hold values from -6 to 6
- wishart_user: float32 [512, 256], P('chain'), parts along dimension 0, as said below
- wishart_item: float32 [512, 256], P('chain'), parts along dimension 0, as said below
Outputs:
- user_factors_out: float32 [65536, 256], P(('chain', 'blk')), parts along dimension 0
- user_momentum_out: float32 [65536, 256], P(('chain', 'blk')), parts along dimension 0
- item_factors_out: float32 [24576, 256], P(('chain', 'blk')), parts along dimension 0
- item_momentum_out: float32 [24576, 256], P(('chain', 'blk')), parts along dimension 0
- user_precision: float32 [512, 256], P('chain'), parts along dimension 0
- item_precision: float32 [512, 256], P('chain'), parts along dimension 0
There are 2 independent parts, one for each index of `chain`. A program takes and returns all parts, laid end to end along the dimension named above; each array names one. Nothing has to cross between parts.
Inputs may be any that keep to these rules, and one draw needn't show every extreme that they name: `wishart_user`: lower triangular with a positive diagonal. `wishart_item`: lower triangular with a positive diagonal.
All inputs are finite; a program needn't handle non-finite values. No bound on the sum of `tile_mask` on one device may be relied on, other than what follows from the above.
Results may differ from a plain program's by a relative error of at most 0.00064.
Values sent between devices are 32-bit elements; how exact they have to be, the bound alone decides.
No kernel may reach another device: no remote copies, remote signals or barrier semaphores. Data moves between devices by JAX's collectives and lax.ppermute only.
A program may use at most 128 MiB of HBM per device.

v0:
```python
import functools

import jax
import jax.numpy as jnp
from jax import lax
from jax.experimental import pallas as pl
from jax.experimental.pallas import tpu as pltpu
from jax.sharding import PartitionSpec as P

TILE = 128
SUBSTEPS = 3
RANK = 256
HALF = 128
LANES = 8
PACKED = 208
RATE = 0.005
DECAY = 0.8
HIGHEST = lax.Precision.HIGHEST
F32 = jnp.float32
BF16 = jnp.bfloat16
VMEM = pl.BlockSpec(memory_space=pltpu.VMEM)
ANY = pl.BlockSpec(memory_space=pl.ANY)
SMEM = pl.BlockSpec(memory_space=pltpu.SMEM)


def dot(a, b, ca, cb, precision=None):
    return lax.dot_general(
        a, b, (((ca,), (cb,)), ((), ())), precision=precision, preferred_element_type=F32
    )


def params(mib=16):
    return pltpu.CompilerParams(vmem_limit_bytes=mib << 20)


def shape(rows, columns, dtype=F32):
    return jax.ShapeDtypeStruct((rows, columns), dtype)


def call(kernel, outs, in_specs, scratch=(), near=True):
    cost = pl.CostEstimate(flops=1000, bytes_accessed=1000, transcendentals=0)
    space = (lambda o: pltpu.VMEM(o.shape, o.dtype)) if near else (lambda o: o)
    run = pl.pallas_call(
        kernel,
        out_shape=jax.tree.map(space, outs),
        in_specs=in_specs,
        out_specs=jax.tree.map(lambda _: VMEM, outs),
        scratch_shapes=list(scratch),
        compiler_params=params(),
        cost_estimate=cost,
    )

    def placed(*args):
        spaces = {id(ANY): pltpu.HBM, id(VMEM): pltpu.VMEM}
        return run(
            *(
                pltpu.with_memory_space_constraint(a, spaces[id(s)]) if id(s) in spaces else a
                for a, s in zip(args, in_specs)
            )
        )

    return placed


def split(x):
    high = x.astype(BF16)
    rest = x - high.astype(F32)
    mid = rest.astype(BF16)
    low = (rest - mid.astype(F32)).astype(BF16)
    return high, mid, low


def split_rows(precision):
    high, mid, low = split(-precision)
    return jnp.concatenate([high, high, high, mid, mid, low], 0)


def split_columns(x):
    high, mid, low = split(x)
    return [high, mid, low, high, mid, high]


def gram_of(x):
    high, mid, low = split(x)
    cross = dot(high, mid, 0, 0) + dot(high, low, 0, 0)
    return (dot(mid, mid, 0, 0) + (cross + cross.T)) + dot(high, high, 0, 0)


def store_packed(ref, gram, total):
    ref[0:HALF, 0:HALF] = gram[0:HALF, 0:HALF]
    ref[0:HALF, HALF:] = gram[HALF:, 0:HALF]
    ref[HALF : HALF + 64, 0:HALF] = gram[HALF : HALF + 64, HALF:]
    ref[HALF : HALF + 64, HALF:] = gram[HALF + 64 :, HALF:]
    ref[HALF + 64 :] = jnp.broadcast_to(total, (PACKED - HALF - 64, RANK))


def gram_kernel(core_ref, mask_ref, u_hbm, w_hbm, *refs):
    sems = refs[-1]
    count = (len(refs) - 5) // 2
    others, (keep_ref, send_ref, u_ref, w_ref) = refs[:count], refs[count : count + 4]
    nears = refs[count + 4 : -1]
    first = core_ref[0] == 0
    rows = u_ref.shape[0] // 2
    copies = [pltpu.make_async_copy(w_hbm, w_ref, sems.at[0])]
    for j in range(2):
        part = pl.ds(j * rows, rows)
        copies.append(pltpu.make_async_copy(u_hbm.at[part], u_ref.at[part], sems.at[j + 1]))
    for j, (far, near) in enumerate(zip(others, nears)):
        source = far if len(far.shape) == 2 else far.at[0]
        copies.append(pltpu.make_async_copy(source, near, sems.at[j + 3]))
    for copy in copies:
        copy.start()
    copies[0].wait()
    item = w_ref[...]
    gram_i = gram_of(item)
    total_i = jnp.sum(item, 0, keepdims=True)
    gram_u, total_u = 0.0, 0.0
    for j in range(2):
        copies[j + 1].wait()
        user = u_ref[j * rows : (j + 1) * rows]
        gram_u += gram_of(user)
        total_u += jnp.sum(user, 0, keepdims=True)
    store_packed(
        keep_ref, jnp.where(first, gram_u, gram_i), jnp.where(first, total_u, total_i)
    )
    store_packed(
        send_ref, jnp.where(first, gram_i, gram_u), jnp.where(first, total_i, total_u)
    )
    for copy in copies[3:]:
        copy.wait()


def grams(core, mask, users, items, others):
    packed = shape(PACKED, RANK)
    nears = [shape(*x.shape[-2:], x.dtype) for x in others]
    return call(
        gram_kernel,
        (packed, packed, shape(*users.shape), shape(*items.shape), *nears),
        [SMEM, SMEM, ANY, ANY] + [ANY] * len(others),
        [pltpu.SemaphoreType.DMA((3 + len(others),))],
    )(core, mask, users, items, *others)


def halves_kernel(core_ref, keep_ref, got_ref, mine_ref, send_ref):
    lower = core_ref[1] == 0
    rows = mine_ref.shape[0]
    both = keep_ref[...] + got_ref[...]
    mine_ref[...] = jnp.where(lower, both[:rows], both[rows:])
    send_ref[...] = jnp.where(lower, both[rows:], both[:rows])


def halves(core, keep, got):
    half = shape(PACKED // 2, RANK)
    return call(halves_kernel, (half, half), [SMEM, VMEM, VMEM])(core, keep, got)


def sum_kernel(a_ref, b_ref, out_ref):
    out_ref[...] = a_ref[...] + b_ref[...]


def added(a, b):
    return call(sum_kernel, shape(*a.shape), [VMEM, VMEM])(a, b)


def inverse_factor(x):
    count = HALF // LANES
    tile = (LANES, HALF)
    rows = [x[LANES * q : LANES * (q + 1)] for q in range(count)]
    sub = lax.broadcasted_iota(jnp.int32, tile, 0)
    lane = lax.broadcasted_iota(jnp.int32, tile, 1)
    done = []
    for p in range(count):
        k = LANES * p
        cols = [
            [jnp.broadcast_to(rows[q][:, k + c : k + c + 1], tile) for q in range(p, count)]
            for c in range(LANES)
        ]
        panel = (lane >= k) & (lane < k + LANES)
        rows[p] = jnp.where(panel, jnp.where(lane - k == sub, 1.0, 0.0), rows[p])
        for q in range(p + 1, count):
            rows[q] = jnp.where(panel, 0.0, rows[q])
        scale = jnp.zeros(tile, F32)
        for i in range(LANES):
            pivot = jnp.broadcast_to(cols[i][0][i : i + 1], tile)
            inverse = 1.0 / pivot
            scale = jnp.where(sub == i, pivot, scale)
            factor = [v * inverse for v in cols[i]]
            factor[0] = jnp.where(sub > i, factor[0], 0.0)
            for c in range(i + 1, LANES):
                row = jnp.broadcast_to(cols[c][0][i : i + 1], tile)
                for q in range(count - p):
                    cols[c][q] = cols[c][q] - factor[q] * row
            row = jnp.broadcast_to(rows[p][i : i + 1], tile)
            for q in range(count - p):
                rows[p + q] = rows[p + q] - factor[q] * row
        done.append(jnp.where(lane < k + LANES, rows[p] * lax.rsqrt(scale), 0.0))
    return jnp.concatenate(done, 0)


def draw_kernel(counts, core_ref, mine_ref, other_ref, wu_ref, wi_ref, out_ref):
    first = core_ref[0] == 0
    lower = core_ref[1] == 0
    n = jnp.where(first, counts[0], counts[1])
    mine, other = mine_ref[...], other_ref[...]
    packed = jnp.concatenate(
        [jnp.where(lower, mine, other), jnp.where(lower, other, mine)], 0
    )
    bartlett_top = jnp.where(first, wu_ref[0:HALF], wi_ref[0:HALF])
    bartlett_low = jnp.where(first, wu_ref[HALF:], wi_ref[HALF:])
    mean = packed[HALF + 64 : HALF + 72] / n
    outer = dot(mean * 0.125, mean, 0, 0, HIGHEST)
    factor = n * n / (2.0 + n)
    diag = lax.broadcasted_iota(jnp.int32, (HALF, HALF), 0) == lax.broadcasted_iota(
        jnp.int32, (HALF, HALF), 1
    )
    eye = jnp.where(diag, 1.0, 0.0)
    s11 = eye + packed[0:HALF, 0:HALF] - factor * outer[0:HALF, 0:HALF]
    s21 = packed[0:HALF, HALF:] - factor * outer[HALF:, 0:HALF]
    gram22 = jnp.concatenate(
        [packed[HALF : HALF + 64, 0:HALF], packed[HALF : HALF + 64, HALF:]], 0
    )
    s22 = eye + gram22 - factor * outer[HALF:, HALF:]
    g1 = inverse_factor(s11)
    l21 = dot(s21, g1, 1, 1, HIGHEST)
    s22 = s22 - dot(l21, l21, 1, 1, HIGHEST)
    top = dot(g1, bartlett_top, 0, 0, HIGHEST)
    carry = dot(l21, g1, 1, 0, HIGHEST)
    g2 = inverse_factor(s22)
    low = dot(g2, bartlett_low, 0, 0, HIGHEST)
    top = top - dot(carry, low, 0, 0, HIGHEST)
    both = jnp.concatenate([top, low], 0)
    out_ref[0:RANK] = dot(both, both, 1, 1, HIGHEST)
    out_ref[RANK:] = n * mean / (2.0 + n)


def draw(counts, core, mine, other, wishart_user, wishart_item):
    return call(
        functools.partial(draw_kernel, counts),
        shape(RANK + 8, RANK),
        [SMEM, VMEM, VMEM, VMEM, VMEM],
    )(core, mine, other, wishart_user, wishart_item)


def prior_of(users, core_ref, mine_ref, other_ref):
    take = (core_ref[0] == 0) == users
    precision = jnp.where(take, mine_ref[0:RANK], other_ref[0:RANK])
    center = jnp.where(take, mine_ref[RANK : RANK + 1], other_ref[RANK : RANK + 1])
    return split_rows(precision), center


def residue_into(res_ref, at, ratings_ref, mask_ref, substep, row, rows, low_u, low_w):
    predicted = dot(low_u, low_w, 1, 1)
    for a in range(rows // TILE):
        for j in range(low_w.shape[0] // TILE):
            ra = slice(at + a * TILE, at + (a + 1) * TILE)
            pa = slice(a * TILE, (a + 1) * TILE)
            ij = slice(j * TILE, (j + 1) * TILE)
            seen = mask_ref[substep, j, (row + at) // TILE + a].astype(F32)
            gap = ratings_ref[ra, ij].astype(F32) - predicted[pa, ij]
            res_ref[ra, ij] = (gap * seen).astype(BF16)


def first_kernel(weight, row, slots, mask_ref, ratings_ref, r_ref, un_ref, u_ref, w_ref, *refs):
    count = len(slots)
    fars, (rt_ref, acc_ref) = refs[:count], refs[count : count + 2]
    nears = refs[count + 2 : 2 * count + 2]
    res_ref, low_ref, sems = refs[2 * count + 2 :]
    copies = [
        pltpu.make_async_copy(far.at[slot], near, sems.at[j])
        for j, (slot, far, near) in enumerate(zip(slots, fars, nears))
    ]
    for copy in copies:
        copy.start()
    low_w = w_ref[...].astype(BF16)
    total = rt_ref.shape[0]
    here = slice(row, row + total)
    low_ref[...] = u_ref[here].astype(BF16)
    rows = 256
    for t in range(total // rows):
        low_u = low_ref[t * rows : (t + 1) * rows]
        residue_into(
            res_ref, t * rows, ratings_ref.at[here], mask_ref, 0, row, rows, low_u, low_w
        )
    acc_ref[...] = dot(low_ref[...], res_ref[...], 0, 0)
    like_u = dot(res_ref[...], low_w, 1, 0)
    rt_ref[...] = (
        DECAY * r_ref[here]
        + RATE * weight * like_u
        + jnp.sqrt(0.4) * un_ref[here].astype(F32)
    )
    for copy in copies:
        copy.wait()


def first_part(weight, row, rows, mask, ratings, user_mom, user_noise, users, items, later):
    k = users.shape[1]
    ni = items.shape[0]
    slots = tuple(slot for slot, _ in later)
    fars = [far for _, far in later]
    rt, acc, *nears = call(
        functools.partial(first_kernel, weight, row, slots),
        (shape(rows, k), shape(k, ni), *(shape(*x.shape[1:], x.dtype) for x in fars)),
        [SMEM, VMEM, VMEM, VMEM, VMEM, VMEM] + [ANY] * len(fars),
        [
            pltpu.VMEM((rows, ni), BF16),
            pltpu.VMEM((rows, k), BF16),
            pltpu.SemaphoreType.DMA((max(len(fars), 1),)),
        ],
    )(mask, ratings, user_mom, user_noise, users, items, *fars)
    return rt, acc, nears


def item_start_kernel(weight, q_ref, in_ref, *refs):
    accs, out_ref = refs[:-1], refs[-1]
    like = accs[0][...]
    for acc in accs[1:]:
        like = like + acc[...]
    out_ref[...] = (
        DECAY * q_ref[...] + RATE * weight * like.T + jnp.sqrt(0.4) * in_ref[...].astype(F32)
    )


def item_start(weight, item_mom, item_noise, accs):
    return call(
        functools.partial(item_start_kernel, weight),
        shape(*item_mom.shape),
        [VMEM] * (2 + len(accs)),
    )(item_mom, item_noise, *accs)


def finish_kernel(is_user, pieces, core_ref, mine_ref, other_ref, *refs):
    (x_out, m_out, rhs_ref), ins = refs[-3:], refs[:-3]
    rhs, center = prior_of(is_user, core_ref, mine_ref, other_ref)
    rhs_ref[...] = rhs
    rows = 256
    read = lambda piece, at, size: ins[piece[0]][piece[1] + at : piece[1] + at + size]
    base = 0
    for size, factors, momenta in pieces:
        for at in range(0, size, rows):
            step = min(rows, size - at)
            x = read(factors, at, step)
            columns = jnp.concatenate(split_columns(x - center), 1)
            m = read(momenta, at, step) + RATE * dot(columns, rhs_ref[...], 1, 0)
            m_out[base : base + step] = m
            x_out[base : base + step] = x + RATE * m
            base += step


def finish(is_user, core, mine, other, arrays, pieces):
    n, k = sum(p[0] for p in pieces), arrays[0].shape[1]
    return call(
        functools.partial(finish_kernel, is_user, pieces),
        (shape(n, k), shape(n, k)),
        [SMEM] + [VMEM] * (2 + len(arrays)),
        [pltpu.VMEM((6 * RANK, k), BF16)],
    )(core, mine, other, *arrays)


def items_kernel(
    weight,
    substep,
    mask_ref,
    core_ref,
    mine_ref,
    other_ref,
    ratings_ref,
    u_ref,
    w_ref,
    q_ref,
    in_ref,
    res_ref,
    q_out,
    low_ref,
):
    low_w = w_ref[...].astype(BF16)
    rows = 256
    for t in range(u_ref.shape[0] // rows):
        here = slice(t * rows, (t + 1) * rows)
        low_u = u_ref[here].astype(BF16)
        low_ref[here] = low_u
        residue_into(res_ref, t * rows, ratings_ref, mask_ref, substep, 0, rows, low_u, low_w)
    like = dot(low_ref[...], res_ref[...], 0, 0)
    rhs, center = prior_of(False, core_ref, mine_ref, other_ref)
    prior = dot(jnp.concatenate(split_columns(w_ref[...] - center), 1), rhs, 1, 0)
    q_out[...] = (
        DECAY * q_ref[...]
        + RATE * (weight * like.T + prior)
        + jnp.sqrt(0.4) * in_ref[...].astype(F32)
    )


def items_step(weight, substep, mask, core, mine, other, ratings, users, w, q, item_noise):
    n, k = users.shape
    ni = w.shape[0]
    return call(
        functools.partial(items_kernel, weight, substep),
        (shape(n, ni, BF16), shape(ni, k)),
        [SMEM, SMEM] + [VMEM] * 7,
        [pltpu.VMEM((n, k), BF16)],
    )(mask, core, mine, other, ratings, users, w, q, item_noise)


def users_kernel(
    weight,
    core_ref,
    mine_ref,
    other_ref,
    res_ref,
    w_ref,
    u_ref,
    r_ref,
    un_ref,
    u_out,
    r_out,
    *refs,
):
    draws, rhs_ref = refs[:-1], refs[-1]
    if draws:
        mine, other = mine_ref[0:RANK], other_ref[0:RANK]
        first = core_ref[0] == 0
        draws[0][...] = jnp.where(first, mine, other)
        draws[1][...] = jnp.where(first, other, mine)
    ni = w_ref.shape[0]
    rhs_ref[0:ni] = w_ref[...].astype(BF16)
    rhs, center = prior_of(True, core_ref, mine_ref, other_ref)
    rhs_ref[ni:] = rhs
    rows = 256
    for t in range(u_ref.shape[0] // rows):
        here = slice(t * rows, (t + 1) * rows)
        x = u_ref[here]
        columns = jnp.concatenate(split_columns(x - center), 1)
        like = dot(res_ref[here], rhs_ref[0:ni], 1, 0)
        r = (
            DECAY * r_ref[here]
            + RATE * (weight * like + dot(columns, rhs_ref[ni:], 1, 0))
            + jnp.sqrt(0.4) * un_ref[here].astype(F32)
        )
        r_out[here] = r
        u_out[here] = x + RATE * r


def users_step(weight, last, core, mine, other, res, w, users, user_mom, user_noise):
    n, k = users.shape
    ni = w.shape[0]
    return call(
        functools.partial(users_kernel, weight),
        (shape(n, k), shape(n, k)) + (shape(RANK, RANK),) * (2 * last),
        [SMEM] + [VMEM] * 7,
        [pltpu.VMEM((ni + 6 * RANK, k), BF16)],
        near=not last,
    )(core, mine, other, res, w, users, user_mom, user_noise)


def arrived_kernel(w_ref, q_ref, w_out, q_out, sum_ref, sems):
    first = pltpu.make_async_copy(q_ref, q_out, sems.at[0])
    first.start()
    sum_ref[...] = w_ref[...] + RATE * q_ref[...]
    second = pltpu.make_async_copy(sum_ref, w_out, sems.at[1])
    second.start()
    first.wait()
    second.wait()


def arrived(before, came):
    out = pltpu.HBM(came.shape, F32)
    return pl.pallas_call(
        arrived_kernel,
        out_shape=(out, out),
        in_specs=[VMEM, VMEM],
        out_specs=(ANY, ANY),
        scratch_shapes=[pltpu.VMEM(came.shape, F32), pltpu.SemaphoreType.DMA((2,))],
        compiler_params=params(),
        cost_estimate=pl.CostEstimate(flops=1000, bytes_accessed=1000, transcendentals=0),
    )(before, came)


def swapped(array, by, size):
    return lax.ppermute(array, "blk", [(i, i ^ by) for i in range(size)])


def local(
    ratings,
    tile_mask,
    user_factors,
    user_momentum,
    item_factors,
    item_momentum,
    user_noise,
    item_noise,
    wishart_user,
    wishart_item,
):
    blocks = lax.axis_size("blk")
    blk = lax.axis_index("blk")
    user_rows = user_factors.shape[0]
    item_rows = item_factors.shape[0]
    weight = 1.0 * blocks
    back = [(i, (i - 1) % blocks) for i in range(blocks)]
    shift = lambda array: lax.ppermute(array, "blk", back)
    fence = lax.optimization_barrier

    odd = blk % 2
    half = (blk // 2) % 2
    core = jnp.stack([odd, half]).astype(jnp.int32)

    mask = tile_mask.transpose(0, 2, 1)
    parts = 4
    rows = user_rows // parts
    rts, accs, loaded = [], [], []
    later = [
        [(1, ratings)],
        [(2, ratings)],
        [(1, user_noise), (2, user_noise)],
        [(1, item_noise), (2, item_noise)],
    ]

    head = item_rows // 2
    early_w = shift(item_factors)

    keep, send, near_u, near_w, near_ratings, near_r, near_un, near_q, near_in, wu, wi = grams(
        core,
        mask,
        user_factors,
        item_factors,
        (
            ratings,
            user_momentum,
            user_noise,
            item_momentum,
            item_noise,
            wishart_user,
            wishart_item,
        ),
    )
    got = swapped(send, 1, blocks)
    mine, send = halves(core, keep, got)

    def part():
        j = len(rts)
        rt, acc, nears = first_part(
            weight,
            j * rows,
            rows,
            mask,
            near_ratings,
            near_r,
            near_un,
            near_u,
            near_w,
            later[j],
        )
        rts.append(rt)
        accs.append(acc)
        loaded.extend(nears)

    by = 2
    while by < blocks:
        send, near_u = fence((send, near_u))
        got = swapped(send, by, blocks)
        if len(rts) < parts:
            part()
            got, rts[-1], accs[-1] = fence((got, rts[-1], accs[-1]))
        if by == 2:
            got, early_w = fence((got, early_w))
        mine = added(mine, got)
        send = mine
        by = by * 2
    send, near_u = fence((send, near_u))
    other = swapped(send, 2, blocks)
    while len(rts) < parts:
        part()
    item_part = item_start(weight, near_q, near_in, accs)
    other, item_part, *rts = fence((other, item_part, *rts))
    early_q = shift(item_part)
    near_ratings = [None, *loaded[0:2]]
    near_un = [None, *loaded[2:4]]
    near_in = [None, *loaded[4:6]]

    counts = (1.0 * user_rows * blocks, 1.0 * item_rows * blocks)
    drawn = draw(counts, core, mine, other, wu, wi)
    peer = swapped(drawn, 1, blocks)

    users, user_mom = finish(
        True,
        core,
        drawn,
        peer,
        (near_u, *rts),
        tuple((rows, (0, j * rows), (1 + j, 0)) for j in range(parts)),
    )
    items, item_mom = finish(
        False,
        core,
        drawn,
        peer,
        (early_w, early_q),
        ((item_rows, (0, 0), (1, 0)),),
    )
    for substep in range(1, SUBSTEPS):
        last = substep == SUBSTEPS - 1
        before = shift(items)
        res, item_next = items_step(
            weight,
            substep,
            mask,
            core,
            drawn,
            peer,
            near_ratings[substep],
            users,
            items,
            item_mom,
            near_in[substep],
        )
        came = shift(item_next)
        users, user_mom, *precisions = users_step(
            weight, last, core, drawn, peer, res, items, users, user_mom, near_un[substep]
        )
        if not last:
            came, before, users, user_mom = fence((came, before, users, user_mom))
            items = before + RATE * came
            item_mom = came
    items, item_mom = arrived(before, came)
    return (users, user_mom, items, item_mom, *precisions)


def solution(mesh):
    placed = (
        P(None, ("chain", "blk"), None),
        P(None, ("chain", "blk"), None),
        P(("chain", "blk"), None),
        P(("chain", "blk"), None),
        P(("chain", "blk"), None),
        P(("chain", "blk"), None),
        P(None, ("chain", "blk"), None),
        P(None, ("chain", "blk"), None),
        P("chain", None),
        P("chain", None),
    )
    return jax.shard_map(
        local,
        mesh=mesh,
        in_specs=placed,
        out_specs=(
            P(("chain", "blk"), None),
            P(("chain", "blk"), None),
            P(("chain", "blk"), None),
            P(("chain", "blk"), None),
            P("chain", None),
            P("chain", None),
        ),
        check_vma=False,
    )
```

profile of v0, /device:TPU:0, one launch (start us, length us, event | category | flops | bytes accessed | tf_op | source)
XLA Modules:
  0.0 106.8 jit_solution(10363468984419837954)
XLA Ops:
  0.6 5.5 %collective-permute-start.2 = (f32[768,256]{1,0:T(8,128)}, f32[768,256]{1,0:T(8,128)S(1)}, u32[]{:S(2)}, u32[]{:S(2)}) collective-permute-start(f32[768,256]{1,0:T(8,128)} %w_hbm.1), channel_id=1, source_target_pairs={{0,15},{1,0},{2,1},{3,2},{4,3},{5,4},{6,5},{7,6},{8,7},{9,8},{10,9... | collective-permute-start | bytes 2359304 | tf_op jit(solution)/shard_map/ppermute | solution.py:499
  6.2 0.7 copy-done
  6.9 4.9 %shard_map.145 = (f32[208,256]{1,0:T(8,128)S(1)}, f32[208,256]{1,0:T(8,128)S(1)}, f32[2048,256]{1,0:T(8,128)S(1)}, f32[768,256]{1,0:T(8,128)S(1)}, bf16[2048,768...) custom-call(s32[2]{0:T(128)S(1)} %pad_add_fusion.core_ref, ...), custom_call_target="tpu_custom_call" | custom-call | flops 1000 | bytes 1000 | tf_op jit(solution)/shard_map/pallas_call | solution.py:55
  11.9 1.5 %collective-permute-done.got_ref = f32[208,256]{1,0:T(8,128)S(1)} collective-permute-done((f32[208,256]{1,0:T(8,128)S(1)}, f32[208,256]{1,0:T(8,128)S(1)}, u32[]{:S(2)}, u32[]{:S(2)}) %collective-permute-start) | collective-permute-done | bytes 213024 | tf_op jit(solution)/shard_map/ppermute | solution.py:478
  13.3 0.6 shard_map.146
  14.0 3.4 %shard_map.147 = (f32[512,256]{1,0:T(8,128)S(1)}, f32[256,768]{1,0:T(8,128)S(1)}, bf16[2048,768]{1,0:T(8,128)(2,1)S(1)}) custom-call(s32[3,6,16]{2,1,0:T(8,128)S(1)} %bitcast.4, bf16[2048,768]{1,0:T(8,128)(2,1)S(1)} %get-tuple-element.84.ratings_ref, f32[2048,256]{1,0:T(8,128)S(1)} %get-tuple-element.85.r_ref, ...), custom_call_target="tpu_custom_call" | custom-call | flops 1000 | bytes 1000 | tf_op jit(solution)/shard_map/pallas_call | solution.py:55
  17.4 1.6 %collective-permute-done.1.b_ref = f32[104,256]{1,0:T(8,128)S(1)} collective-permute-done((f32[104,256]{1,0:T(8,128)S(1)}, f32[104,256]{1,0:T(8,128)S(1)}, u32[]{:S(2)}, u32[]{:S(2)}) %collective-permute-start.1) | collective-permute-done | bytes 106528 | tf_op jit(solution)/shard_map/ppermute | solution.py:478
  19.1 3.4 %shard_map.149 = (f32[512,256]{1,0:T(8,128)S(1)}, f32[256,768]{1,0:T(8,128)S(1)}, bf16[2048,768]{1,0:T(8,128)(2,1)S(1)}) custom-call(s32[3,6,16]{2,1,0:T(8,128)S(1)} %bitcast.5, bf16[2048,768]{1,0:T(8,128)(2,1)S(1)} %get-tuple-element.84.ratings_ref, f32[2048,256]{1,0:T(8,128)S(1)} %get-tuple-element.85.r_ref, ...), custom_call_target="tpu_custom_call" | custom-call | flops 1000 | bytes 1000 | tf_op jit(solution)/shard_map/pallas_call | solution.py:55
  22.5 1.3 %collective-permute-done.3.b_ref = f32[104,256]{1,0:T(8,128)S(1)} collective-permute-done((f32[104,256]{1,0:T(8,128)S(1)}, f32[104,256]{1,0:T(8,128)S(1)}, u32[]{:S(2)}, u32[]{:S(2)}) %collective-permute-start.3) | collective-permute-done | bytes 106528 | tf_op jit(solution)/shard_map/ppermute | solution.py:478
  23.8 1.8 %collective-permute-start.4 = (f32[104,256]{1,0:T(8,128)S(1)}, f32[104,256]{1,0:T(8,128)S(1)}, u32[]{:S(2)}, u32[]{:S(2)}) collective-permute-start(f32[104,256]{1,0:T(8,128)S(1)} %shard_map.150.a_ref), channel_id=1, source_target_pairs={{0,8},{1,9},{2,10},{3,11},{4,12},{5,13},{6,14},{7,15},{8,0},{9,1},... | collective-permute-start | bytes 319496 | tf_op jit(solution)/shard_map/ppermute | solution.py:478
  25.6 2.6 %shard_map.151 = (f32[512,256]{1,0:T(8,128)S(1)}, f32[256,768]{1,0:T(8,128)S(1)}, bf16[2048,256]{1,0:T(8,128)(2,1)S(1)}, bf16[2048,256]{1,0:T(8,128)(2,1)S(1)}) custom-call(s32[3,6,16]{2,1,0:T(8,128)S(1)} %bitcast.6, bf16[2048,768]{1,0:T(8,128)(2,1)S(1)} %get-tuple-element.84.ratings_ref, f32[2048,256]{1,0:T(8,128)S(1)} %get-tuple-element.85.r_ref, ...), custom_call_target="tpu_custom_call" | custom-call | flops 1000 | bytes 1000 | tf_op jit(solution)/shard_map/pallas_call | solution.py:55
  28.2 2.5 %collective-permute-done.4.b_ref = f32[104,256]{1,0:T(8,128)S(1)} collective-permute-done((f32[104,256]{1,0:T(8,128)S(1)}, f32[104,256]{1,0:T(8,128)S(1)}, u32[]{:S(2)}, u32[]{:S(2)}) %collective-permute-start.4) | collective-permute-done | bytes 106528 | tf_op jit(solution)/shard_map/ppermute | solution.py:478
  30.8 2.5 %collective-permute-start.5 = (f32[104,256]{1,0:T(8,128)S(1)}, f32[104,256]{1,0:T(8,128)S(1)}, u32[]{:S(2)}, u32[]{:S(2)}) collective-permute-start(f32[104,256]{1,0:T(8,128)S(1)} %shard_map.152.mine_ref), channel_id=1, source_target_pairs={{0,2},{1,3},{2,0},{3,1},{4,6},{5,7},{6,4},{7,5},{8,10},{9,11},{10,... | collective-permute-start | bytes 319496 | tf_op jit(solution)/shard_map/ppermute | solution.py:478
  33.3 2.2 %shard_map.153 = (f32[512,256]{1,0:T(8,128)S(1)}, f32[256,768]{1,0:T(8,128)S(1)}, bf16[768,256]{1,0:T(8,128)(2,1)S(1)}, bf16[768,256]{1,0:T(8,128)(2,1)S(1)}) custom-call(s32[3,6,16]{2,1,0:T(8,128)S(1)} %bitcast.7, bf16[2048,768]{1,0:T(8,128)(2,1)S(1)} %get-tuple-element.84.ratings_ref, f32[2048,256]{1,0:T(8,128)S(1)} %get-tuple-element.85.r_ref, ...), custom_call_target="tpu_custom_call" | custom-call | flops 1000 | bytes 1000 | tf_op jit(solution)/shard_map/pallas_call | solution.py:55
  35.5 0.4 shard_map.154
  35.9 0.2 collective-permute-done.5.other_ref
  36.1 2.3 %collective-permute-start.7 = (f32[768,256]{1,0:T(8,128)S(1)}, f32[768,256]{1,0:T(8,128)S(1)}, u32[]{:S(2)}, u32[]{:S(2)}) collective-permute-start(f32[768,256]{1,0:T(8,128)S(1)} %shard_map.154), channel_id=1, source_target_pairs={{0,15},{1,0},{2,1},{3,2},{4,3},{5,4},{6,5},{7,6},{8,7},{9,8},{10,9... | collective-permute-start | bytes 2359304 | tf_op jit(solution)/shard_map/ppermute | solution.py:499
  38.4 11.0 %shard_map.155.mine_ref = f32[264,256]{1,0:T(8,128)S(1)} custom-call(s32[2]{0:T(128)S(1)} %pad_add_fusion.core_ref, f32[104,256]{1,0:T(8,128)S(1)} %shard_map.152.mine_ref, f32[104,256]{1,0:T(8,128)S(1)} %collective-permute-done.5.other_ref, f32[256,256]{1,0:T(8,128)S(1)} %get-tuple-element.116.wu_ref, f32[256,256]{1,0:T(8,128)S(1)} %get-tuple-element.117.wi_ref), custom_call_target="tpu_custom_call" | custom-call | flops 1000 | bytes 1000 | tf_op jit(solution)/shard_map/pallas_call | solution.py:55
  49.5 1.5 %collective-permute-done.6.other_ref = f32[264,256]{1,0:T(8,128)S(1)} collective-permute-done((f32[264,256]{1,0:T(8,128)S(1)}, f32[264,256]{1,0:T(8,128)S(1)}, u32[]{:S(2)}, u32[]{:S(2)}) %collective-permute-start.6) | collective-permute-done | bytes 270368 | tf_op jit(solution)/shard_map/ppermute | solution.py:478
  51.0 2.7 %shard_map.156 = (f32[2048,256]{1,0:T(8,128)S(1)}, f32[2048,256]{1,0:T(8,128)S(1)}) custom-call(s32[2]{0:T(128)S(1)} %pad_add_fusion.core_ref, f32[264,256]{1,0:T(8,128)S(1)} %shard_map.155.mine_ref, f32[264,256]{1,0:T(8,128)S(1)} %collective-permute-done.6.other_ref, f32[2048,256]{1,0:T(8,128)S(1)} %get-tuple-element.109.u_ref.refs_0_, ...), custom_call_target="tpu_custom_call" | custom-call | flops 1000 | bytes 1000 | tf_op jit(solution)/shard_map/pallas_call | solution.py:55
  53.7 1.4 %shard_map.157 = (f32[768,256]{1,0:T(8,128)S(1)}, f32[768,256]{1,0:T(8,128)S(1)}) custom-call(s32[2]{0:T(128)S(1)} %pad_add_fusion.core_ref, f32[264,256]{1,0:T(8,128)S(1)} %shard_map.155.mine_ref, f32[264,256]{1,0:T(8,128)S(1)} %collective-permute-done.6.other_ref, f32[768,256]{1,0:T(8,128)S(1)} %collective-permute-done.2.refs_0_, ...), custom_call_target="tpu_custom_call" | custom-call | flops 1000 | bytes 1000 | tf_op jit(solution)/shard_map/pallas_call | solution.py:55
  55.1 3.8 %shard_map.158 = (bf16[2048,768]{1,0:T(8,128)(2,1)S(1)}, f32[768,256]{1,0:T(8,128)S(1)}) custom-call(s32[3,6,16]{2,1,0:T(8,128)S(1)} %bitcast.8, s32[2]{0:T(128)S(1)} %pad_add_fusion.core_ref, f32[264,256]{1,0:T(8,128)S(1)} %shard_map.155.mine_ref, f32[264,256]{1,0:T(8,128)S(1)} %collective-permute-done.6.other_ref, ...), custom_call_target="tpu_custom_call" | custom-call | flops 1000 | bytes 1000 | tf_op jit(solution)/shard_map/pallas_call | solution.py:55
  59.0 2.3 %collective-permute-start.8 = (f32[768,256]{1,0:T(8,128)S(1)}, f32[768,256]{1,0:T(8,128)S(1)}, u32[]{:S(2)}, u32[]{:S(2)}) collective-permute-start(f32[768,256]{1,0:T(8,128)S(1)} %get-tuple-element.130), channel_id=1, source_target_pairs={{0,15},{1,0},{2,1},{3,2},{4,3},{5,4},{6,5},{7,6},{8,7},{9,8},{10,9... | collective-permute-start | bytes 2359304 | tf_op jit(solution)/shard_map/ppermute | solution.py:499
  61.4 3.6 %shard_map.159 = (f32[2048,256]{1,0:T(8,128)S(1)}, f32[2048,256]{1,0:T(8,128)S(1)}) custom-call(s32[2]{0:T(128)S(1)} %pad_add_fusion.core_ref, f32[264,256]{1,0:T(8,128)S(1)} %shard_map.155.mine_ref, f32[264,256]{1,0:T(8,128)S(1)} %collective-permute-done.6.other_ref, bf16[2048,768]{1,0:T(8,128)(2,1)S(1)} %get-tuple-element.131.res_ref, ...), custom_call_target="tpu_custom_call" | custom-call | flops 1000 | bytes 1000 | tf_op jit(solution)/shard_map/pallas_call | solution.py:55
  65.0 5.7 %collective-permute-done.8.q_ref = f32[768,256]{1,0:T(8,128)S(1)} collective-permute-done((f32[768,256]{1,0:T(8,128)S(1)}, f32[768,256]{1,0:T(8,128)S(1)}, u32[]{:S(2)}, u32[]{:S(2)}) %collective-permute-start.8) | collective-permute-done | bytes 786464 | tf_op jit(solution)/shard_map/ppermute | solution.py:499
  70.7 8.4 %collective-permute-done.9 = f32[768,256]{1,0:T(8,128)S(1)} collective-permute-done((f32[768,256]{1,0:T(8,128)S(1)}, f32[768,256]{1,0:T(8,128)S(1)}, u32[]{:S(2)}, u32[]{:S(2)}) %collective-permute-start.9) | collective-permute-done | bytes 786464 | tf_op jit(solution)/shard_map/ppermute | solution.py:499
  79.3 3.6 %shard_map.160 = (bf16[2048,768]{1,0:T(8,128)(2,1)S(1)}, f32[768,256]{1,0:T(8,128)S(1)}) custom-call(s32[3,6,16]{2,1,0:T(8,128)S(1)} %bitcast.9, s32[2]{0:T(128)S(1)} %pad_add_fusion.core_ref, f32[264,256]{1,0:T(8,128)S(1)} %shard_map.155.mine_ref, f32[264,256]{1,0:T(8,128)S(1)} %collective-permute-done.6.other_ref, ...), custom_call_target="tpu_custom_call" | custom-call | flops 1000 | bytes 1000 | tf_op jit(solution)/shard_map/pallas_call | solution.py:55
  82.9 4.6 %collective-permute-start.11 = (f32[768,256]{1,0:T(8,128)S(1)}, f32[768,256]{1,0:T(8,128)S(1)}, u32[]{:S(2)}, u32[]{:S(2)}) collective-permute-start(f32[768,256]{1,0:T(8,128)S(1)} %get-tuple-element.145), channel_id=1, source_target_pairs={{0,15},{1,0},{2,1},{3,2},{4,3},{5,4},{6,5},{7,6},{8,7},{9,8},{10,9... | collective-permute-start | bytes 2359304 | tf_op jit(solution)/shard_map/ppermute | solution.py:499
  87.6 5.8 %shard_map.161 = (f32[2048,256]{1,0:T(8,128)}, f32[2048,256]{1,0:T(8,128)}, f32[256,256]{1,0:T(8,128)}, f32[256,256]{1,0:T(8,128)}) custom-call(s32[2]{0:T(128)S(1)} %pad_add_fusion.core_ref, f32[264,256]{1,0:T(8,128)S(1)} %shard_map.155.mine_ref, f32[264,256]{1,0:T(8,128)S(1)} %collective-permute-done.6.other_ref, ...), custom_call_target="tpu_custom_call" | custom-call | flops 1000 | bytes 1000 | tf_op jit(solution)/shard_map/pallas_call | solution.py:55
  93.4 3.6 %collective-permute-done.11.q_ref = f32[768,256]{1,0:T(8,128)S(1)} collective-permute-done((f32[768,256]{1,0:T(8,128)S(1)}, f32[768,256]{1,0:T(8,128)S(1)}, u32[]{:S(2)}, u32[]{:S(2)}) %collective-permute-start.11) | collective-permute-done | bytes 786464 | tf_op jit(solution)/shard_map/ppermute | solution.py:499
  97.0 8.4 %collective-permute-done.10.w_ref = f32[768,256]{1,0:T(8,128)S(1)} collective-permute-done((f32[768,256]{1,0:T(8,128)S(1)}, f32[768,256]{1,0:T(8,128)S(1)}, u32[]{:S(2)}, u32[]{:S(2)}) %collective-permute-start.10) | collective-permute-done | bytes 786464 | tf_op jit(solution)/shard_map/ppermute | solution.py:499
  105.4 1.2 %shard_map.162 = (f32[768,256]{1,0:T(8,128)}, f32[768,256]{1,0:T(8,128)}) custom-call(f32[768,256]{1,0:T(8,128)S(1)} %collective-permute-done.10.w_ref, f32[768,256]{1,0:T(8,128)S(1)} %collective-permute-done.11.q_ref), custom_call_target="tpu_custom_call" | custom-call | flops 1000 | bytes 1000 | tf_op jit(solution)/shard_map/pallas_call | solution.py:466
  (16 shorter events, 0.7 us)
Async XLA Ops:
  0.6 18.3 %collective-permute-start.2 = (f32[768,256]{1,0:T(8,128)}, f32[768,256]{1,0:T(8,128)S(1)}, u32[]{:S(2)}, u32[]{:S(2)}) collective-permute-start(f32[768,256]{1,0:T(8,128)} %w_hbm.1), channel_id=1, source_target_pairs={{0,15},{1,0},{2,1},{3,2},{4,3},{5,4},{6,5},{7,6},{8,7},{9,8},{10,9... | collective-permute-start | bytes 2359304 | tf_op jit(solution)/shard_map/ppermute | solution.py:499
  6.2 0.7 copy-start
  6.9 7.1 %copy-start.1 = (s32[3,16,6]{1,2,0:T(8,128)S(1)}, s32[3,16,6]{1,2,0:T(8,128)}, u32[]{:S(2)}) copy-start(s32[3,16,6]{1,2,0:T(8,128)} %param.11) | copy-start | bytes 3460
  11.8 1.5 %collective-permute-start = (f32[208,256]{1,0:T(8,128)S(1)}, f32[208,256]{1,0:T(8,128)S(1)}, u32[]{:S(2)}, u32[]{:S(2)}) collective-permute-start(f32[208,256]{1,0:T(8,128)S(1)} %get-tuple-element.79), channel_id=1, source_target_pairs={{0,1},{1,0},{2,3},{3,2},{4,5},{5,4},{6,7},{7,6},{8,9},{9,8},{10,11... | collective-permute-start | bytes 638984 | tf_op jit(solution)/shard_map/ppermute | solution.py:478
  13.9 5.1 %collective-permute-start.1 = (f32[104,256]{1,0:T(8,128)S(1)}, f32[104,256]{1,0:T(8,128)S(1)}, u32[]{:S(2)}, u32[]{:S(2)}) collective-permute-start(f32[104,256]{1,0:T(8,128)S(1)} %get-tuple-element.83), channel_id=1, source_target_pairs={{0,2},{1,3},{2,0},{3,1},{4,6},{5,7},{6,4},{7,5},{8,10},{9,11},{10,... | collective-permute-start | bytes 319496 | tf_op jit(solution)/shard_map/ppermute | solution.py:478
  19.0 4.8 %collective-permute-start.3 = (f32[104,256]{1,0:T(8,128)S(1)}, f32[104,256]{1,0:T(8,128)S(1)}, u32[]{:S(2)}, u32[]{:S(2)}) collective-permute-start(f32[104,256]{1,0:T(8,128)S(1)} %shard_map.148.a_ref), channel_id=1, source_target_pairs={{0,4},{1,5},{2,6},{3,7},{4,0},{5,1},{6,2},{7,3},{8,12},{9,13},{10,... | collective-permute-start | bytes 319496 | tf_op jit(solution)/shard_map/ppermute | solution.py:478
  23.8 7.0 %collective-permute-start.4 = (f32[104,256]{1,0:T(8,128)S(1)}, f32[104,256]{1,0:T(8,128)S(1)}, u32[]{:S(2)}, u32[]{:S(2)}) collective-permute-start(f32[104,256]{1,0:T(8,128)S(1)} %shard_map.150.a_ref), channel_id=1, source_target_pairs={{0,8},{1,9},{2,10},{3,11},{4,12},{5,13},{6,14},{7,15},{8,0},{9,1},... | collective-permute-start | bytes 319496 | tf_op jit(solution)/shard_map/ppermute | solution.py:478
  30.8 5.3 %collective-permute-start.5 = (f32[104,256]{1,0:T(8,128)S(1)}, f32[104,256]{1,0:T(8,128)S(1)}, u32[]{:S(2)}, u32[]{:S(2)}) collective-permute-start(f32[104,256]{1,0:T(8,128)S(1)} %shard_map.152.mine_ref), channel_id=1, source_target_pairs={{0,2},{1,3},{2,0},{3,1},{4,6},{5,7},{6,4},{7,5},{8,10},{9,11},{10,... | collective-permute-start | bytes 319496 | tf_op jit(solution)/shard_map/ppermute | solution.py:478
  36.1 17.6 %collective-permute-start.7 = (f32[768,256]{1,0:T(8,128)S(1)}, f32[768,256]{1,0:T(8,128)S(1)}, u32[]{:S(2)}, u32[]{:S(2)}) collective-permute-start(f32[768,256]{1,0:T(8,128)S(1)} %shard_map.154), channel_id=1, source_target_pairs={{0,15},{1,0},{2,1},{3,2},{4,3},{5,4},{6,5},{7,6},{8,7},{9,8},{10,9... | collective-permute-start | bytes 2359304 | tf_op jit(solution)/shard_map/ppermute | solution.py:499
  49.4 1.6 %collective-permute-start.6 = (f32[264,256]{1,0:T(8,128)S(1)}, f32[264,256]{1,0:T(8,128)S(1)}, u32[]{:S(2)}, u32[]{:S(2)}) collective-permute-start(f32[264,256]{1,0:T(8,128)S(1)} %shard_map.155.mine_ref), channel_id=1, source_target_pairs={{0,1},{1,0},{2,3},{3,2},{4,5},{5,4},{6,7},{7,6},{8,9},{9,8},{10,11... | collective-permute-start | bytes 811016 | tf_op jit(solution)/shard_map/ppermute | solution.py:478
  59.0 11.8 %collective-permute-start.8 = (f32[768,256]{1,0:T(8,128)S(1)}, f32[768,256]{1,0:T(8,128)S(1)}, u32[]{:S(2)}, u32[]{:S(2)}) collective-permute-start(f32[768,256]{1,0:T(8,128)S(1)} %get-tuple-element.130), channel_id=1, source_target_pairs={{0,15},{1,0},{2,1},{3,2},{4,3},{5,4},{6,5},{7,6},{8,7},{9,8},{10,9... | collective-permute-start | bytes 2359304 | tf_op jit(solution)/shard_map/ppermute | solution.py:499
  61.2 17.9 %collective-permute-start.9 = (f32[768,256]{1,0:T(8,128)S(1)}, f32[768,256]{1,0:T(8,128)S(1)}, u32[]{:S(2)}, u32[]{:S(2)}) collective-permute-start(f32[768,256]{1,0:T(8,128)S(1)} %get-tuple-element.127.w_ref), channel_id=1, source_target_pairs={{0,15},{1,0},{2,1},{3,2},{4,3},{5,4},{6,5},{7,6},{8,7},{9,8},{10,9... | collective-permute-start | bytes 2359304 | tf_op jit(solution)/shard_map/ppermute | solution.py:499
  82.9 14.2 %collective-permute-start.11 = (f32[768,256]{1,0:T(8,128)S(1)}, f32[768,256]{1,0:T(8,128)S(1)}, u32[]{:S(2)}, u32[]{:S(2)}) collective-permute-start(f32[768,256]{1,0:T(8,128)S(1)} %get-tuple-element.145), channel_id=1, source_target_pairs={{0,15},{1,0},{2,1},{3,2},{4,3},{5,4},{6,5},{7,6},{8,7},{9,8},{10,9... | collective-permute-start | bytes 2359304 | tf_op jit(solution)/shard_map/ppermute | solution.py:499
  87.5 17.9 %collective-permute-start.10 = (f32[768,256]{1,0:T(8,128)S(1)}, f32[768,256]{1,0:T(8,128)S(1)}, u32[]{:S(2)}, u32[]{:S(2)}) collective-permute-start(f32[768,256]{1,0:T(8,128)S(1)} %multiply_add_fusion.w_ref), channel_id=1, source_target_pairs={{0,15},{1,0},{2,1},{3,2},{4,3},{5,4},{6,5},{7,6},{8,7},{9,8},{10,9... | collective-permute-start | bytes 2359304 | tf_op jit(solution)/shard_map/ppermute | solution.py:499
where the time goes:
time: 107 us
  Pallas kernels  50.7 us (47%)
  waiting for transfers between devices  34.8 us (33%)
  starting transfers between devices  19.5 us (18%)
    pallas_call x17, Pallas kernels, placed(): run(*(pltpu.with_memory_space_constraint(a, spaces[id(s)]) if id(s) in sp...  49.5 us
    ppermute x6, waiting for transfers between devices, local(): shift = lambda array: lax.ppermute(array, 'blk', back)  26.2 us
    ppermute x6, starting transfers between devices, local(): shift = lambda array: lax.ppermute(array, 'blk', back)  14.9 us
    ppermute x6, waiting for transfers between devices, swapped(): return lax.ppermute(array, 'blk', [(i, i ^ by) for i in range(size)])  8.56 us
    ppermute x6, starting transfers between devices, swapped(): return lax.ppermute(array, 'blk', [(i, i ^ by) for i in range(size)])  4.63 us
  transfers between devices with their start and end apart: 12, of which 10 were waited for; matrix products, arithmetic and copies ran while one was open for 0% of the time, Pallas kernels for 38%

commit v1 on v0

--- a/solution.py
+++ b/solution.py
@@ -62,6 +62,30 @@
     return placed
 
 
+CHUNKS = 4
+
+
+def fetches(slots, fars, nears, sems):
+    copies = []
+    for slot, far, near in zip(slots, fars, nears):
+        source = far if slot is None else far.at[slot]
+        rows = near.shape[0] // CHUNKS
+        for c in range(CHUNKS):
+            part = pl.ds(c * rows, rows)
+            copies.append(
+                pltpu.make_async_copy(source.at[part], near.at[part], sems.at[len(copies)])
+            )
+    return copies
+
+
+def near_shapes(later):
+    return [shape(*far.shape[-2:], far.dtype) for _, far in later]
+
+
+def fetch_sems(later, more=0):
+    return pltpu.SemaphoreType.DMA((max(CHUNKS * len(later) + more, 1),))
+
+
 def split(x):
     high = x.astype(BF16)
     rest = x - high.astype(F32)
@@ -94,9 +118,9 @@
     ref[HALF + 64 :] = jnp.broadcast_to(total, (PACKED - HALF - 64, RANK))
 
 
-def gram_kernel(core_ref, mask_ref, u_hbm, w_hbm, *refs):
+def gram_kernel(slots, core_ref, mask_ref, u_hbm, w_hbm, *refs):
     sems = refs[-1]
-    count = (len(refs) - 5) // 2
+    count = len(slots)
     others, (keep_ref, send_ref, u_ref, w_ref) = refs[:count], refs[count : count + 4]
     nears = refs[count + 4 : -1]
     first = core_ref[0] == 0
@@ -105,9 +129,7 @@
     for j in range(2):
         part = pl.ds(j * rows, rows)
         copies.append(pltpu.make_async_copy(u_hbm.at[part], u_ref.at[part], sems.at[j + 1]))
-    for j, (far, near) in enumerate(zip(others, nears)):
-        source = far if len(far.shape) == 2 else far.at[0]
-        copies.append(pltpu.make_async_copy(source, near, sems.at[j + 3]))
+    copies += fetches(slots, others, nears, sems.at[pl.ds(3, CHUNKS * count)])
     for copy in copies:
         copy.start()
     copies[0].wait()
@@ -130,15 +152,15 @@
         copy.wait()
 
 
-def grams(core, mask, users, items, others):
+def grams(core, mask, users, items, later):
     packed = shape(PACKED, RANK)
-    nears = [shape(*x.shape[-2:], x.dtype) for x in others]
+    slots, fars = zip(*later)
     return call(
-        gram_kernel,
-        (packed, packed, shape(*users.shape), shape(*items.shape), *nears),
-        [SMEM, SMEM, ANY, ANY] + [ANY] * len(others),
-        [pltpu.SemaphoreType.DMA((3 + len(others),))],
-    )(core, mask, users, items, *others)
+        functools.partial(gram_kernel, slots),
+        (packed, packed, shape(*users.shape), shape(*items.shape), *near_shapes(later)),
+        [SMEM, SMEM, ANY, ANY] + [ANY] * len(later),
+        [fetch_sems(later, 3)],
+    )(core, mask, users, items, *fars)
 
 
 def halves_kernel(core_ref, keep_ref, got_ref, mine_ref, send_ref):
@@ -260,15 +282,13 @@
             res_ref[ra, ij] = (gap * seen).astype(BF16)
 
 
-def first_kernel(weight, row, slots, mask_ref, ratings_ref, r_ref, un_ref, u_ref, w_ref, *refs):
+def first_kernel(weight, row, slots, noisy, mask_ref, ratings_ref, r_ref, u_ref, w_ref, *refs):
+    un_ref, refs = (refs[0], refs[1:]) if noisy else (None, refs)
     count = len(slots)
     fars, (rt_ref, acc_ref) = refs[:count], refs[count : count + 2]
     nears = refs[count + 2 : 2 * count + 2]
     res_ref, low_ref, sems = refs[2 * count + 2 :]
-    copies = [
-        pltpu.make_async_copy(far.at[slot], near, sems.at[j])
-        for j, (slot, far, near) in enumerate(zip(slots, fars, nears))
-    ]
+    copies = fetches(slots, fars, nears, sems)
     for copy in copies:
         copy.start()
     low_w = w_ref[...].astype(BF16)
@@ -283,6 +303,11 @@
         )
     acc_ref[...] = dot(low_ref[...], res_ref[...], 0, 0)
     like_u = dot(res_ref[...], low_w, 1, 0)
+    if un_ref is None:
+        for copy in copies:
+            copy.wait()
+        un_ref = nears[0]
+        copies = []
     rt_ref[...] = (
         DECAY * r_ref[here]
         + RATE * weight * like_u
@@ -292,40 +317,40 @@
         copy.wait()
 
 
-def first_part(weight, row, rows, mask, ratings, user_mom, user_noise, users, items, later):
+def first_part(weight, row, rows, mask, ratings, user_mom, users, items, noise, later):
     k = users.shape[1]
     ni = items.shape[0]
     slots = tuple(slot for slot, _ in later)
     fars = [far for _, far in later]
+    noise = [] if noise is None else [noise]
     rt, acc, *nears = call(
-        functools.partial(first_kernel, weight, row, slots),
-        (shape(rows, k), shape(k, ni), *(shape(*x.shape[1:], x.dtype) for x in fars)),
-        [SMEM, VMEM, VMEM, VMEM, VMEM, VMEM] + [ANY] * len(fars),
-        [
-            pltpu.VMEM((rows, ni), BF16),
-            pltpu.VMEM((rows, k), BF16),
-            pltpu.SemaphoreType.DMA((max(len(fars), 1),)),
-        ],
-    )(mask, ratings, user_mom, user_noise, users, items, *fars)
+        functools.partial(first_kernel, weight, row, slots, len(noise)),
+        (shape(rows, k), shape(k, ni), *near_shapes(later)),
+        [SMEM, VMEM, VMEM, VMEM, VMEM] + [VMEM] * len(noise) + [ANY] * len(fars),
+        [pltpu.VMEM((rows, ni), BF16), pltpu.VMEM((rows, k), BF16), fetch_sems(later)],
+    )(mask, ratings, user_mom, users, items, *noise, *fars)
     return rt, acc, nears
 
 
-def item_start_kernel(weight, q_ref, in_ref, *refs):
+def item_start_kernel(weight, w_ref, q_ref, in_ref, *refs):
     accs, out_ref = refs[:-1], refs[-1]
     like = accs[0][...]
     for acc in accs[1:]:
         like = like + acc[...]
-    out_ref[...] = (
+    ni = w_ref.shape[0]
+    out_ref[0:ni] = (
         DECAY * q_ref[...] + RATE * weight * like.T + jnp.sqrt(0.4) * in_ref[...].astype(F32)
     )
-
-
-def item_start(weight, item_mom, item_noise, accs):
+    out_ref[ni:] = w_ref[...]
+
+
+def item_start(weight, items, item_mom, item_noise, accs):
+    ni, k = item_mom.shape
     return call(
         functools.partial(item_start_kernel, weight),
-        shape(*item_mom.shape),
-        [VMEM] * (2 + len(accs)),
-    )(item_mom, item_noise, *accs)
+        shape(2 * ni, k),
+        [VMEM] * (3 + len(accs)),
+    )(items, item_mom, item_noise, *accs)
 
 
 def finish_kernel(is_user, pieces, core_ref, mine_ref, other_ref, *refs):
@@ -402,6 +427,7 @@
 
 def users_kernel(
     weight,
+    slots,
     core_ref,
     mine_ref,
     other_ref,
@@ -410,12 +436,18 @@
     u_ref,
     r_ref,
     un_ref,
-    u_out,
-    r_out,
     *refs,
 ):
-    draws, rhs_ref = refs[:-1], refs[-1]
-    if draws:
+    if slots:
+        count = len(slots)
+        fars, (u_out, r_out), nears = refs[:count], refs[count : count + 2], refs[count + 2 : -2]
+        rhs_ref, sems = refs[-2:]
+        copies = fetches(slots, fars, nears, sems)
+    else:
+        (u_out, r_out, *draws), rhs_ref, copies = refs[:-1], refs[-1], []
+    for copy in copies:
+        copy.start()
+    if not slots:
         mine, other = mine_ref[0:RANK], other_ref[0:RANK]
         first = core_ref[0] == 0
         draws[0][...] = jnp.where(first, mine, other)
@@ -437,18 +469,23 @@
         )
         r_out[here] = r
         u_out[here] = x + RATE * r
-
-
-def users_step(weight, last, core, mine, other, res, w, users, user_mom, user_noise):
+    for copy in copies:
+        copy.wait()
+
+
+def users_step(weight, later, core, mine, other, res, w, users, user_mom, user_noise):
     n, k = users.shape
     ni = w.shape[0]
+    slots = tuple(slot for slot, _ in later)
+    fars = [far for _, far in later]
+    more = near_shapes(later) if later else [shape(RANK, RANK)] * 2
     return call(
-        functools.partial(users_kernel, weight),
-        (shape(n, k), shape(n, k)) + (shape(RANK, RANK),) * (2 * last),
-        [SMEM] + [VMEM] * 7,
-        [pltpu.VMEM((ni + 6 * RANK, k), BF16)],
-        near=not last,
-    )(core, mine, other, res, w, users, user_mom, user_noise)
+        functools.partial(users_kernel, weight, slots),
+        (shape(n, k), shape(n, k), *more),
+        [SMEM] + [VMEM] * 7 + [ANY] * len(fars),
+        [pltpu.VMEM((ni + 6 * RANK, k), BF16)] + [fetch_sems(later)] * bool(later),
+        near=bool(later),
+    )(core, mine, other, res, w, users, user_mom, user_noise, *fars)
 
 
 def arrived_kernel(w_ref, q_ref, w_out, q_out, sum_ref, sems):
@@ -508,29 +545,18 @@
     rows = user_rows // parts
     rts, accs, loaded = [], [], []
     later = [
+        [(0, user_noise), (None, item_momentum), (0, item_noise)],
         [(1, ratings)],
-        [(2, ratings)],
-        [(1, user_noise), (2, user_noise)],
-        [(1, item_noise), (2, item_noise)],
+        [(1, user_noise), (1, item_noise)],
+        [(None, wishart_user), (None, wishart_item)],
     ]
 
-    head = item_rows // 2
-    early_w = shift(item_factors)
-
-    keep, send, near_u, near_w, near_ratings, near_r, near_un, near_q, near_in, wu, wi = grams(
+    keep, send, near_u, near_w, near_ratings, near_r = grams(
         core,
         mask,
         user_factors,
         item_factors,
-        (
-            ratings,
-            user_momentum,
-            user_noise,
-            item_momentum,
-            item_noise,
-            wishart_user,
-            wishart_item,
-        ),
+        [(0, ratings), (None, user_momentum)],
     )
     got = swapped(send, 1, blocks)
     mine, send = halves(core, keep, got)
@@ -544,14 +570,14 @@
             mask,
             near_ratings,
             near_r,
-            near_un,
             near_u,
             near_w,
+            loaded[0][0] if j else None,
             later[j],
         )
         rts.append(rt)
         accs.append(acc)
-        loaded.extend(nears)
+        loaded.append(nears)
 
     by = 2
     while by < blocks:
@@ -560,8 +586,6 @@
         if len(rts) < parts:
             part()
             got, rts[-1], accs[-1] = fence((got, rts[-1], accs[-1]))
-        if by == 2:
-            got, early_w = fence((got, early_w))
         mine = added(mine, got)
         send = mine
         by = by * 2
@@ -569,13 +593,11 @@
     other = swapped(send, 2, blocks)
     while len(rts) < parts:
         part()
-    item_part = item_start(weight, near_q, near_in, accs)
+    item_part = item_start(weight, near_w, loaded[0][1], loaded[0][2], accs)
     other, item_part, *rts = fence((other, item_part, *rts))
-    early_q = shift(item_part)
-    near_ratings = [None, *loaded[0:2]]
-    near_un = [None, *loaded[2:4]]
-    near_in = [None, *loaded[4:6]]
-
+    early = shift(item_part)
+    wu, wi = loaded[3]
+    near = {1: (loaded[1][0], *loaded[2])}
     counts = (1.0 * user_rows * blocks, 1.0 * item_rows * blocks)
     drawn = draw(counts, core, mine, other, wu, wi)
     peer = swapped(drawn, 1, blocks)
@@ -593,11 +615,13 @@
         core,
         drawn,
         peer,
-        (early_w, early_q),
-        ((item_rows, (0, 0), (1, 0)),),
+        (early,),
+        ((item_rows, (0, item_rows), (0, 0)),),
     )
     for substep in range(1, SUBSTEPS):
         last = substep == SUBSTEPS - 1
+        here_ratings, here_un, here_in = near[substep]
+        later = [] if last else [(substep + 1, x) for x in (ratings, user_noise, item_noise)]
         before = shift(items)
         res, item_next = items_step(
             weight,
@@ -606,22 +630,23 @@
             core,
             drawn,
             peer,
-            near_ratings[substep],
+            here_ratings,
             users,
             items,
             item_mom,
-            near_in[substep],
+            here_in,
         )
         came = shift(item_next)
-        users, user_mom, *precisions = users_step(
-            weight, last, core, drawn, peer, res, items, users, user_mom, near_un[substep]
+        users, user_mom, *more = users_step(
+            weight, later, core, drawn, peer, res, items, users, user_mom, here_un
         )
+        before, users, user_mom, *more = fence((before, users, user_mom, *more))
         if not last:
-            came, before, users, user_mom = fence((came, before, users, user_mom))
+            near[substep + 1] = more
             items = before + RATE * came
             item_mom = came
     items, item_mom = arrived(before, came)
-    return (users, user_mom, items, item_mom, *precisions)
+    return (users, user_mom, items, item_mom, *more)
 
 
 def solution(mesh):

time: 107 us -> 97.7 us (0.913)
  waiting for transfers between devices: 34.8 us -> 25.7 us
    ppermute x6, starting transfers between devices: 4.63 us -> 10.1 us  [swapped(): return lax.ppermute(array, 'blk', [(i, i ^ by) for i in range(size)])]
    ppermute x6 -> x5, waiting for transfers between devices: 26.2 us -> 21.2 us  [local(): shift = lambda array: lax.ppermute(array, 'blk', back)]
    ppermute x6 -> x5, starting transfers between devices: 14.9 us -> 9.94 us  [local(): shift = lambda array: lax.ppermute(array, 'blk', back)]
    ppermute x6, waiting for transfers between devices: 8.56 us -> 4.5 us  [swapped(): return lax.ppermute(array, 'blk', [(i, i ^ by) for i in range(size)])]
  transfers between devices with their start and end apart: 12 -> 11, of which waited for: 10 -> 8; matrix products, arithmetic and copies ran while one was open for 0% -> 0% of each run, Pallas kernels for 38% -> 43%
where the time goes in v1:
time: 97.7 us; the launch traced here: 97.4 us
  Pallas kernels  49.7 us (51%)
  waiting for transfers between devices  25.7 us (26%)
  starting transfers between devices  20.1 us (21%)
  between operations  1 us (1%)
    pallas_call x17, Pallas kernels, placed(): run(*(pltpu.with_memory_space_constraint(a, spaces[id(s)]) if id(s) in sp...  48.6 us
    ppermute x5, waiting for transfers between devices, local(): shift = lambda array: lax.ppermute(array, 'blk', back)  21.2 us
    ppermute x6, starting transfers between devices, swapped(): return lax.ppermute(array, 'blk', [(i, i ^ by) for i in range(size)])  10.1 us
    ppermute x5, starting transfers between devices, local(): shift = lambda array: lax.ppermute(array, 'blk', back)  9.94 us
    ppermute x6, waiting for transfers between devices, swapped(): return lax.ppermute(array, 'blk', [(i, i ^ by) for i in range(size)])  4.5 us
  transfers between devices with their start and end apart: 11, of which 8 were waited for; matrix products, arithmetic and copies ran while one was open for 0% of the time, Pallas kernels for 43%

profile of v1, /device:TPU:0, one launch (start us, length us, event | category | flops | bytes accessed | tf_op | source)
XLA Modules:
  0.0 97.4 jit_solution(5481480451831030571)
XLA Ops:
  0.7 0.7 copy-done
  1.4 4.3 %shard_map.145 = (f32[208,256]{1,0:T(8,128)S(1)}, f32[208,256]{1,0:T(8,128)S(1)}, f32[2048,256]{1,0:T(8,128)S(1)}, f32[768,256]{1,0:T(8,128)S(1)}, bf16[2048,768...) custom-call(s32[2]{0:T(128)S(1)} %pad_add_fusion.core_ref, s32[3,6,16]{2,1,0:T(8,128)S(1)} %bitcast.3, f32[2048,256]{1,0:T(8,128)} %u_hbm.1, ...), custom_call_target="tpu_custom_call" | custom-call | flops 1000 | bytes 1000 | tf_op jit(solution)/shard_map/pallas_call | solution.py:55
  5.8 0.5 collective-permute-start
  6.3 1.1 %collective-permute-done.got_ref = f32[208,256]{1,0:T(8,128)S(1)} collective-permute-done((f32[208,256]{1,0:T(8,128)S(1)}, f32[208,256]{1,0:T(8,128)S(1)}, u32[]{:S(2)}, u32[]{:S(2)}) %collective-permute-start) | collective-permute-done | bytes 213024 | tf_op jit(solution)/shard_map/ppermute | solution.py:515
  7.4 0.6 shard_map.146
  8.0 3.0 %collective-permute-start.1 = (f32[104,256]{1,0:T(8,128)S(1)}, f32[104,256]{1,0:T(8,128)S(1)}, u32[]{:S(2)}, u32[]{:S(2)}) collective-permute-start(f32[104,256]{1,0:T(8,128)S(1)} %get-tuple-element.88), channel_id=1, source_target_pairs={{0,2},{1,3},{2,0},{3,1},{4,6},{5,7},{6,4},{7,5},{8,10},{9,11},{10,... | collective-permute-start | bytes 319496 | tf_op jit(solution)/shard_map/ppermute | solution.py:515
  10.9 3.0 %shard_map.147 = (f32[512,256]{1,0:T(8,128)S(1)}, f32[256,768]{1,0:T(8,128)S(1)}, bf16[2048,256]{1,0:T(8,128)(2,1)S(1)}, f32[768,256]{1,0:T(8,128)S(1)}, bf16[768,256]{1,0:T(8,128)(2,1)S(1)}) custom-call(s32[3,6,16]{2,1,0:T(8,128)S(1)} %bitcast.4, bf16[2048,768]{1,0:T(8,128)(2,1)S(1)} %get-tuple-element.89.ratings_ref, ...), custom_call_target="tpu_custom_call" | custom-call | flops 1000 | bytes 1000 | tf_op jit(solution)/shard_map/pallas_call | solution.py:55
  14.2 1.9 %collective-permute-start.2 = (f32[104,256]{1,0:T(8,128)S(1)}, f32[104,256]{1,0:T(8,128)S(1)}, u32[]{:S(2)}, u32[]{:S(2)}) collective-permute-start(f32[104,256]{1,0:T(8,128)S(1)} %shard_map.148.a_ref), channel_id=1, source_target_pairs={{0,4},{1,5},{2,6},{3,7},{4,0},{5,1},{6,2},{7,3},{8,12},{9,13},{10,... | collective-permute-start | bytes 319496 | tf_op jit(solution)/shard_map/ppermute | solution.py:515
  16.1 3.0 %shard_map.149 = (f32[512,256]{1,0:T(8,128)S(1)}, f32[256,768]{1,0:T(8,128)S(1)}, bf16[2048,768]{1,0:T(8,128)(2,1)S(1)}) custom-call(s32[3,6,16]{2,1,0:T(8,128)S(1)} %bitcast.5, bf16[2048,768]{1,0:T(8,128)(2,1)S(1)} %get-tuple-element.89.ratings_ref, f32[2048,256]{1,0:T(8,128)S(1)} %get-tuple-element.90.r_ref, ...), custom_call_target="tpu_custom_call" | custom-call | flops 1000 | bytes 1000 | tf_op jit(solution)/shard_map/pallas_call | solution.py:55
  19.1 2.7 %collective-permute-start.3 = (f32[104,256]{1,0:T(8,128)S(1)}, f32[104,256]{1,0:T(8,128)S(1)}, u32[]{:S(2)}, u32[]{:S(2)}) collective-permute-start(f32[104,256]{1,0:T(8,128)S(1)} %shard_map.150.a_ref), channel_id=1, source_target_pairs={{0,8},{1,9},{2,10},{3,11},{4,12},{5,13},{6,14},{7,15},{8,0},{9,1},... | collective-permute-start | bytes 319496 | tf_op jit(solution)/shard_map/ppermute | solution.py:515
  21.9 2.8 %shard_map.151 = (f32[512,256]{1,0:T(8,128)S(1)}, f32[256,768]{1,0:T(8,128)S(1)}, bf16[2048,256]{1,0:T(8,128)(2,1)S(1)}, bf16[768,256]{1,0:T(8,128)(2,1)S(1)}) custom-call(s32[3,6,16]{2,1,0:T(8,128)S(1)} %bitcast.6, bf16[2048,768]{1,0:T(8,128)(2,1)S(1)} %get-tuple-element.89.ratings_ref, f32[2048,256]{1,0:T(8,128)S(1)} %get-tuple-element.90.r_ref, ...), custom_call_target="tpu_custom_call" | custom-call | flops 1000 | bytes 1000 | tf_op jit(solution)/shard_map/pallas_call | solution.py:55
  24.7 1.7 %collective-permute-done.3.b_ref = f32[104,256]{1,0:T(8,128)S(1)} collective-permute-done((f32[104,256]{1,0:T(8,128)S(1)}, f32[104,256]{1,0:T(8,128)S(1)}, u32[]{:S(2)}, u32[]{:S(2)}) %collective-permute-start.3) | collective-permute-done | bytes 106528 | tf_op jit(solution)/shard_map/ppermute | solution.py:515
  26.4 1.5 %collective-permute-start.4 = (f32[104,256]{1,0:T(8,128)S(1)}, f32[104,256]{1,0:T(8,128)S(1)}, u32[]{:S(2)}, u32[]{:S(2)}) collective-permute-start(f32[104,256]{1,0:T(8,128)S(1)} %shard_map.152.mine_ref), channel_id=1, source_target_pairs={{0,2},{1,3},{2,0},{3,1},{4,6},{5,7},{6,4},{7,5},{8,10},{9,11},{10,... | collective-permute-start | bytes 319496 | tf_op jit(solution)/shard_map/ppermute | solution.py:515
  27.9 2.6 %shard_map.153 = (f32[512,256]{1,0:T(8,128)S(1)}, f32[256,768]{1,0:T(8,128)S(1)}, f32[256,256]{1,0:T(8,128)S(1)}, f32[256,256]{1,0:T(8,128)S(1)}) custom-call(s32[3,6,16]{2,1,0:T(8,128)S(1)} %bitcast.7, bf16[2048,768]{1,0:T(8,128)(2,1)S(1)} %get-tuple-element.89.ratings_ref, f32[2048,256]{1,0:T(8,128)S(1)} %get-tuple-element.90.r_ref, ...), custom_call_target="tpu_custom_call" | custom-call | flops 1000 | bytes 1000 | tf_op jit(solution)/shard_map/pallas_call | solution.py:55
  30.5 0.4 shard_map.154
  30.9 0.3 collective-permute-done.4.other_ref
  31.2 11.0 %shard_map.155.mine_ref = f32[264,256]{1,0:T(8,128)S(1)} custom-call(s32[2]{0:T(128)S(1)} %pad_add_fusion.core_ref, f32[104,256]{1,0:T(8,128)S(1)} %shard_map.152.mine_ref, f32[104,256]{1,0:T(8,128)S(1)} %collective-permute-done.4.other_ref, f32[256,256]{1,0:T(8,128)S(1)} %get-tuple-element.120.wu_ref, f32[256,256]{1,0:T(8,128)S(1)} %get-tuple-element.121.wi_ref), custom_call_target="tpu_custom_call" | custom-call | flops 1000 | bytes 1000 | tf_op jit(solution)/shard_map/pallas_call | solution.py:55
  42.2 0.6 collective-permute-start.5
  42.8 1.2 %collective-permute-done.5.other_ref = f32[264,256]{1,0:T(8,128)S(1)} collective-permute-done((f32[264,256]{1,0:T(8,128)S(1)}, f32[264,256]{1,0:T(8,128)S(1)}, u32[]{:S(2)}, u32[]{:S(2)}) %collective-permute-start.5) | collective-permute-done | bytes 270368 | tf_op jit(solution)/shard_map/ppermute | solution.py:515
  43.9 5.2 %collective-permute-done.6.refs_0_ = f32[1536,256]{1,0:T(8,128)S(1)} collective-permute-done((f32[1536,256]{1,0:T(8,128)S(1)}, f32[1536,256]{1,0:T(8,128)S(1)}, u32[]{:S(2)}, u32[]{:S(2)}) %collective-permute-start.6) | collective-permute-done | bytes 1572896 | tf_op jit(solution)/shard_map/ppermute | solution.py:536
  49.1 1.4 %shard_map.156 = (f32[768,256]{1,0:T(8,128)S(1)}, f32[768,256]{1,0:T(8,128)S(1)}) custom-call(s32[2]{0:T(128)S(1)} %pad_add_fusion.core_ref, f32[264,256]{1,0:T(8,128)S(1)} %shard_map.155.mine_ref, f32[264,256]{1,0:T(8,128)S(1)} %collective-permute-done.5.other_ref, f32[1536,256]{1,0:T(8,128)S(1)} %collective-permute-done.6.refs_0_), custom_call_target="tpu_custom_call" | custom-call | flops 1000 | bytes 1000 | tf_op jit(solution)/shard_map/pallas_call | solution.py:55
  50.5 4.9 %collective-permute-start.7 = (f32[768,256]{1,0:T(8,128)S(1)}, f32[768,256]{1,0:T(8,128)S(1)}, u32[]{:S(2)}, u32[]{:S(2)}) collective-permute-start(f32[768,256]{1,0:T(8,128)S(1)} %get-tuple-element.123.w_ref), channel_id=1, source_target_pairs={{0,15},{1,0},{2,1},{3,2},{4,3},{5,4},{6,5},{7,6},{8,7},{9,8},{10,9... | collective-permute-start | bytes 2359304 | tf_op jit(solution)/shard_map/ppermute | solution.py:536
  55.4 2.7 %shard_map.157 = (f32[2048,256]{1,0:T(8,128)S(1)}, f32[2048,256]{1,0:T(8,128)S(1)}) custom-call(s32[2]{0:T(128)S(1)} %pad_add_fusion.core_ref, f32[264,256]{1,0:T(8,128)S(1)} %shard_map.155.mine_ref, f32[264,256]{1,0:T(8,128)S(1)} %collective-permute-done.5.other_ref, f32[2048,256]{1,0:T(8,128)S(1)} %get-tuple-element.113.u_ref.refs_0_, ...), custom_call_target="tpu_custom_call" | custom-call | flops 1000 | bytes 1000 | tf_op jit(solution)/shard_map/pallas_call | solution.py:55
  58.1 3.6 %shard_map.158 = (bf16[2048,768]{1,0:T(8,128)(2,1)S(1)}, f32[768,256]{1,0:T(8,128)S(1)}) custom-call(s32[3,6,16]{2,1,0:T(8,128)S(1)} %bitcast.8, s32[2]{0:T(128)S(1)} %pad_add_fusion.core_ref, f32[264,256]{1,0:T(8,128)S(1)} %shard_map.155.mine_ref, f32[264,256]{1,0:T(8,128)S(1)} %collective-permute-done.5.other_ref, ...), custom_call_target="tpu_custom_call" | custom-call | flops 1000 | bytes 1000 | tf_op jit(solution)/shard_map/pallas_call | solution.py:55
  61.7 3.8 %shard_map.159 = (f32[2048,256]{1,0:T(8,128)S(1)}, f32[2048,256]{1,0:T(8,128)S(1)}, bf16[2048,768]{1,0:T(8,128)(2,1)S(1)}, bf16[2048,256]{1,0:T(8,128)(2,1)S(1)}, bf16[768,256]{1,0:T(8,128)(2,1)S(1)}) custom-call(s32[2]{0:T(128)S(1)} %pad_add_fusion.core_ref, f32[264,256]{1,0:T(8,128)S(1)} %shard_map.155.mine_ref, ...), custom_call_target="tpu_custom_call" | custom-call | flops 1000 | bytes 1000 | tf_op jit(solution)/shard_map/pallas_call | solution.py:55
  65.5 7.8 %collective-permute-done.8.q_ref = f32[768,256]{1,0:T(8,128)S(1)} collective-permute-done((f32[768,256]{1,0:T(8,128)S(1)}, f32[768,256]{1,0:T(8,128)S(1)}, u32[]{:S(2)}, u32[]{:S(2)}) %collective-permute-start.8) | collective-permute-done | bytes 786464 | tf_op jit(solution)/shard_map/ppermute | solution.py:536
  73.4 4.7 %collective-permute-start.9 = (f32[768,256]{1,0:T(8,128)S(1)}, f32[768,256]{1,0:T(8,128)S(1)}, u32[]{:S(2)}, u32[]{:S(2)}) collective-permute-start(f32[768,256]{1,0:T(8,128)S(1)} %multiply_add_fusion.w_ref), channel_id=1, source_target_pairs={{0,15},{1,0},{2,1},{3,2},{4,3},{5,4},{6,5},{7,6},{8,7},{9,8},{10,9... | collective-permute-start | bytes 2359304 | tf_op jit(solution)/shard_map/ppermute | solution.py:536
  78.1 3.6 %shard_map.160 = (bf16[2048,768]{1,0:T(8,128)(2,1)S(1)}, f32[768,256]{1,0:T(8,128)S(1)}) custom-call(s32[3,6,16]{2,1,0:T(8,128)S(1)} %bitcast.9, s32[2]{0:T(128)S(1)} %pad_add_fusion.core_ref, f32[264,256]{1,0:T(8,128)S(1)} %shard_map.155.mine_ref, f32[264,256]{1,0:T(8,128)S(1)} %collective-permute-done.5.other_ref, ...), custom_call_target="tpu_custom_call" | custom-call | flops 1000 | bytes 1000 | tf_op jit(solution)/shard_map/pallas_call | solution.py:55
  81.7 0.3 collective-permute-start.10
  82.0 5.8 %shard_map.161 = (f32[2048,256]{1,0:T(8,128)}, f32[2048,256]{1,0:T(8,128)}, f32[256,256]{1,0:T(8,128)}, f32[256,256]{1,0:T(8,128)}) custom-call(s32[2]{0:T(128)S(1)} %pad_add_fusion.core_ref, f32[264,256]{1,0:T(8,128)S(1)} %shard_map.155.mine_ref, f32[264,256]{1,0:T(8,128)S(1)} %collective-permute-done.5.other_ref, ...), custom_call_target="tpu_custom_call" | custom-call | flops 1000 | bytes 1000 | tf_op jit(solution)/shard_map/pallas_call | solution.py:55
  87.8 8.2 %collective-permute-done.10.q_ref = f32[768,256]{1,0:T(8,128)S(1)} collective-permute-done((f32[768,256]{1,0:T(8,128)S(1)}, f32[768,256]{1,0:T(8,128)S(1)}, u32[]{:S(2)}, u32[]{:S(2)}) %collective-permute-start.10) | collective-permute-done | bytes 786464 | tf_op jit(solution)/shard_map/ppermute | solution.py:536
  96.0 1.2 %shard_map.162 = (f32[768,256]{1,0:T(8,128)}, f32[768,256]{1,0:T(8,128)}) custom-call(f32[768,256]{1,0:T(8,128)S(1)} %collective-permute-done.9.w_ref, f32[768,256]{1,0:T(8,128)S(1)} %collective-permute-done.10.q_ref), custom_call_target="tpu_custom_call" | custom-call | flops 1000 | bytes 1000 | tf_op jit(solution)/shard_map/pallas_call | solution.py:503
  (14 shorter events, 0.6 us)
Async XLA Ops:
  0.7 0.7 copy-start
  1.4 9.5 %copy-start.1 = (s32[3,16,6]{1,2,0:T(8,128)S(1)}, s32[3,16,6]{1,2,0:T(8,128)}, u32[]{:S(2)}) copy-start(s32[3,16,6]{1,2,0:T(8,128)} %param.11) | copy-start | bytes 3460
  5.8 1.6 %collective-permute-start = (f32[208,256]{1,0:T(8,128)S(1)}, f32[208,256]{1,0:T(8,128)S(1)}, u32[]{:S(2)}, u32[]{:S(2)}) collective-permute-start(f32[208,256]{1,0:T(8,128)S(1)} %get-tuple-element.84), channel_id=1, source_target_pairs={{0,1},{1,0},{2,3},{3,2},{4,5},{5,4},{6,7},{7,6},{8,9},{9,8},{10,11... | collective-permute-start | bytes 638984 | tf_op jit(solution)/shard_map/ppermute | solution.py:515
  8.0 6.2 %collective-permute-start.1 = (f32[104,256]{1,0:T(8,128)S(1)}, f32[104,256]{1,0:T(8,128)S(1)}, u32[]{:S(2)}, u32[]{:S(2)}) collective-permute-start(f32[104,256]{1,0:T(8,128)S(1)} %get-tuple-element.88), channel_id=1, source_target_pairs={{0,2},{1,3},{2,0},{3,1},{4,6},{5,7},{6,4},{7,5},{8,10},{9,11},{10,... | collective-permute-start | bytes 319496 | tf_op jit(solution)/shard_map/ppermute | solution.py:515
  14.2 4.9 %collective-permute-start.2 = (f32[104,256]{1,0:T(8,128)S(1)}, f32[104,256]{1,0:T(8,128)S(1)}, u32[]{:S(2)}, u32[]{:S(2)}) collective-permute-start(f32[104,256]{1,0:T(8,128)S(1)} %shard_map.148.a_ref), channel_id=1, source_target_pairs={{0,4},{1,5},{2,6},{3,7},{4,0},{5,1},{6,2},{7,3},{8,12},{9,13},{10,... | collective-permute-start | bytes 319496 | tf_op jit(solution)/shard_map/ppermute | solution.py:515
  19.1 7.2 %collective-permute-start.3 = (f32[104,256]{1,0:T(8,128)S(1)}, f32[104,256]{1,0:T(8,128)S(1)}, u32[]{:S(2)}, u32[]{:S(2)}) collective-permute-start(f32[104,256]{1,0:T(8,128)S(1)} %shard_map.150.a_ref), channel_id=1, source_target_pairs={{0,8},{1,9},{2,10},{3,11},{4,12},{5,13},{6,14},{7,15},{8,0},{9,1},... | collective-permute-start | bytes 319496 | tf_op jit(solution)/shard_map/ppermute | solution.py:515
  26.4 4.8 %collective-permute-start.4 = (f32[104,256]{1,0:T(8,128)S(1)}, f32[104,256]{1,0:T(8,128)S(1)}, u32[]{:S(2)}, u32[]{:S(2)}) collective-permute-start(f32[104,256]{1,0:T(8,128)S(1)} %shard_map.152.mine_ref), channel_id=1, source_target_pairs={{0,2},{1,3},{2,0},{3,1},{4,6},{5,7},{6,4},{7,5},{8,10},{9,11},{10,... | collective-permute-start | bytes 319496 | tf_op jit(solution)/shard_map/ppermute | solution.py:515
  31.2 17.9 %collective-permute-start.6 = (f32[1536,256]{1,0:T(8,128)S(1)}, f32[1536,256]{1,0:T(8,128)S(1)}, u32[]{:S(2)}, u32[]{:S(2)}) collective-permute-start(f32[1536,256]{1,0:T(8,128)S(1)} %shard_map.154), channel_id=1, source_target_pairs={{0,15},{1,0},{2,1},{3,2},{4,3},{5,4},{6,5},{7,6},{8,7},{9,8},{10,9... | collective-permute-start | bytes 4718600 | tf_op jit(solution)/shard_map/ppermute | solution.py:536
  42.2 1.7 %collective-permute-start.5 = (f32[264,256]{1,0:T(8,128)S(1)}, f32[264,256]{1,0:T(8,128)S(1)}, u32[]{:S(2)}, u32[]{:S(2)}) collective-permute-start(f32[264,256]{1,0:T(8,128)S(1)} %shard_map.155.mine_ref), channel_id=1, source_target_pairs={{0,1},{1,0},{2,3},{3,2},{4,5},{5,4},{6,7},{7,6},{8,9},{9,8},{10,11... | collective-permute-start | bytes 811016 | tf_op jit(solution)/shard_map/ppermute | solution.py:515
  50.5 15.0 %collective-permute-start.7 = (f32[768,256]{1,0:T(8,128)S(1)}, f32[768,256]{1,0:T(8,128)S(1)}, u32[]{:S(2)}, u32[]{:S(2)}) collective-permute-start(f32[768,256]{1,0:T(8,128)S(1)} %get-tuple-element.123.w_ref), channel_id=1, source_target_pairs={{0,15},{1,0},{2,1},{3,2},{4,3},{5,4},{6,5},{7,6},{8,7},{9,8},{10,9... | collective-permute-start | bytes 2359304 | tf_op jit(solution)/shard_map/ppermute | solution.py:536
  61.7 11.7 %collective-permute-start.8 = (f32[768,256]{1,0:T(8,128)S(1)}, f32[768,256]{1,0:T(8,128)S(1)}, u32[]{:S(2)}, u32[]{:S(2)}) collective-permute-start(f32[768,256]{1,0:T(8,128)S(1)} %get-tuple-element.141), channel_id=1, source_target_pairs={{0,15},{1,0},{2,1},{3,2},{4,3},{5,4},{6,5},{7,6},{8,7},{9,8},{10,9... | collective-permute-start | bytes 2359304 | tf_op jit(solution)/shard_map/ppermute | solution.py:536
  73.4 14.4 %collective-permute-start.9 = (f32[768,256]{1,0:T(8,128)S(1)}, f32[768,256]{1,0:T(8,128)S(1)}, u32[]{:S(2)}, u32[]{:S(2)}) collective-permute-start(f32[768,256]{1,0:T(8,128)S(1)} %multiply_add_fusion.w_ref), channel_id=1, source_target_pairs={{0,15},{1,0},{2,1},{3,2},{4,3},{5,4},{6,5},{7,6},{8,7},{9,8},{10,9... | collective-permute-start | bytes 2359304 | tf_op jit(solution)/shard_map/ppermute | solution.py:536
  81.7 14.4 %collective-permute-start.10 = (f32[768,256]{1,0:T(8,128)S(1)}, f32[768,256]{1,0:T(8,128)S(1)}, u32[]{:S(2)}, u32[]{:S(2)}) collective-permute-start(f32[768,256]{1,0:T(8,128)S(1)} %get-tuple-element.155), channel_id=1, source_target_pairs={{0,15},{1,0},{2,1},{3,2},{4,3},{5,4},{6,5},{7,6},{8,7},{9,8},{10,9... | collective-permute-start | bytes 2359304 | tf_op jit(solution)/shard_map/ppermute | solution.py:536

commit v2 on v1

--- a/solution.py
+++ b/solution.py
@@ -23,6 +23,14 @@
 SMEM = pl.BlockSpec(memory_space=pltpu.SMEM)
 
 
+def parity():
+    return lax.rem(lax.axis_index("blk"), 2)
+
+
+def upper_half():
+    return lax.rem(lax.div(lax.axis_index("blk"), 2), 2)
+
+
 def dot(a, b, ca, cb, precision=None):
     return lax.dot_general(
         a, b, (((ca,), (cb,)), ((), ())), precision=precision, preferred_element_type=F32
@@ -37,7 +45,7 @@
     return jax.ShapeDtypeStruct((rows, columns), dtype)
 
 
-def call(kernel, outs, in_specs, scratch=(), near=True):
+def call(kernel, outs, in_specs, scratch=(), near=True, aliases={}):
     cost = pl.CostEstimate(flops=1000, bytes_accessed=1000, transcendentals=0)
     space = (lambda o: pltpu.VMEM(o.shape, o.dtype)) if near else (lambda o: o)
     run = pl.pallas_call(
@@ -46,6 +54,7 @@
         in_specs=in_specs,
         out_specs=jax.tree.map(lambda _: VMEM, outs),
         scratch_shapes=list(scratch),
+        input_output_aliases=aliases,
         compiler_params=params(),
         cost_estimate=cost,
     )
@@ -69,6 +78,9 @@
     copies = []
     for slot, far, near in zip(slots, fars, nears):
         source = far if slot is None else far.at[slot]
+        if len(near.shape) > 2:
+            copies.append(pltpu.make_async_copy(source, near, sems.at[len(copies)]))
+            continue
         rows = near.shape[0] // CHUNKS
         for c in range(CHUNKS):
             part = pl.ds(c * rows, rows)
@@ -79,7 +91,8 @@
 
 
 def near_shapes(later):
-    return [shape(*far.shape[-2:], far.dtype) for _, far in later]
+    cut = [far.shape if slot is None else far.shape[1:] for slot, far in later]
+    return [jax.ShapeDtypeStruct(c, far.dtype) for c, (_, far) in zip(cut, later)]
 
 
 def fetch_sems(later, more=0):
@@ -118,12 +131,12 @@
     ref[HALF + 64 :] = jnp.broadcast_to(total, (PACKED - HALF - 64, RANK))
 
 
-def gram_kernel(slots, core_ref, mask_ref, u_hbm, w_hbm, *refs):
+def gram_kernel(slots, u_hbm, w_hbm, *refs):
     sems = refs[-1]
     count = len(slots)
     others, (keep_ref, send_ref, u_ref, w_ref) = refs[:count], refs[count : count + 4]
     nears = refs[count + 4 : -1]
-    first = core_ref[0] == 0
+    first = parity() == 0
     rows = u_ref.shape[0] // 2
     copies = [pltpu.make_async_copy(w_hbm, w_ref, sems.at[0])]
     for j in range(2):
@@ -152,28 +165,28 @@
         copy.wait()
 
 
-def grams(core, mask, users, items, later):
+def grams(users, items, later):
     packed = shape(PACKED, RANK)
     slots, fars = zip(*later)
     return call(
         functools.partial(gram_kernel, slots),
         (packed, packed, shape(*users.shape), shape(*items.shape), *near_shapes(later)),
-        [SMEM, SMEM, ANY, ANY] + [ANY] * len(later),
+        [ANY, ANY] + [ANY] * len(later),
         [fetch_sems(later, 3)],
-    )(core, mask, users, items, *fars)
-
-
-def halves_kernel(core_ref, keep_ref, got_ref, mine_ref, send_ref):
-    lower = core_ref[1] == 0
+    )(users, items, *fars)
+
+
+def halves_kernel(keep_ref, got_ref, mine_ref, send_ref):
+    lower = upper_half() == 0
     rows = mine_ref.shape[0]
     both = keep_ref[...] + got_ref[...]
     mine_ref[...] = jnp.where(lower, both[:rows], both[rows:])
     send_ref[...] = jnp.where(lower, both[rows:], both[:rows])
 
 
-def halves(core, keep, got):
+def halves(keep, got):
     half = shape(PACKED // 2, RANK)
-    return call(halves_kernel, (half, half), [SMEM, VMEM, VMEM])(core, keep, got)
+    return call(halves_kernel, (half, half), [VMEM, VMEM])(keep, got)
 
 
 def sum_kernel(a_ref, b_ref, out_ref):
@@ -219,9 +232,9 @@
     return jnp.concatenate(done, 0)
 
 
-def draw_kernel(counts, core_ref, mine_ref, other_ref, wu_ref, wi_ref, out_ref):
-    first = core_ref[0] == 0
-    lower = core_ref[1] == 0
+def draw_kernel(counts, mine_ref, other_ref, wu_ref, wi_ref, out_ref):
+    first = parity() == 0
+    lower = upper_half() == 0
     n = jnp.where(first, counts[0], counts[1])
     mine, other = mine_ref[...], other_ref[...]
     packed = jnp.concatenate(
@@ -255,16 +268,16 @@
     out_ref[RANK:] = n * mean / (2.0 + n)
 
 
-def draw(counts, core, mine, other, wishart_user, wishart_item):
+def draw(counts, mine, other, wishart_user, wishart_item):
     return call(
         functools.partial(draw_kernel, counts),
         shape(RANK + 8, RANK),
-        [SMEM, VMEM, VMEM, VMEM, VMEM],
-    )(core, mine, other, wishart_user, wishart_item)
-
-
-def prior_of(users, core_ref, mine_ref, other_ref):
-    take = (core_ref[0] == 0) == users
+        [VMEM, VMEM, VMEM, VMEM],
+    )(mine, other, wishart_user, wishart_item)
+
+
+def prior_of(users, mine_ref, other_ref):
+    take = parity() == (0 if users else 1)
     precision = jnp.where(take, mine_ref[0:RANK], other_ref[0:RANK])
     center = jnp.where(take, mine_ref[RANK : RANK + 1], other_ref[RANK : RANK + 1])
     return split_rows(precision), center
@@ -277,7 +290,8 @@
             ra = slice(at + a * TILE, at + (a + 1) * TILE)
             pa = slice(a * TILE, (a + 1) * TILE)
             ij = slice(j * TILE, (j + 1) * TILE)
-            seen = mask_ref[substep, j, (row + at) // TILE + a].astype(F32)
+            t = (row + at) // TILE + a
+            seen = mask_ref[substep, j : j + 1, t : t + 1].astype(F32)
             gap = ratings_ref[ra, ij].astype(F32) - predicted[pa, ij]
             res_ref[ra, ij] = (gap * seen).astype(BF16)
 
@@ -326,7 +340,7 @@
     rt, acc, *nears = call(
         functools.partial(first_kernel, weight, row, slots, len(noise)),
         (shape(rows, k), shape(k, ni), *near_shapes(later)),
-        [SMEM, VMEM, VMEM, VMEM, VMEM] + [VMEM] * len(noise) + [ANY] * len(fars),
+        [VMEM] * 5 + [VMEM] * len(noise) + [ANY] * len(fars),
         [pltpu.VMEM((rows, ni), BF16), pltpu.VMEM((rows, k), BF16), fetch_sems(later)],
     )(mask, ratings, user_mom, users, items, *noise, *fars)
     return rt, acc, nears
@@ -338,10 +352,10 @@
     for acc in accs[1:]:
         like = like + acc[...]
     ni = w_ref.shape[0]
-    out_ref[0:ni] = (
+    out_ref[0:ni] = w_ref[...]
+    out_ref[ni:] = (
         DECAY * q_ref[...] + RATE * weight * like.T + jnp.sqrt(0.4) * in_ref[...].astype(F32)
     )
-    out_ref[ni:] = w_ref[...]
 
 
 def item_start(weight, items, item_mom, item_noise, accs):
@@ -353,89 +367,103 @@
     )(items, item_mom, item_noise, *accs)
 
 
-def finish_kernel(is_user, pieces, core_ref, mine_ref, other_ref, *refs):
-    (x_out, m_out, rhs_ref), ins = refs[-3:], refs[:-3]
-    rhs, center = prior_of(is_user, core_ref, mine_ref, other_ref)
+def finish_kernel(mine_ref, other_ref, x_ref, *refs):
+    parts, (x_out, m_out, rhs_ref) = refs[:-3], refs[-3:]
+    rhs, center = prior_of(True, mine_ref, other_ref)
     rhs_ref[...] = rhs
     rows = 256
-    read = lambda piece, at, size: ins[piece[0]][piece[1] + at : piece[1] + at + size]
     base = 0
-    for size, factors, momenta in pieces:
-        for at in range(0, size, rows):
-            step = min(rows, size - at)
-            x = read(factors, at, step)
+    for part in parts:
+        for at in range(0, part.shape[0], rows):
+            here = slice(base, base + rows)
+            x = x_ref[here]
             columns = jnp.concatenate(split_columns(x - center), 1)
-            m = read(momenta, at, step) + RATE * dot(columns, rhs_ref[...], 1, 0)
-            m_out[base : base + step] = m
-            x_out[base : base + step] = x + RATE * m
-            base += step
-
-
-def finish(is_user, core, mine, other, arrays, pieces):
-    n, k = sum(p[0] for p in pieces), arrays[0].shape[1]
+            m = part[at : at + rows] + RATE * dot(columns, rhs_ref[...], 1, 0)
+            m_out[here] = m
+            x_out[here] = x + RATE * m
+            base += rows
+
+
+def finish(mine, other, x, parts):
+    n, k = x.shape
     return call(
-        functools.partial(finish_kernel, is_user, pieces),
+        finish_kernel,
         (shape(n, k), shape(n, k)),
-        [SMEM] + [VMEM] * (2 + len(arrays)),
+        [VMEM] * (3 + len(parts)),
         [pltpu.VMEM((6 * RANK, k), BF16)],
-    )(core, mine, other, *arrays)
-
-
-def items_kernel(
-    weight,
-    substep,
-    mask_ref,
-    core_ref,
-    mine_ref,
-    other_ref,
-    ratings_ref,
-    u_ref,
-    w_ref,
-    q_ref,
-    in_ref,
-    res_ref,
-    q_out,
-    low_ref,
-):
-    low_w = w_ref[...].astype(BF16)
-    rows = 256
-    for t in range(u_ref.shape[0] // rows):
-        here = slice(t * rows, (t + 1) * rows)
-        low_u = u_ref[here].astype(BF16)
-        low_ref[here] = low_u
-        residue_into(res_ref, t * rows, ratings_ref, mask_ref, substep, 0, rows, low_u, low_w)
-    like = dot(low_ref[...], res_ref[...], 0, 0)
-    rhs, center = prior_of(False, core_ref, mine_ref, other_ref)
-    prior = dot(jnp.concatenate(split_columns(w_ref[...] - center), 1), rhs, 1, 0)
-    q_out[...] = (
-        DECAY * q_ref[...]
-        + RATE * (weight * like.T + prior)
-        + jnp.sqrt(0.4) * in_ref[...].astype(F32)
-    )
-
-
-def items_step(weight, substep, mask, core, mine, other, ratings, users, w, q, item_noise):
+    )(mine, other, x, *parts)
+
+
+def first_items_kernel(mine_ref, other_ref, pack_ref, w_out, q_out):
+    rhs, center = prior_of(False, mine_ref, other_ref)
+    ni = w_out.shape[0]
+    w = pack_ref[0:ni]
+    prior = dot(jnp.concatenate(split_columns(w - center), 1), rhs, 1, 0)
+    q = pack_ref[ni:] + RATE * prior
+    q_out[...] = q
+    w_out[...] = w + RATE * q
+
+
+def first_items(mine, other, pack):
+    ni, k = pack.shape[0] // 2, pack.shape[1]
+    return call(first_items_kernel, (shape(ni, k),) * 2, [VMEM] * 3)(mine, other, pack)
+
+
+def items_kernel(weight, substep, turn, mask_ref, mine_ref, other_ref, *refs):
+    ratings_ref, u_ref, in_ref, w_ref, q_ref = refs[:5]
+    res_ref, out_ref, low_ref, part_ref = refs[-4:]
+
+    def work():
+        rhs, center = prior_of(False, mine_ref, other_ref)
+        ni = in_ref.shape[0]
+        w, q = w_ref[...], q_ref[...]
+        if turn is not None:
+            w = w + RATE * q
+            out_ref[0:ni] = w
+        prior = dot(jnp.concatenate(split_columns(w - center), 1), rhs, 1, 0)
+        part_ref[...] = DECAY * q + RATE * prior + jnp.sqrt(0.4) * in_ref[...].astype(F32)
+        low_w = w.astype(BF16)
+        rows = 256
+        for t in range(u_ref.shape[0] // rows):
+            here = slice(t * rows, (t + 1) * rows)
+            low_u = u_ref[here].astype(BF16)
+            low_ref[here] = low_u
+            residue_into(
+                res_ref, t * rows, ratings_ref, mask_ref, substep, 0, rows, low_u, low_w
+            )
+        like = dot(low_ref[...], res_ref[...], 0, 0)
+        out_ref[out_ref.shape[0] - ni :] = part_ref[...] + RATE * weight * like.T
+
+    if turn is None:
+        work()
+    else:
+        pl.when(parity() == turn)(work)
+
+
+def items_step(weight, substep, turn, mask, mine, other, ratings, users, noise, w, q, res=None):
     n, k = users.shape
-    ni = w.shape[0]
+    ni = noise.shape[0]
+    more = [] if res is None else [res]
     return call(
-        functools.partial(items_kernel, weight, substep),
-        (shape(n, ni, BF16), shape(ni, k)),
-        [SMEM, SMEM] + [VMEM] * 7,
-        [pltpu.VMEM((n, k), BF16)],
-    )(mask, core, mine, other, ratings, users, w, q, item_noise)
+        functools.partial(items_kernel, weight, substep, turn),
+        (shape(n, ni, BF16), shape(ni if turn is None else 2 * ni, k)),
+        [VMEM] * (8 + len(more)),
+        [pltpu.VMEM((n, k), BF16), pltpu.VMEM((ni, k), F32)],
+        aliases={8: 0} if more else {},
+    )(mask, mine, other, ratings, users, noise, w, q, *more)
 
 
 def users_kernel(
     weight,
     slots,
-    core_ref,
     mine_ref,
     other_ref,
     res_ref,
-    w_ref,
     u_ref,
     r_ref,
     un_ref,
+    even_ref,
+    odd_ref,
     *refs,
 ):
     if slots:
@@ -449,12 +477,12 @@
         copy.start()
     if not slots:
         mine, other = mine_ref[0:RANK], other_ref[0:RANK]
-        first = core_ref[0] == 0
+        first = parity() == 0
         draws[0][...] = jnp.where(first, mine, other)
         draws[1][...] = jnp.where(first, other, mine)
-    ni = w_ref.shape[0]
-    rhs_ref[0:ni] = w_ref[...].astype(BF16)
-    rhs, center = prior_of(True, core_ref, mine_ref, other_ref)
+    ni = res_ref.shape[1]
+    rhs_ref[0:ni] = jnp.where(parity() == 0, even_ref[0:ni], odd_ref[0:ni]).astype(BF16)
+    rhs, center = prior_of(True, mine_ref, other_ref)
     rhs_ref[ni:] = rhs
     rows = 256
     for t in range(u_ref.shape[0] // rows):
@@ -473,42 +501,50 @@
         copy.wait()
 
 
-def users_step(weight, later, core, mine, other, res, w, users, user_mom, user_noise):
+def users_step(weight, later, mine, other, res, even, odd, users, user_mom, user_noise):
     n, k = users.shape
-    ni = w.shape[0]
+    ni = res.shape[1]
     slots = tuple(slot for slot, _ in later)
     fars = [far for _, far in later]
     more = near_shapes(later) if later else [shape(RANK, RANK)] * 2
     return call(
         functools.partial(users_kernel, weight, slots),
         (shape(n, k), shape(n, k), *more),
-        [SMEM] + [VMEM] * 7 + [ANY] * len(fars),
+        [VMEM] * 8 + [ANY] * len(fars),
         [pltpu.VMEM((ni + 6 * RANK, k), BF16)] + [fetch_sems(later)] * bool(later),
         near=bool(later),
-    )(core, mine, other, res, w, users, user_mom, user_noise, *fars)
-
-
-def arrived_kernel(w_ref, q_ref, w_out, q_out, sum_ref, sems):
-    first = pltpu.make_async_copy(q_ref, q_out, sems.at[0])
-    first.start()
-    sum_ref[...] = w_ref[...] + RATE * q_ref[...]
-    second = pltpu.make_async_copy(sum_ref, w_out, sems.at[1])
-    second.start()
-    first.wait()
-    second.wait()
-
-
-def arrived(before, came):
-    out = pltpu.HBM(came.shape, F32)
+    )(mine, other, res, users, user_mom, user_noise, even, odd, *fars)
+
+
+def arrived_kernel(even_ref, odd_ref, w_out, q_out, w_ref, sems):
+    ni = w_ref.shape[0]
+
+    def run(pack_ref):
+        first = pltpu.make_async_copy(pack_ref.at[pl.ds(ni, ni)], q_out, sems.at[0])
+        first.start()
+        w_ref[...] = pack_ref[0:ni] + RATE * pack_ref[ni:]
+        second = pltpu.make_async_copy(w_ref, w_out, sems.at[1])
+        second.start()
+        first.wait()
+        second.wait()
+
+    pl.when(parity() == 0)(lambda: run(even_ref))
+    pl.when(parity() == 1)(lambda: run(odd_ref))
+
+
+def arrived(even, odd):
+    ni, k = even.shape[0] // 2, even.shape[1]
+    out = pltpu.HBM((ni, k), F32)
+    near = lambda x: pltpu.with_memory_space_constraint(x, pltpu.VMEM)
     return pl.pallas_call(
         arrived_kernel,
         out_shape=(out, out),
         in_specs=[VMEM, VMEM],
         out_specs=(ANY, ANY),
-        scratch_shapes=[pltpu.VMEM(came.shape, F32), pltpu.SemaphoreType.DMA((2,))],
+        scratch_shapes=[pltpu.VMEM((ni, k), F32), pltpu.SemaphoreType.DMA((2,))],
         compiler_params=params(),
         cost_estimate=pl.CostEstimate(flops=1000, bytes_accessed=1000, transcendentals=0),
-    )(before, came)
+    )(near(even), near(odd))
 
 
 def swapped(array, by, size):
@@ -528,17 +564,12 @@
     wishart_item,
 ):
     blocks = lax.axis_size("blk")
-    blk = lax.axis_index("blk")
     user_rows = user_factors.shape[0]
     item_rows = item_factors.shape[0]
     weight = 1.0 * blocks
-    back = [(i, (i - 1) % blocks) for i in range(blocks)]
-    shift = lambda array: lax.ppermute(array, "blk", back)
     fence = lax.optimization_barrier
-
-    odd = blk % 2
-    half = (blk // 2) % 2
-    core = jnp.stack([odd, half]).astype(jnp.int32)
+    inside = [(i, i - 1) for i in range(1, blocks, 2)]
+    across = [(i, (i - 1) % blocks) for i in range(0, blocks, 2)]
 
     mask = tile_mask.transpose(0, 2, 1)
     parts = 4
@@ -551,15 +582,13 @@
         [(None, wishart_user), (None, wishart_item)],
     ]
 
-    keep, send, near_u, near_w, near_ratings, near_r = grams(
-        core,
-        mask,
+    keep, send, near_u, near_w, near_ratings, near_r, mask = grams(
         user_factors,
         item_factors,
-        [(0, ratings), (None, user_momentum)],
+        [(0, ratings), (None, user_momentum), (None, mask)],
     )
     got = swapped(send, 1, blocks)
-    mine, send = halves(core, keep, got)
+    mine, send = halves(keep, got)
 
     def part():
         j = len(rts)
@@ -595,58 +624,38 @@
         part()
     item_part = item_start(weight, near_w, loaded[0][1], loaded[0][2], accs)
     other, item_part, *rts = fence((other, item_part, *rts))
-    early = shift(item_part)
+    send = lambda array, pairs: lax.ppermute(array, "blk", pairs)
+    early = send(item_part, inside + across)
     wu, wi = loaded[3]
-    near = {1: (loaded[1][0], *loaded[2])}
+    near = (loaded[1][0], *loaded[2])
     counts = (1.0 * user_rows * blocks, 1.0 * item_rows * blocks)
-    drawn = draw(counts, core, mine, other, wu, wi)
+    drawn = draw(counts, mine, other, wu, wi)
     peer = swapped(drawn, 1, blocks)
-
-    users, user_mom = finish(
-        True,
-        core,
-        drawn,
-        peer,
-        (near_u, *rts),
-        tuple((rows, (0, j * rows), (1 + j, 0)) for j in range(parts)),
-    )
-    items, item_mom = finish(
-        False,
-        core,
-        drawn,
-        peer,
-        (early,),
-        ((item_rows, (0, item_rows), (0, 0)),),
-    )
-    for substep in range(1, SUBSTEPS):
-        last = substep == SUBSTEPS - 1
-        here_ratings, here_un, here_in = near[substep]
-        later = [] if last else [(substep + 1, x) for x in (ratings, user_noise, item_noise)]
-        before = shift(items)
-        res, item_next = items_step(
-            weight,
-            substep,
-            mask,
-            core,
-            drawn,
-            peer,
-            here_ratings,
-            users,
-            items,
-            item_mom,
-            here_in,
-        )
-        came = shift(item_next)
-        users, user_mom, *more = users_step(
-            weight, later, core, drawn, peer, res, items, users, user_mom, here_un
-        )
-        before, users, user_mom, *more = fence((before, users, user_mom, *more))
-        if not last:
-            near[substep + 1] = more
-            items = before + RATE * came
-            item_mom = came
-    items, item_mom = arrived(before, came)
-    return (users, user_mom, items, item_mom, *more)
+    users, user_mom = finish(drawn, peer, near_u, rts)
+    users, early = fence((users, early))
+    items, item_mom = first_items(drawn, peer, early)
+
+    before = send(items, inside + across)
+    args = (mask, drawn, peer, near[0], users, near[2])
+    res, item_mom = items_step(weight, 1, None, *args, items, item_mom)
+    q_even, q_odd = send(item_mom, inside), send(item_mom, across)
+    later = [(2, x) for x in (ratings, user_noise, item_noise)]
+    users, user_mom, *near = users_step(
+        weight, later, drawn, peer, res, items, items, users, user_mom, near[1]
+    )
+    before, users, user_mom, *near = fence((before, users, user_mom, *near))
+
+    args = (mask, drawn, peer, near[0], users, near[2])
+    res, even = items_step(weight, 2, 0, *args, before, q_even)
+    pack_odd = send(even, across)
+    res, odd = items_step(weight, 2, 1, *args, before, q_odd, res)
+    pack_even = send(odd, inside)
+    users, user_mom, *precisions = users_step(
+        weight, [], drawn, peer, res, even, odd, users, user_mom, near[1]
+    )
+    pack_odd, users, user_mom, *precisions = fence((pack_odd, users, user_mom, *precisions))
+    items, item_mom = arrived(pack_even, pack_odd)
+    return (users, user_mom, items, item_mom, *precisions)
 
 
 def solution(mesh):

time: 97.7 us -> 89.2 us (0.913)
  Pallas kernels: 49.7 us -> 41.6 us
  starting transfers between devices: 20.1 us -> 25.4 us
  waiting for transfers between devices: 25.7 us -> 20.9 us
    pallas_call x17 -> x18, Pallas kernels: 48.6 us -> 40.4 us  [placed(): run(*(pltpu.with_memory_space_constraint(a, spaces[id(s)]) if id(s) in sp...]
    ppermute x5 -> x6, waiting for transfers between devices: 21.2 us -> 15.5 us  [local(): send = lambda array, pairs: lax.ppermute(array, 'blk', pairs)]
    ppermute x5 -> x6, starting transfers between devices: 9.94 us -> 14.1 us  [local(): send = lambda array, pairs: lax.ppermute(array, 'blk', pairs)]
    ppermute x6, starting transfers between devices: 10.1 us -> 11.3 us  [swapped(): return lax.ppermute(array, 'blk', [(i, i ^ by) for i in range(size)])]
  transfers between devices with their start and end apart: 11 -> 12, of which waited for: 8 -> 9; matrix products, arithmetic and copies ran while one was open for 0% -> 0% of each run, Pallas kernels for 43% -> 40%
where the time goes in v2:
time: 89.2 us; the launch traced here: 88.8 us
  Pallas kernels  41.6 us (47%)
  starting transfers between devices  25.4 us (28%)
  waiting for transfers between devices  20.9 us (23%)
  between operations  0.99 us (1%)
    pallas_call x18, Pallas kernels, placed(): run(*(pltpu.with_memory_space_constraint(a, spaces[id(s)]) if id(s) in sp...  40.4 us
    ppermute x6, waiting for transfers between devices, local(): send = lambda array, pairs: lax.ppermute(array, 'blk', pairs)  15.5 us
    ppermute x6, starting transfers between devices, local(): send = lambda array, pairs: lax.ppermute(array, 'blk', pairs)  14.1 us
    ppermute x6, starting transfers between devices, swapped(): return lax.ppermute(array, 'blk', [(i, i ^ by) for i in range(size)])  11.3 us
    ppermute x6, waiting for transfers between devices, swapped(): return lax.ppermute(array, 'blk', [(i, i ^ by) for i in range(size)])  5.38 us
  transfers between devices with their start and end apart: 12, of which 9 were waited for; matrix products, arithmetic and copies ran while one was open for 0% of the time, Pallas kernels for 40%

profile of v2, /device:TPU:0, one launch (start us, length us, event | category | flops | bytes accessed | tf_op | source)
XLA Modules:
  0.0 88.8 jit_solution(3967551108873251657)
XLA Ops:
  0.6 3.6 %shard_map.145 = (f32[208,256]{1,0:T(8,128)S(1)}, f32[208,256]{1,0:T(8,128)S(1)}, f32[2048,256]{1,0:T(8,128)S(1)}, f32[768,256]{1,0:T(8,128)S(1)}, bf16[2048,768...) custom-call(f32[2048,256]{1,0:T(8,128)} %u_hbm.1, f32[768,256]{1,0:T(8,128)} %w_hbm.1, ...), custom_call_target="tpu_custom_call" | custom-call | flops 1000 | bytes 1000 | tf_op jit(solution)/shard_map/pallas_call | solution.py:64
  4.3 0.5 collective-permute-start
  4.8 1.1 %collective-permute-done.got_ref = f32[208,256]{1,0:T(8,128)S(1)} collective-permute-done((f32[208,256]{1,0:T(8,128)S(1)}, f32[208,256]{1,0:T(8,128)S(1)}, u32[]{:S(2)}, u32[]{:S(2)}) %collective-permute-start) | collective-permute-done | bytes 213024 | tf_op jit(solution)/shard_map/ppermute | solution.py:551
  5.9 3.0 %collective-permute-start.1 = (f32[104,256]{1,0:T(8,128)S(1)}, f32[104,256]{1,0:T(8,128)S(1)}, u32[]{:S(2)}, u32[]{:S(2)}) collective-permute-start(f32[104,256]{1,0:T(8,128)S(1)} %get-tuple-element.94), channel_id=1, source_target_pairs={{0,2},{1,3},{2,0},{3,1},{4,6},{5,7},{6,4},{7,5},{8,10},{9,11},{10,... | collective-permute-start | bytes 319496 | tf_op jit(solution)/shard_map/ppermute | solution.py:551
  8.9 2.2 %shard_map.147 = (f32[512,256]{1,0:T(8,128)S(1)}, f32[256,768]{1,0:T(8,128)S(1)}, bf16[2048,256]{1,0:T(8,128)(2,1)S(1)}, f32[768,256]{1,0:T(8,128)S(1)}, bf16[768,256]{1,0:T(8,128)(2,1)S(1)}) custom-call(s32[3,6,16]{2,1,0:T(8,128)S(1)} %get-tuple-element.88.mask_ref, bf16[2048,768]{1,0:T(8,128)(2,1)S(1)} %get-tuple-element.95.ratings_ref, ...), custom_call_target="tpu_custom_call" | custom-call | flops 1000 | bytes 1000 | tf_op jit(solution)/shard_map/pallas_call | solution.py:64
  11.1 1.0 %collective-permute-done.1.b_ref = f32[104,256]{1,0:T(8,128)S(1)} collective-permute-done((f32[104,256]{1,0:T(8,128)S(1)}, f32[104,256]{1,0:T(8,128)S(1)}, u32[]{:S(2)}, u32[]{:S(2)}) %collective-permute-start.1) | collective-permute-done | bytes 106528 | tf_op jit(solution)/shard_map/ppermute | solution.py:551
  12.1 1.9 %collective-permute-start.2 = (f32[104,256]{1,0:T(8,128)S(1)}, f32[104,256]{1,0:T(8,128)S(1)}, u32[]{:S(2)}, u32[]{:S(2)}) collective-permute-start(f32[104,256]{1,0:T(8,128)S(1)} %shard_map.148.a_ref), channel_id=1, source_target_pairs={{0,4},{1,5},{2,6},{3,7},{4,0},{5,1},{6,2},{7,3},{8,12},{9,13},{10,... | collective-permute-start | bytes 319496 | tf_op jit(solution)/shard_map/ppermute | solution.py:551
  14.0 2.2 %shard_map.149 = (f32[512,256]{1,0:T(8,128)S(1)}, f32[256,768]{1,0:T(8,128)S(1)}, bf16[2048,768]{1,0:T(8,128)(2,1)S(1)}) custom-call(s32[3,6,16]{2,1,0:T(8,128)S(1)} %get-tuple-element.88.mask_ref, bf16[2048,768]{1,0:T(8,128)(2,1)S(1)} %get-tuple-element.95.ratings_ref, f32[2048,256]{1,0:T(8,128)S(1)} %get-tuple-element.96.r_ref, ...), custom_call_target="tpu_custom_call" | custom-call | flops 1000 | bytes 1000 | tf_op jit(solution)/shard_map/pallas_call | solution.py:64
  16.2 0.7 collective-permute-done.2.b_ref
  16.9 2.9 %collective-permute-start.3 = (f32[104,256]{1,0:T(8,128)S(1)}, f32[104,256]{1,0:T(8,128)S(1)}, u32[]{:S(2)}, u32[]{:S(2)}) collective-permute-start(f32[104,256]{1,0:T(8,128)S(1)} %shard_map.150.a_ref), channel_id=1, source_target_pairs={{0,8},{1,9},{2,10},{3,11},{4,12},{5,13},{6,14},{7,15},{8,0},{9,1},... | collective-permute-start | bytes 319496 | tf_op jit(solution)/shard_map/ppermute | solution.py:551
  19.8 2.1 %shard_map.151 = (f32[512,256]{1,0:T(8,128)S(1)}, f32[256,768]{1,0:T(8,128)S(1)}, bf16[2048,256]{1,0:T(8,128)(2,1)S(1)}, bf16[768,256]{1,0:T(8,128)(2,1)S(1)}) custom-call(s32[3,6,16]{2,1,0:T(8,128)S(1)} %get-tuple-element.88.mask_ref, bf16[2048,768]{1,0:T(8,128)(2,1)S(1)} %get-tuple-element.95.ratings_ref, f32[2048,256]{1,0:T(8,128)S(1)} %get-tuple-element.96.r_ref, ...), custom_call_target="tpu_custom_call" | custom-call | flops 1000 | bytes 1000 | tf_op jit(solution)/shard_map/pallas_call | solution.py:64
  21.9 0.7 collective-permute-done.3.b_ref
  22.6 2.9 %collective-permute-start.4 = (f32[104,256]{1,0:T(8,128)S(1)}, f32[104,256]{1,0:T(8,128)S(1)}, u32[]{:S(2)}, u32[]{:S(2)}) collective-permute-start(f32[104,256]{1,0:T(8,128)S(1)} %shard_map.152.mine_ref), channel_id=1, source_target_pairs={{0,2},{1,3},{2,0},{3,1},{4,6},{5,7},{6,4},{7,5},{8,10},{9,11},{10,... | collective-permute-start | bytes 319496 | tf_op jit(solution)/shard_map/ppermute | solution.py:551
  25.6 1.8 %shard_map.153 = (f32[512,256]{1,0:T(8,128)S(1)}, f32[256,768]{1,0:T(8,128)S(1)}, f32[256,256]{1,0:T(8,128)S(1)}, f32[256,256]{1,0:T(8,128)S(1)}) custom-call(s32[3,6,16]{2,1,0:T(8,128)S(1)} %get-tuple-element.88.mask_ref, bf16[2048,768]{1,0:T(8,128)(2,1)S(1)} %get-tuple-element.95.ratings_ref, f32[2048,256]{1,0:T(8,128)S(1)} %get-tuple-element.96.r_ref, ...), custom_call_target="tpu_custom_call" | custom-call | flops 1000 | bytes 1000 | tf_op jit(solution)/shard_map/pallas_call | solution.py:64
  27.8 0.4 collective-permute-done.4.other_ref
  28.7 10.5 %shard_map.155.mine_ref = f32[264,256]{1,0:T(8,128)S(1)} custom-call(f32[104,256]{1,0:T(8,128)S(1)} %shard_map.152.mine_ref, f32[104,256]{1,0:T(8,128)S(1)} %collective-permute-done.4.other_ref, f32[256,256]{1,0:T(8,128)S(1)} %get-tuple-element.126.wu_ref, f32[256,256]{1,0:T(8,128)S(1)} %get-tuple-element.127.wi_ref), custom_call_target="tpu_custom_call" | custom-call | flops 1000 | bytes 1000 | tf_op jit(solution)/shard_map/pallas_call | solution.py:64
  39.3 1.4 %collective-permute-done.5.other_ref = f32[264,256]{1,0:T(8,128)S(1)} collective-permute-done((f32[264,256]{1,0:T(8,128)S(1)}, f32[264,256]{1,0:T(8,128)S(1)}, u32[]{:S(2)}, u32[]{:S(2)}) %collective-permute-start.5) | collective-permute-done | bytes 270368 | tf_op jit(solution)/shard_map/ppermute | solution.py:551
  40.8 2.1 %shard_map.156 = (f32[2048,256]{1,0:T(8,128)S(1)}, f32[2048,256]{1,0:T(8,128)S(1)}) custom-call(f32[264,256]{1,0:T(8,128)S(1)} %shard_map.155.mine_ref, f32[264,256]{1,0:T(8,128)S(1)} %collective-permute-done.5.other_ref, f32[2048,256]{1,0:T(8,128)S(1)} %get-tuple-element.119.u_ref.x_ref, f32[512,256]{1,0:T(8,128)S(1)} %get-tuple-element.128.refs_0_, ...), custom_call_target="tpu_custom_call" | custom-call | flops 1000 | bytes 1000 | tf_op jit(solution)/shard_map/pallas_call | solution.py:64
  42.9 3.7 %collective-permute-done.6.pack_ref = f32[1536,256]{1,0:T(8,128)S(1)} collective-permute-done((f32[1536,256]{1,0:T(8,128)S(1)}, f32[1536,256]{1,0:T(8,128)S(1)}, u32[]{:S(2)}, u32[]{:S(2)}) %collective-permute-start.6) | collective-permute-done | bytes 1572896 | tf_op jit(solution)/shard_map/ppermute | solution.py:627
  46.6 0.8 shard_map.157
  47.4 4.9 %collective-permute-start.7 = (f32[768,256]{1,0:T(8,128)S(1)}, f32[768,256]{1,0:T(8,128)S(1)}, u32[]{:S(2)}, u32[]{:S(2)}) collective-permute-start(f32[768,256]{1,0:T(8,128)S(1)} %get-tuple-element.135.refs_3_.even_ref.odd_ref), channel_id=1, source_target_pairs={{1,0},{3,2},{5,4},{7,6},{9,8},{11,10},{13,12},{15,14},{0,15},{2,1}... | collective-permute-start | bytes 2359304 | tf_op jit(solution)/shard_map/ppermute | solution.py:627
  52.3 3.0 %shard_map.158 = (bf16[2048,768]{1,0:T(8,128)(2,1)S(1)}, f32[768,256]{1,0:T(8,128)S(1)}) custom-call(s32[3,6,16]{2,1,0:T(8,128)S(1)} %get-tuple-element.88.mask_ref, f32[264,256]{1,0:T(8,128)S(1)} %shard_map.155.mine_ref, f32[264,256]{1,0:T(8,128)S(1)} %collective-permute-done.5.other_ref, bf16[2048,768]{1,0:T(8,128)(2,1)S(1)} %get-tuple-element.136.refs_0_, ...), custom_call_target="tpu_custom_call" | custom-call | flops 1000 | bytes 1000 | tf_op jit(solution)/shard_map/pallas_call | solution.py:64
  55.3 1.3 %collective-permute-start.8 = (f32[768,256]{1,0:T(8,128)S(1)}, f32[768,256]{1,0:T(8,128)S(1)}, u32[]{:S(2)}, u32[]{:S(2)}) collective-permute-start(f32[768,256]{1,0:T(8,128)S(1)} %get-tuple-element.152), channel_id=1, source_target_pairs={{1,0},{3,2},{5,4},{7,6},{9,8},{11,10},{13,12},{15,14},{17,16},{19,... | collective-permute-start | bytes 2359304 | tf_op jit(solution)/shard_map/ppermute | solution.py:627
  56.6 4.6 %collective-permute-start.10 = (f32[768,256]{1,0:T(8,128)S(1)}, f32[768,256]{1,0:T(8,128)S(1)}, u32[]{:S(2)}, u32[]{:S(2)}) collective-permute-start(f32[768,256]{1,0:T(8,128)S(1)} %get-tuple-element.152), channel_id=1, source_target_pairs={{0,15},{2,1},{4,3},{6,5},{8,7},{10,9},{12,11},{14,13},{16,31},{18,... | collective-permute-start | bytes 2359304 | tf_op jit(solution)/shard_map/ppermute | solution.py:627
  61.2 3.3 %shard_map.159 = (f32[2048,256]{1,0:T(8,128)S(1)}, f32[2048,256]{1,0:T(8,128)S(1)}, bf16[2048,768]{1,0:T(8,128)(2,1)S(1)}, bf16[2048,256]{1,0:T(8,128)(2,1)S(1)}, bf16[768,256]{1,0:T(8,128)(2,1)S(1)}) custom-call(f32[264,256]{1,0:T(8,128)S(1)} %shard_map.155.mine_ref, f32[264,256]{1,0:T(8,128)S(1)} %collective-permute-done.5.other_ref, ...), custom_call_target="tpu_custom_call" | custom-call | flops 1000 | bytes 1000 | tf_op jit(solution)/shard_map/pallas_call | solution.py:64
  64.5 3.0 %shard_map.160 = (bf16[2048,768]{1,0:T(8,128)(2,1)S(1)}, f32[1536,256]{1,0:T(8,128)S(1)}) custom-call(s32[3,6,16]{2,1,0:T(8,128)S(1)} %get-tuple-element.88.mask_ref, f32[264,256]{1,0:T(8,128)S(1)} %shard_map.155.mine_ref, f32[264,256]{1,0:T(8,128)S(1)} %collective-permute-done.5.other_ref, bf16[2048,768]{1,0:T(8,128)(2,1)S(1)} %get-tuple-element.148.refs_0_, ...), custom_call_target="tpu_custom_call" | custom-call | flops 1000 | bytes 1000 | tf_op jit(solution)/shard_map/pallas_call | solution.py:64
  67.5 1.4 %collective-permute-start.9 = (f32[1536,256]{1,0:T(8,128)S(1)}, f32[1536,256]{1,0:T(8,128)S(1)}, u32[]{:S(2)}, u32[]{:S(2)}) collective-permute-start(f32[1536,256]{1,0:T(8,128)S(1)} %get-tuple-element.153.even_ref), channel_id=1, source_target_pairs={{0,15},{2,1},{4,3},{6,5},{8,7},{10,9},{12,11},{14,13},{16,31},{18,... | collective-permute-start | bytes 4718600 | tf_op jit(solution)/shard_map/ppermute | solution.py:627
  68.9 1.8 %collective-permute-done.10.refs_4_ = f32[768,256]{1,0:T(8,128)S(1)} collective-permute-done((f32[768,256]{1,0:T(8,128)S(1)}, f32[768,256]{1,0:T(8,128)S(1)}, u32[]{:S(2)}, u32[]{:S(2)}) %collective-permute-start.10) | collective-permute-done | bytes 786464 | tf_op jit(solution)/shard_map/ppermute | solution.py:627
  70.6 1.5 %collective-permute-start.11 = (f32[1536,256]{1,0:T(8,128)S(1)}, f32[1536,256]{1,0:T(8,128)S(1)}, u32[]{:S(2)}, u32[]{:S(2)}) collective-permute-start(f32[1536,256]{1,0:T(8,128)S(1)} %get-tuple-element.158.odd_ref), channel_id=1, source_target_pairs={{1,0},{3,2},{5,4},{7,6},{9,8},{11,10},{13,12},{15,14},{17,16},{19,... | collective-permute-start | bytes 4718600 | tf_op jit(solution)/shard_map/ppermute | solution.py:627
  72.2 5.3 %shard_map.162 = (f32[2048,256]{1,0:T(8,128)}, f32[2048,256]{1,0:T(8,128)}, f32[256,256]{1,0:T(8,128)}, f32[256,256]{1,0:T(8,128)}) custom-call(f32[264,256]{1,0:T(8,128)S(1)} %shard_map.155.mine_ref, f32[264,256]{1,0:T(8,128)S(1)} %collective-permute-done.5.other_ref, bf16[2048,768]{1,0:T(8,128)(2,1)S(1)} %get-tuple-element.155.res_ref, ...), custom_call_target="tpu_custom_call" | custom-call | flops 1000 | bytes 1000 | tf_op jit(solution)/shard_map/pallas_call | solution.py:64
  77.4 10.0 %collective-permute-done.9.odd_ref = f32[1536,256]{1,0:T(8,128)S(1)} collective-permute-done((f32[1536,256]{1,0:T(8,128)S(1)}, f32[1536,256]{1,0:T(8,128)S(1)}, u32[]{:S(2)}, u32[]{:S(2)}) %collective-permute-start.9) | collective-permute-done | bytes 1572896 | tf_op jit(solution)/shard_map/ppermute | solution.py:627
  87.5 1.2 %shard_map.163 = (f32[768,256]{1,0:T(8,128)}, f32[768,256]{1,0:T(8,128)}) custom-call(f32[1536,256]{1,0:T(8,128)S(1)} %collective-permute-done.11.even_ref, f32[1536,256]{1,0:T(8,128)S(1)} %collective-permute-done.9.odd_ref), custom_call_target="tpu_custom_call" | custom-call | flops 1000 | bytes 1000 | tf_op jit(solution)/shard_map/pallas_call | solution.py:539
  (11 shorter events, 1.1 us)
Async XLA Ops:
  4.3 1.6 %collective-permute-start = (f32[208,256]{1,0:T(8,128)S(1)}, f32[208,256]{1,0:T(8,128)S(1)}, u32[]{:S(2)}, u32[]{:S(2)}) collective-permute-start(f32[208,256]{1,0:T(8,128)S(1)} %get-tuple-element.90), channel_id=1, source_target_pairs={{0,1},{1,0},{2,3},{3,2},{4,5},{5,4},{6,7},{7,6},{8,9},{9,8},{10,11... | collective-permute-start | bytes 638984 | tf_op jit(solution)/shard_map/ppermute | solution.py:551
  5.9 6.2 %collective-permute-start.1 = (f32[104,256]{1,0:T(8,128)S(1)}, f32[104,256]{1,0:T(8,128)S(1)}, u32[]{:S(2)}, u32[]{:S(2)}) collective-permute-start(f32[104,256]{1,0:T(8,128)S(1)} %get-tuple-element.94), channel_id=1, source_target_pairs={{0,2},{1,3},{2,0},{3,1},{4,6},{5,7},{6,4},{7,5},{8,10},{9,11},{10,... | collective-permute-start | bytes 319496 | tf_op jit(solution)/shard_map/ppermute | solution.py:551
  12.1 4.8 %collective-permute-start.2 = (f32[104,256]{1,0:T(8,128)S(1)}, f32[104,256]{1,0:T(8,128)S(1)}, u32[]{:S(2)}, u32[]{:S(2)}) collective-permute-start(f32[104,256]{1,0:T(8,128)S(1)} %shard_map.148.a_ref), channel_id=1, source_target_pairs={{0,4},{1,5},{2,6},{3,7},{4,0},{5,1},{6,2},{7,3},{8,12},{9,13},{10,... | collective-permute-start | bytes 319496 | tf_op jit(solution)/shard_map/ppermute | solution.py:551
  16.9 5.7 %collective-permute-start.3 = (f32[104,256]{1,0:T(8,128)S(1)}, f32[104,256]{1,0:T(8,128)S(1)}, u32[]{:S(2)}, u32[]{:S(2)}) collective-permute-start(f32[104,256]{1,0:T(8,128)S(1)} %shard_map.150.a_ref), channel_id=1, source_target_pairs={{0,8},{1,9},{2,10},{3,11},{4,12},{5,13},{6,14},{7,15},{8,0},{9,1},... | collective-permute-start | bytes 319496 | tf_op jit(solution)/shard_map/ppermute | solution.py:551
  22.6 5.6 %collective-permute-start.4 = (f32[104,256]{1,0:T(8,128)S(1)}, f32[104,256]{1,0:T(8,128)S(1)}, u32[]{:S(2)}, u32[]{:S(2)}) collective-permute-start(f32[104,256]{1,0:T(8,128)S(1)} %shard_map.152.mine_ref), channel_id=1, source_target_pairs={{0,2},{1,3},{2,0},{3,1},{4,6},{5,7},{6,4},{7,5},{8,10},{9,11},{10,... | collective-permute-start | bytes 319496 | tf_op jit(solution)/shard_map/ppermute | solution.py:551
  28.3 18.3 %collective-permute-start.6 = (f32[1536,256]{1,0:T(8,128)S(1)}, f32[1536,256]{1,0:T(8,128)S(1)}, u32[]{:S(2)}, u32[]{:S(2)}) collective-permute-start(f32[1536,256]{1,0:T(8,128)S(1)} %shard_map.154), channel_id=1, source_target_pairs={{1,0},{3,2},{5,4},{7,6},{9,8},{11,10},{13,12},{15,14},{0,15},{2,1}... | collective-permute-start | bytes 4718600 | tf_op jit(solution)/shard_map/ppermute | solution.py:627
  39.1 1.6 %collective-permute-start.5 = (f32[264,256]{1,0:T(8,128)S(1)}, f32[264,256]{1,0:T(8,128)S(1)}, u32[]{:S(2)}, u32[]{:S(2)}) collective-permute-start(f32[264,256]{1,0:T(8,128)S(1)} %shard_map.155.mine_ref), channel_id=1, source_target_pairs={{0,1},{1,0},{2,3},{3,2},{4,5},{5,4},{6,7},{7,6},{8,9},{9,8},{10,11... | collective-permute-start | bytes 811016 | tf_op jit(solution)/shard_map/ppermute | solution.py:551
  47.4 17.1 %collective-permute-start.7 = (f32[768,256]{1,0:T(8,128)S(1)}, f32[768,256]{1,0:T(8,128)S(1)}, u32[]{:S(2)}, u32[]{:S(2)}) collective-permute-start(f32[768,256]{1,0:T(8,128)S(1)} %get-tuple-element.135.refs_3_.even_ref.odd_ref), channel_id=1, source_target_pairs={{1,0},{3,2},{5,4},{7,6},{9,8},{11,10},{13,12},{15,14},{0,15},{2,1}... | collective-permute-start | bytes 2359304 | tf_op jit(solution)/shard_map/ppermute | solution.py:627
  55.3 9.2 %collective-permute-start.8 = (f32[768,256]{1,0:T(8,128)S(1)}, f32[768,256]{1,0:T(8,128)S(1)}, u32[]{:S(2)}, u32[]{:S(2)}) collective-permute-start(f32[768,256]{1,0:T(8,128)S(1)} %get-tuple-element.152), channel_id=1, source_target_pairs={{1,0},{3,2},{5,4},{7,6},{9,8},{11,10},{13,12},{15,14},{17,16},{19,... | collective-permute-start | bytes 2359304 | tf_op jit(solution)/shard_map/ppermute | solution.py:627
  56.6 14.0 %collective-permute-start.10 = (f32[768,256]{1,0:T(8,128)S(1)}, f32[768,256]{1,0:T(8,128)S(1)}, u32[]{:S(2)}, u32[]{:S(2)}) collective-permute-start(f32[768,256]{1,0:T(8,128)S(1)} %get-tuple-element.152), channel_id=1, source_target_pairs={{0,15},{2,1},{4,3},{6,5},{8,7},{10,9},{12,11},{14,13},{16,31},{18,... | collective-permute-start | bytes 2359304 | tf_op jit(solution)/shard_map/ppermute | solution.py:627
  67.5 20.0 %collective-permute-start.9 = (f32[1536,256]{1,0:T(8,128)S(1)}, f32[1536,256]{1,0:T(8,128)S(1)}, u32[]{:S(2)}, u32[]{:S(2)}) collective-permute-start(f32[1536,256]{1,0:T(8,128)S(1)} %get-tuple-element.153.even_ref), channel_id=1, source_target_pairs={{0,15},{2,1},{4,3},{6,5},{8,7},{10,9},{12,11},{14,13},{16,31},{18,... | collective-permute-start | bytes 4718600 | tf_op jit(solution)/shard_map/ppermute | solution.py:627
  70.6 16.9 %collective-permute-start.11 = (f32[1536,256]{1,0:T(8,128)S(1)}, f32[1536,256]{1,0:T(8,128)S(1)}, u32[]{:S(2)}, u32[]{:S(2)}) collective-permute-start(f32[1536,256]{1,0:T(8,128)S(1)} %get-tuple-element.158.odd_ref), channel_id=1, source_target_pairs={{1,0},{3,2},{5,4},{7,6},{9,8},{11,10},{13,12},{15,14},{17,16},{19,... | collective-permute-start | bytes 4718600 | tf_op jit(solution)/shard_map/ppermute | solution.py:627

commit v3 on v2

--- a/solution.py
+++ b/solution.py
@@ -12,7 +12,7 @@
 RANK = 256
 HALF = 128
 LANES = 8
-PACKED = 208
+PACKED = 144
 RATE = 0.005
 DECAY = 0.8
 HIGHEST = lax.Precision.HIGHEST
@@ -123,12 +123,20 @@
     return (dot(mid, mid, 0, 0) + (cross + cross.T)) + dot(high, high, 0, 0)
 
 
+def corner():
+    row = lax.broadcasted_iota(jnp.int32, (HALF, HALF), 0)
+    column = lax.broadcasted_iota(jnp.int32, (HALF, HALF), 1)
+    return column >= row, column == row
+
+
 def store_packed(ref, gram, total):
-    ref[0:HALF, 0:HALF] = gram[0:HALF, 0:HALF]
-    ref[0:HALF, HALF:] = gram[HALF:, 0:HALF]
-    ref[HALF : HALF + 64, 0:HALF] = gram[HALF : HALF + 64, HALF:]
-    ref[HALF : HALF + 64, HALF:] = gram[HALF + 64 :, HALF:]
-    ref[HALF + 64 :] = jnp.broadcast_to(total, (PACKED - HALF - 64, RANK))
+    upper, diagonal = corner()
+    last = gram[HALF:, HALF:]
+    ref[0:HALF, 0:HALF] = jnp.where(upper, gram[0:HALF, 0:HALF], last)
+    ref[0:HALF, HALF:] = gram[0:HALF, HALF:]
+    ref[HALF : HALF + 8] = jnp.broadcast_to(total, (8, RANK))
+    line = jnp.sum(jnp.where(diagonal, last, 0.0), 0, keepdims=True)
+    ref[HALF + 8 :] = jnp.concatenate([jnp.broadcast_to(line, (8, HALF))] * 2, 1)
 
 
 def gram_kernel(slots, u_hbm, w_hbm, *refs):
@@ -242,18 +250,19 @@
     )
     bartlett_top = jnp.where(first, wu_ref[0:HALF], wi_ref[0:HALF])
     bartlett_low = jnp.where(first, wu_ref[HALF:], wi_ref[HALF:])
-    mean = packed[HALF + 64 : HALF + 72] / n
+    mean = packed[HALF : HALF + 8] / n
     outer = dot(mean * 0.125, mean, 0, 0, HIGHEST)
     factor = n * n / (2.0 + n)
-    diag = lax.broadcasted_iota(jnp.int32, (HALF, HALF), 0) == lax.broadcasted_iota(
-        jnp.int32, (HALF, HALF), 1
-    )
-    eye = jnp.where(diag, 1.0, 0.0)
-    s11 = eye + packed[0:HALF, 0:HALF] - factor * outer[0:HALF, 0:HALF]
-    s21 = packed[0:HALF, HALF:] - factor * outer[HALF:, 0:HALF]
-    gram22 = jnp.concatenate(
-        [packed[HALF : HALF + 64, 0:HALF], packed[HALF : HALF + 64, HALF:]], 0
-    )
+    upper, diagonal = corner()
+    eye = jnp.where(diagonal, 1.0, 0.0)
+    mixed = packed[0:HALF, 0:HALF]
+    above = jnp.where(upper & ~diagonal, mixed, 0.0)
+    below = jnp.where(upper, 0.0, mixed)
+    line = jnp.broadcast_to(packed[HALF + 8 : HALF + 9, 0:HALF], (HALF, HALF))
+    gram11 = jnp.where(upper, mixed, above.T)
+    gram22 = jnp.where(diagonal, line, below + below.T)
+    s11 = eye + gram11 - factor * outer[0:HALF, 0:HALF]
+    s21 = packed[0:HALF, HALF:].T - factor * outer[HALF:, 0:HALF]
     s22 = eye + gram22 - factor * outer[HALF:, HALF:]
     g1 = inverse_factor(s11)
     l21 = dot(s21, g1, 1, 1, HIGHEST)

time: 89.2 us -> 87 us (0.975)
  waiting for transfers between devices: 20.9 us -> 19.3 us
    ppermute x6, waiting for transfers between devices: 5.38 us -> 3.83 us  [swapped(): return lax.ppermute(array, 'blk', [(i, i ^ by) for i in range(size)])]
    ppermute x6, starting transfers between devices: 11.3 us -> 10.2 us  [swapped(): return lax.ppermute(array, 'blk', [(i, i ^ by) for i in range(size)])]
  transfers between devices with their start and end apart: 12 -> 12, of which waited for: 9 -> 9; matrix products, arithmetic and copies ran while one was open for 0% -> 0% of each run, Pallas kernels for 40% -> 41%
where the time goes in v3:
time: 87 us; the launch traced here: 86.7 us
  Pallas kernels  41.5 us (48%)
  starting transfers between devices  24.8 us (29%)
  waiting for transfers between devices  19.3 us (22%)
  between operations  1 us (1%)
    pallas_call x18, Pallas kernels, placed(): run(*(pltpu.with_memory_space_constraint(a, spaces[id(s)]) if id(s) in sp...  40.4 us
    ppermute x6, waiting for transfers between devices, local(): send = lambda array, pairs: lax.ppermute(array, 'blk', pairs)  15.5 us
    ppermute x6, starting transfers between devices, local(): send = lambda array, pairs: lax.ppermute(array, 'blk', pairs)  14.6 us
    ppermute x6, starting transfers between devices, swapped(): return lax.ppermute(array, 'blk', [(i, i ^ by) for i in range(size)])  10.2 us
    ppermute x6, waiting for transfers between devices, swapped(): return lax.ppermute(array, 'blk', [(i, i ^ by) for i in range(size)])  3.83 us
  transfers between devices with their start and end apart: 12, of which 9 were waited for; matrix products, arithmetic and copies ran while one was open for 0% of the time, Pallas kernels for 41%

profile of v3, /device:TPU:0, one launch (start us, length us, event | category | flops | bytes accessed | tf_op | source)
XLA Modules:
  0.0 86.7 jit_solution(5503157217006120341)
XLA Ops:
  0.6 3.6 %shard_map.145 = (f32[144,256]{1,0:T(8,128)S(1)}, f32[144,256]{1,0:T(8,128)S(1)}, f32[2048,256]{1,0:T(8,128)S(1)}, f32[768,256]{1,0:T(8,128)S(1)}, bf16[2048,768...) custom-call(f32[2048,256]{1,0:T(8,128)} %u_hbm.1, f32[768,256]{1,0:T(8,128)} %w_hbm.1, ...), custom_call_target="tpu_custom_call" | custom-call | flops 1000 | bytes 1000 | tf_op jit(solution)/shard_map/pallas_call | solution.py:64
  4.3 0.5 collective-permute-start
  4.8 1.0 %collective-permute-done.got_ref = f32[144,256]{1,0:T(8,128)S(1)} collective-permute-done((f32[144,256]{1,0:T(8,128)S(1)}, f32[144,256]{1,0:T(8,128)S(1)}, u32[]{:S(2)}, u32[]{:S(2)}) %collective-permute-start) | collective-permute-done | bytes 147488 | tf_op jit(solution)/shard_map/ppermute | solution.py:560
  5.8 2.9 %collective-permute-start.1 = (f32[72,256]{1,0:T(8,128)S(1)}, f32[72,256]{1,0:T(8,128)S(1)}, u32[]{:S(2)}, u32[]{:S(2)}) collective-permute-start(f32[72,256]{1,0:T(8,128)S(1)} %get-tuple-element.94), channel_id=1, source_target_pairs={{0,2},{1,3},{2,0},{3,1},{4,6},{5,7},{6,4},{7,5},{8,10},{9,11},{10,... | collective-permute-start | bytes 221192 | tf_op jit(solution)/shard_map/ppermute | solution.py:560
  8.8 2.2 %shard_map.147 = (f32[512,256]{1,0:T(8,128)S(1)}, f32[256,768]{1,0:T(8,128)S(1)}, bf16[2048,256]{1,0:T(8,128)(2,1)S(1)}, f32[768,256]{1,0:T(8,128)S(1)}, bf16[768,256]{1,0:T(8,128)(2,1)S(1)}) custom-call(s32[3,6,16]{2,1,0:T(8,128)S(1)} %get-tuple-element.88.mask_ref, bf16[2048,768]{1,0:T(8,128)(2,1)S(1)} %get-tuple-element.95.ratings_ref, ...), custom_call_target="tpu_custom_call" | custom-call | flops 1000 | bytes 1000 | tf_op jit(solution)/shard_map/pallas_call | solution.py:64
  11.0 0.3 collective-permute-done.1.b_ref
  11.4 1.9 %collective-permute-start.2 = (f32[72,256]{1,0:T(8,128)S(1)}, f32[72,256]{1,0:T(8,128)S(1)}, u32[]{:S(2)}, u32[]{:S(2)}) collective-permute-start(f32[72,256]{1,0:T(8,128)S(1)} %shard_map.148.a_ref), channel_id=1, source_target_pairs={{0,4},{1,5},{2,6},{3,7},{4,0},{5,1},{6,2},{7,3},{8,12},{9,13},{10,... | collective-permute-start | bytes 221192 | tf_op jit(solution)/shard_map/ppermute | solution.py:560
  13.3 2.2 %shard_map.149 = (f32[512,256]{1,0:T(8,128)S(1)}, f32[256,768]{1,0:T(8,128)S(1)}, bf16[2048,768]{1,0:T(8,128)(2,1)S(1)}) custom-call(s32[3,6,16]{2,1,0:T(8,128)S(1)} %get-tuple-element.88.mask_ref, bf16[2048,768]{1,0:T(8,128)(2,1)S(1)} %get-tuple-element.95.ratings_ref, f32[2048,256]{1,0:T(8,128)S(1)} %get-tuple-element.96.r_ref, ...), custom_call_target="tpu_custom_call" | custom-call | flops 1000 | bytes 1000 | tf_op jit(solution)/shard_map/pallas_call | solution.py:64
  15.8 2.9 %collective-permute-start.3 = (f32[72,256]{1,0:T(8,128)S(1)}, f32[72,256]{1,0:T(8,128)S(1)}, u32[]{:S(2)}, u32[]{:S(2)}) collective-permute-start(f32[72,256]{1,0:T(8,128)S(1)} %shard_map.150.a_ref), channel_id=1, source_target_pairs={{0,8},{1,9},{2,10},{3,11},{4,12},{5,13},{6,14},{7,15},{8,0},{9,1},... | collective-permute-start | bytes 221192 | tf_op jit(solution)/shard_map/ppermute | solution.py:560
  18.7 2.1 %shard_map.151 = (f32[512,256]{1,0:T(8,128)S(1)}, f32[256,768]{1,0:T(8,128)S(1)}, bf16[2048,256]{1,0:T(8,128)(2,1)S(1)}, bf16[768,256]{1,0:T(8,128)(2,1)S(1)}) custom-call(s32[3,6,16]{2,1,0:T(8,128)S(1)} %get-tuple-element.88.mask_ref, bf16[2048,768]{1,0:T(8,128)(2,1)S(1)} %get-tuple-element.95.ratings_ref, f32[2048,256]{1,0:T(8,128)S(1)} %get-tuple-element.96.r_ref, ...), custom_call_target="tpu_custom_call" | custom-call | flops 1000 | bytes 1000 | tf_op jit(solution)/shard_map/pallas_call | solution.py:64
  21.1 1.8 %collective-permute-start.4 = (f32[72,256]{1,0:T(8,128)S(1)}, f32[72,256]{1,0:T(8,128)S(1)}, u32[]{:S(2)}, u32[]{:S(2)}) collective-permute-start(f32[72,256]{1,0:T(8,128)S(1)} %shard_map.152.mine_ref), channel_id=1, source_target_pairs={{0,2},{1,3},{2,0},{3,1},{4,6},{5,7},{6,4},{7,5},{8,10},{9,11},{10,... | collective-permute-start | bytes 221192 | tf_op jit(solution)/shard_map/ppermute | solution.py:560
  23.0 1.8 %shard_map.153 = (f32[512,256]{1,0:T(8,128)S(1)}, f32[256,768]{1,0:T(8,128)S(1)}, f32[256,256]{1,0:T(8,128)S(1)}, f32[256,256]{1,0:T(8,128)S(1)}) custom-call(s32[3,6,16]{2,1,0:T(8,128)S(1)} %get-tuple-element.88.mask_ref, bf16[2048,768]{1,0:T(8,128)(2,1)S(1)} %get-tuple-element.95.ratings_ref, f32[2048,256]{1,0:T(8,128)S(1)} %get-tuple-element.96.r_ref, ...), custom_call_target="tpu_custom_call" | custom-call | flops 1000 | bytes 1000 | tf_op jit(solution)/shard_map/pallas_call | solution.py:64
  24.8 0.4 shard_map.154
  25.2 0.3 collective-permute-done.4.other_ref
  25.6 0.8 collective-permute-start.6
  26.3 10.5 %shard_map.155.mine_ref = f32[264,256]{1,0:T(8,128)S(1)} custom-call(f32[72,256]{1,0:T(8,128)S(1)} %shard_map.152.mine_ref, f32[72,256]{1,0:T(8,128)S(1)} %collective-permute-done.4.other_ref, f32[256,256]{1,0:T(8,128)S(1)} %get-tuple-element.126.wu_ref, f32[256,256]{1,0:T(8,128)S(1)} %get-tuple-element.127.wi_ref), custom_call_target="tpu_custom_call" | custom-call | flops 1000 | bytes 1000 | tf_op jit(solution)/shard_map/pallas_call | solution.py:64
  36.9 1.5 %collective-permute-done.5.other_ref = f32[264,256]{1,0:T(8,128)S(1)} collective-permute-done((f32[264,256]{1,0:T(8,128)S(1)}, f32[264,256]{1,0:T(8,128)S(1)}, u32[]{:S(2)}, u32[]{:S(2)}) %collective-permute-start.5) | collective-permute-done | bytes 270368 | tf_op jit(solution)/shard_map/ppermute | solution.py:560
  38.4 2.1 %shard_map.156 = (f32[2048,256]{1,0:T(8,128)S(1)}, f32[2048,256]{1,0:T(8,128)S(1)}) custom-call(f32[264,256]{1,0:T(8,128)S(1)} %shard_map.155.mine_ref, f32[264,256]{1,0:T(8,128)S(1)} %collective-permute-done.5.other_ref, f32[2048,256]{1,0:T(8,128)S(1)} %get-tuple-element.119.u_ref.x_ref, f32[512,256]{1,0:T(8,128)S(1)} %get-tuple-element.128.refs_0_, ...), custom_call_target="tpu_custom_call" | custom-call | flops 1000 | bytes 1000 | tf_op jit(solution)/shard_map/pallas_call | solution.py:64
  40.6 3.7 %collective-permute-done.6.pack_ref = f32[1536,256]{1,0:T(8,128)S(1)} collective-permute-done((f32[1536,256]{1,0:T(8,128)S(1)}, f32[1536,256]{1,0:T(8,128)S(1)}, u32[]{:S(2)}, u32[]{:S(2)}) %collective-permute-start.6) | collective-permute-done | bytes 1572896 | tf_op jit(solution)/shard_map/ppermute | solution.py:636
  44.3 0.8 shard_map.157
  45.1 4.9 %collective-permute-start.7 = (f32[768,256]{1,0:T(8,128)S(1)}, f32[768,256]{1,0:T(8,128)S(1)}, u32[]{:S(2)}, u32[]{:S(2)}) collective-permute-start(f32[768,256]{1,0:T(8,128)S(1)} %get-tuple-element.135.refs_3_.even_ref.odd_ref), channel_id=1, source_target_pairs={{1,0},{3,2},{5,4},{7,6},{9,8},{11,10},{13,12},{15,14},{0,15},{2,1}... | collective-permute-start | bytes 2359304 | tf_op jit(solution)/shard_map/ppermute | solution.py:636
  50.0 3.0 %shard_map.158 = (bf16[2048,768]{1,0:T(8,128)(2,1)S(1)}, f32[768,256]{1,0:T(8,128)S(1)}) custom-call(s32[3,6,16]{2,1,0:T(8,128)S(1)} %get-tuple-element.88.mask_ref, f32[264,256]{1,0:T(8,128)S(1)} %shard_map.155.mine_ref, f32[264,256]{1,0:T(8,128)S(1)} %collective-permute-done.5.other_ref, bf16[2048,768]{1,0:T(8,128)(2,1)S(1)} %get-tuple-element.136.refs_0_, ...), custom_call_target="tpu_custom_call" | custom-call | flops 1000 | bytes 1000 | tf_op jit(solution)/shard_map/pallas_call | solution.py:64
  53.0 1.3 %collective-permute-start.8 = (f32[768,256]{1,0:T(8,128)S(1)}, f32[768,256]{1,0:T(8,128)S(1)}, u32[]{:S(2)}, u32[]{:S(2)}) collective-permute-start(f32[768,256]{1,0:T(8,128)S(1)} %get-tuple-element.152), channel_id=1, source_target_pairs={{1,0},{3,2},{5,4},{7,6},{9,8},{11,10},{13,12},{15,14},{17,16},{19,... | collective-permute-start | bytes 2359304 | tf_op jit(solution)/shard_map/ppermute | solution.py:636
  54.3 4.7 %collective-permute-start.10 = (f32[768,256]{1,0:T(8,128)S(1)}, f32[768,256]{1,0:T(8,128)S(1)}, u32[]{:S(2)}, u32[]{:S(2)}) collective-permute-start(f32[768,256]{1,0:T(8,128)S(1)} %get-tuple-element.152), channel_id=1, source_target_pairs={{0,15},{2,1},{4,3},{6,5},{8,7},{10,9},{12,11},{14,13},{16,31},{18,... | collective-permute-start | bytes 2359304 | tf_op jit(solution)/shard_map/ppermute | solution.py:636
  59.0 3.3 %shard_map.159 = (f32[2048,256]{1,0:T(8,128)S(1)}, f32[2048,256]{1,0:T(8,128)S(1)}, bf16[2048,768]{1,0:T(8,128)(2,1)S(1)}, bf16[2048,256]{1,0:T(8,128)(2,1)S(1)}, bf16[768,256]{1,0:T(8,128)(2,1)S(1)}) custom-call(f32[264,256]{1,0:T(8,128)S(1)} %shard_map.155.mine_ref, f32[264,256]{1,0:T(8,128)S(1)} %collective-permute-done.5.other_ref, ...), custom_call_target="tpu_custom_call" | custom-call | flops 1000 | bytes 1000 | tf_op jit(solution)/shard_map/pallas_call | solution.py:64
  62.3 3.0 %shard_map.160 = (bf16[2048,768]{1,0:T(8,128)(2,1)S(1)}, f32[1536,256]{1,0:T(8,128)S(1)}) custom-call(s32[3,6,16]{2,1,0:T(8,128)S(1)} %get-tuple-element.88.mask_ref, f32[264,256]{1,0:T(8,128)S(1)} %shard_map.155.mine_ref, f32[264,256]{1,0:T(8,128)S(1)} %collective-permute-done.5.other_ref, bf16[2048,768]{1,0:T(8,128)(2,1)S(1)} %get-tuple-element.148.refs_0_, ...), custom_call_target="tpu_custom_call" | custom-call | flops 1000 | bytes 1000 | tf_op jit(solution)/shard_map/pallas_call | solution.py:64
  65.3 1.4 %collective-permute-start.9 = (f32[1536,256]{1,0:T(8,128)S(1)}, f32[1536,256]{1,0:T(8,128)S(1)}, u32[]{:S(2)}, u32[]{:S(2)}) collective-permute-start(f32[1536,256]{1,0:T(8,128)S(1)} %get-tuple-element.153.even_ref), channel_id=1, source_target_pairs={{0,15},{2,1},{4,3},{6,5},{8,7},{10,9},{12,11},{14,13},{16,31},{18,... | collective-permute-start | bytes 4718600 | tf_op jit(solution)/shard_map/ppermute | solution.py:636
  66.7 1.8 %collective-permute-done.10.refs_4_ = f32[768,256]{1,0:T(8,128)S(1)} collective-permute-done((f32[768,256]{1,0:T(8,128)S(1)}, f32[768,256]{1,0:T(8,128)S(1)}, u32[]{:S(2)}, u32[]{:S(2)}) %collective-permute-start.10) | collective-permute-done | bytes 786464 | tf_op jit(solution)/shard_map/ppermute | solution.py:636
  68.5 1.5 %collective-permute-start.11 = (f32[1536,256]{1,0:T(8,128)S(1)}, f32[1536,256]{1,0:T(8,128)S(1)}, u32[]{:S(2)}, u32[]{:S(2)}) collective-permute-start(f32[1536,256]{1,0:T(8,128)S(1)} %get-tuple-element.158.odd_ref), channel_id=1, source_target_pairs={{1,0},{3,2},{5,4},{7,6},{9,8},{11,10},{13,12},{15,14},{17,16},{19,... | collective-permute-start | bytes 4718600 | tf_op jit(solution)/shard_map/ppermute | solution.py:636
  70.0 5.3 %shard_map.162 = (f32[2048,256]{1,0:T(8,128)}, f32[2048,256]{1,0:T(8,128)}, f32[256,256]{1,0:T(8,128)}, f32[256,256]{1,0:T(8,128)}) custom-call(f32[264,256]{1,0:T(8,128)S(1)} %shard_map.155.mine_ref, f32[264,256]{1,0:T(8,128)S(1)} %collective-permute-done.5.other_ref, bf16[2048,768]{1,0:T(8,128)(2,1)S(1)} %get-tuple-element.155.res_ref, ...), custom_call_target="tpu_custom_call" | custom-call | flops 1000 | bytes 1000 | tf_op jit(solution)/shard_map/pallas_call | solution.py:64
  75.3 10.0 %collective-permute-done.9.odd_ref = f32[1536,256]{1,0:T(8,128)S(1)} collective-permute-done((f32[1536,256]{1,0:T(8,128)S(1)}, f32[1536,256]{1,0:T(8,128)S(1)}, u32[]{:S(2)}, u32[]{:S(2)}) %collective-permute-start.9) | collective-permute-done | bytes 1572896 | tf_op jit(solution)/shard_map/ppermute | solution.py:636
  85.3 1.2 %shard_map.163 = (f32[768,256]{1,0:T(8,128)}, f32[768,256]{1,0:T(8,128)}) custom-call(f32[1536,256]{1,0:T(8,128)S(1)} %collective-permute-done.11.even_ref, f32[1536,256]{1,0:T(8,128)S(1)} %collective-permute-done.9.odd_ref), custom_call_target="tpu_custom_call" | custom-call | flops 1000 | bytes 1000 | tf_op jit(solution)/shard_map/pallas_call | solution.py:548
  (11 shorter events, 0.8 us)
Async XLA Ops:
  4.3 1.5 %collective-permute-start = (f32[144,256]{1,0:T(8,128)S(1)}, f32[144,256]{1,0:T(8,128)S(1)}, u32[]{:S(2)}, u32[]{:S(2)}) collective-permute-start(f32[144,256]{1,0:T(8,128)S(1)} %get-tuple-element.90), channel_id=1, source_target_pairs={{0,1},{1,0},{2,3},{3,2},{4,5},{5,4},{6,7},{7,6},{8,9},{9,8},{10,11... | collective-permute-start | bytes 442376 | tf_op jit(solution)/shard_map/ppermute | solution.py:560
  5.8 5.5 %collective-permute-start.1 = (f32[72,256]{1,0:T(8,128)S(1)}, f32[72,256]{1,0:T(8,128)S(1)}, u32[]{:S(2)}, u32[]{:S(2)}) collective-permute-start(f32[72,256]{1,0:T(8,128)S(1)} %get-tuple-element.94), channel_id=1, source_target_pairs={{0,2},{1,3},{2,0},{3,1},{4,6},{5,7},{6,4},{7,5},{8,10},{9,11},{10,... | collective-permute-start | bytes 221192 | tf_op jit(solution)/shard_map/ppermute | solution.py:560
  11.4 4.4 %collective-permute-start.2 = (f32[72,256]{1,0:T(8,128)S(1)}, f32[72,256]{1,0:T(8,128)S(1)}, u32[]{:S(2)}, u32[]{:S(2)}) collective-permute-start(f32[72,256]{1,0:T(8,128)S(1)} %shard_map.148.a_ref), channel_id=1, source_target_pairs={{0,4},{1,5},{2,6},{3,7},{4,0},{5,1},{6,2},{7,3},{8,12},{9,13},{10,... | collective-permute-start | bytes 221192 | tf_op jit(solution)/shard_map/ppermute | solution.py:560
  15.8 5.3 %collective-permute-start.3 = (f32[72,256]{1,0:T(8,128)S(1)}, f32[72,256]{1,0:T(8,128)S(1)}, u32[]{:S(2)}, u32[]{:S(2)}) collective-permute-start(f32[72,256]{1,0:T(8,128)S(1)} %shard_map.150.a_ref), channel_id=1, source_target_pairs={{0,8},{1,9},{2,10},{3,11},{4,12},{5,13},{6,14},{7,15},{8,0},{9,1},... | collective-permute-start | bytes 221192 | tf_op jit(solution)/shard_map/ppermute | solution.py:560
  21.1 4.4 %collective-permute-start.4 = (f32[72,256]{1,0:T(8,128)S(1)}, f32[72,256]{1,0:T(8,128)S(1)}, u32[]{:S(2)}, u32[]{:S(2)}) collective-permute-start(f32[72,256]{1,0:T(8,128)S(1)} %shard_map.152.mine_ref), channel_id=1, source_target_pairs={{0,2},{1,3},{2,0},{3,1},{4,6},{5,7},{6,4},{7,5},{8,10},{9,11},{10,... | collective-permute-start | bytes 221192 | tf_op jit(solution)/shard_map/ppermute | solution.py:560
  25.6 18.7 %collective-permute-start.6 = (f32[1536,256]{1,0:T(8,128)S(1)}, f32[1536,256]{1,0:T(8,128)S(1)}, u32[]{:S(2)}, u32[]{:S(2)}) collective-permute-start(f32[1536,256]{1,0:T(8,128)S(1)} %shard_map.154), channel_id=1, source_target_pairs={{1,0},{3,2},{5,4},{7,6},{9,8},{11,10},{13,12},{15,14},{0,15},{2,1}... | collective-permute-start | bytes 4718600 | tf_op jit(solution)/shard_map/ppermute | solution.py:636
  36.8 1.6 %collective-permute-start.5 = (f32[264,256]{1,0:T(8,128)S(1)}, f32[264,256]{1,0:T(8,128)S(1)}, u32[]{:S(2)}, u32[]{:S(2)}) collective-permute-start(f32[264,256]{1,0:T(8,128)S(1)} %shard_map.155.mine_ref), channel_id=1, source_target_pairs={{0,1},{1,0},{2,3},{3,2},{4,5},{5,4},{6,7},{7,6},{8,9},{9,8},{10,11... | collective-permute-start | bytes 811016 | tf_op jit(solution)/shard_map/ppermute | solution.py:560
  45.1 17.2 %collective-permute-start.7 = (f32[768,256]{1,0:T(8,128)S(1)}, f32[768,256]{1,0:T(8,128)S(1)}, u32[]{:S(2)}, u32[]{:S(2)}) collective-permute-start(f32[768,256]{1,0:T(8,128)S(1)} %get-tuple-element.135.refs_3_.even_ref.odd_ref), channel_id=1, source_target_pairs={{1,0},{3,2},{5,4},{7,6},{9,8},{11,10},{13,12},{15,14},{0,15},{2,1}... | collective-permute-start | bytes 2359304 | tf_op jit(solution)/shard_map/ppermute | solution.py:636
  53.0 9.4 %collective-permute-start.8 = (f32[768,256]{1,0:T(8,128)S(1)}, f32[768,256]{1,0:T(8,128)S(1)}, u32[]{:S(2)}, u32[]{:S(2)}) collective-permute-start(f32[768,256]{1,0:T(8,128)S(1)} %get-tuple-element.152), channel_id=1, source_target_pairs={{1,0},{3,2},{5,4},{7,6},{9,8},{11,10},{13,12},{15,14},{17,16},{19,... | collective-permute-start | bytes 2359304 | tf_op jit(solution)/shard_map/ppermute | solution.py:636
  54.3 14.2 %collective-permute-start.10 = (f32[768,256]{1,0:T(8,128)S(1)}, f32[768,256]{1,0:T(8,128)S(1)}, u32[]{:S(2)}, u32[]{:S(2)}) collective-permute-start(f32[768,256]{1,0:T(8,128)S(1)} %get-tuple-element.152), channel_id=1, source_target_pairs={{0,15},{2,1},{4,3},{6,5},{8,7},{10,9},{12,11},{14,13},{16,31},{18,... | collective-permute-start | bytes 2359304 | tf_op jit(solution)/shard_map/ppermute | solution.py:636
  65.3 20.0 %collective-permute-start.9 = (f32[1536,256]{1,0:T(8,128)S(1)}, f32[1536,256]{1,0:T(8,128)S(1)}, u32[]{:S(2)}, u32[]{:S(2)}) collective-permute-start(f32[1536,256]{1,0:T(8,128)S(1)} %get-tuple-element.153.even_ref), channel_id=1, source_target_pairs={{0,15},{2,1},{4,3},{6,5},{8,7},{10,9},{12,11},{14,13},{16,31},{18,... | collective-permute-start | bytes 4718600 | tf_op jit(solution)/shard_map/ppermute | solution.py:636
  68.5 16.9 %collective-permute-start.11 = (f32[1536,256]{1,0:T(8,128)S(1)}, f32[1536,256]{1,0:T(8,128)S(1)}, u32[]{:S(2)}, u32[]{:S(2)}) collective-permute-start(f32[1536,256]{1,0:T(8,128)S(1)} %get-tuple-element.158.odd_ref), channel_id=1, source_target_pairs={{1,0},{3,2},{5,4},{7,6},{9,8},{11,10},{13,12},{15,14},{17,16},{19,... | collective-permute-start | bytes 4718600 | tf_op jit(solution)/shard_map/ppermute | solution.py:636

commit v4 on v3

--- a/solution.py
+++ b/solution.py
@@ -577,8 +577,9 @@
     item_rows = item_factors.shape[0]
     weight = 1.0 * blocks
     fence = lax.optimization_barrier
-    inside = [(i, i - 1) for i in range(1, blocks, 2)]
+    inside = [(i, i ^ 1) for i in range(blocks)]
     across = [(i, (i - 1) % blocks) for i in range(0, blocks, 2)]
+    ring = [(i, (i - 1) % blocks) for i in range(blocks)]
 
     mask = tile_mask.transpose(0, 2, 1)
     parts = 4
@@ -634,7 +635,7 @@
     item_part = item_start(weight, near_w, loaded[0][1], loaded[0][2], accs)
     other, item_part, *rts = fence((other, item_part, *rts))
     send = lambda array, pairs: lax.ppermute(array, "blk", pairs)
-    early = send(item_part, inside + across)
+    early = send(item_part, ring)
     wu, wi = loaded[3]
     near = (loaded[1][0], *loaded[2])
     counts = (1.0 * user_rows * blocks, 1.0 * item_rows * blocks)
@@ -644,7 +645,7 @@
     users, early = fence((users, early))
     items, item_mom = first_items(drawn, peer, early)
 
-    before = send(items, inside + across)
+    before = send(items, ring)
     args = (mask, drawn, peer, near[0], users, near[2])
     res, item_mom = items_step(weight, 1, None, *args, items, item_mom)
     q_even, q_odd = send(item_mom, inside), send(item_mom, across)

time: 87 us -> 86.4 us (level)
  transfers between devices with their start and end apart: 12 -> 12, of which waited for: 9 -> 9; matrix products, arithmetic and copies ran while one was open for 0% -> 0% of each run, Pallas kernels for 41% -> 42%
where the time goes in v4:
time: 86.4 us; the launch traced here: 86.1 us
  Pallas kernels  41.5 us (48%)
  starting transfers between devices  24.9 us (29%)
  waiting for transfers between devices  18.7 us (22%)
  between operations  1 us (1%)
    pallas_call x18, Pallas kernels, placed(): run(*(pltpu.with_memory_space_constraint(a, spaces[id(s)]) if id(s) in sp...  40.4 us
    ppermute x6, waiting for transfers between devices, local(): send = lambda array, pairs: lax.ppermute(array, 'blk', pairs)  14.9 us
    ppermute x6, starting transfers between devices, local(): send = lambda array, pairs: lax.ppermute(array, 'blk', pairs)  14.7 us
    ppermute x6, starting transfers between devices, swapped(): return lax.ppermute(array, 'blk', [(i, i ^ by) for i in range(size)])  10.2 us
    ppermute x6, waiting for transfers between devices, swapped(): return lax.ppermute(array, 'blk', [(i, i ^ by) for i in range(size)])  3.83 us
  transfers between devices with their start and end apart: 12, of which 9 were waited for; matrix products, arithmetic and copies ran while one was open for 0% of the time, Pallas kernels for 42%

profile of v4, /device:TPU:0, one launch (start us, length us, event | category | flops | bytes accessed | tf_op | source)
XLA Modules:
  0.0 86.1 jit_solution(4100340108685610363)
XLA Ops:
  0.6 3.6 %shard_map.145 = (f32[144,256]{1,0:T(8,128)S(1)}, f32[144,256]{1,0:T(8,128)S(1)}, f32[2048,256]{1,0:T(8,128)S(1)}, f32[768,256]{1,0:T(8,128)S(1)}, bf16[2048,768...) custom-call(f32[2048,256]{1,0:T(8,128)} %u_hbm.1, f32[768,256]{1,0:T(8,128)} %w_hbm.1, ...), custom_call_target="tpu_custom_call" | custom-call | flops 1000 | bytes 1000 | tf_op jit(solution)/shard_map/pallas_call | solution.py:64
  4.3 0.5 collective-permute-start
  4.8 1.0 %collective-permute-done.got_ref = f32[144,256]{1,0:T(8,128)S(1)} collective-permute-done((f32[144,256]{1,0:T(8,128)S(1)}, f32[144,256]{1,0:T(8,128)S(1)}, u32[]{:S(2)}, u32[]{:S(2)}) %collective-permute-start) | collective-permute-done | bytes 147488 | tf_op jit(solution)/shard_map/ppermute | solution.py:560
  5.8 2.9 %collective-permute-start.1 = (f32[72,256]{1,0:T(8,128)S(1)}, f32[72,256]{1,0:T(8,128)S(1)}, u32[]{:S(2)}, u32[]{:S(2)}) collective-permute-start(f32[72,256]{1,0:T(8,128)S(1)} %get-tuple-element.94), channel_id=1, source_target_pairs={{0,2},{1,3},{2,0},{3,1},{4,6},{5,7},{6,4},{7,5},{8,10},{9,11},{10,... | collective-permute-start | bytes 221192 | tf_op jit(solution)/shard_map/ppermute | solution.py:560
  8.8 2.2 %shard_map.147 = (f32[512,256]{1,0:T(8,128)S(1)}, f32[256,768]{1,0:T(8,128)S(1)}, bf16[2048,256]{1,0:T(8,128)(2,1)S(1)}, f32[768,256]{1,0:T(8,128)S(1)}, bf16[768,256]{1,0:T(8,128)(2,1)S(1)}) custom-call(s32[3,6,16]{2,1,0:T(8,128)S(1)} %get-tuple-element.88.mask_ref, bf16[2048,768]{1,0:T(8,128)(2,1)S(1)} %get-tuple-element.95.ratings_ref, ...), custom_call_target="tpu_custom_call" | custom-call | flops 1000 | bytes 1000 | tf_op jit(solution)/shard_map/pallas_call | solution.py:64
  11.0 0.3 collective-permute-done.1.b_ref
  11.4 1.9 %collective-permute-start.2 = (f32[72,256]{1,0:T(8,128)S(1)}, f32[72,256]{1,0:T(8,128)S(1)}, u32[]{:S(2)}, u32[]{:S(2)}) collective-permute-start(f32[72,256]{1,0:T(8,128)S(1)} %shard_map.148.a_ref), channel_id=1, source_target_pairs={{0,4},{1,5},{2,6},{3,7},{4,0},{5,1},{6,2},{7,3},{8,12},{9,13},{10,... | collective-permute-start | bytes 221192 | tf_op jit(solution)/shard_map/ppermute | solution.py:560
  13.3 2.2 %shard_map.149 = (f32[512,256]{1,0:T(8,128)S(1)}, f32[256,768]{1,0:T(8,128)S(1)}, bf16[2048,768]{1,0:T(8,128)(2,1)S(1)}) custom-call(s32[3,6,16]{2,1,0:T(8,128)S(1)} %get-tuple-element.88.mask_ref, bf16[2048,768]{1,0:T(8,128)(2,1)S(1)} %get-tuple-element.95.ratings_ref, f32[2048,256]{1,0:T(8,128)S(1)} %get-tuple-element.96.r_ref, ...), custom_call_target="tpu_custom_call" | custom-call | flops 1000 | bytes 1000 | tf_op jit(solution)/shard_map/pallas_call | solution.py:64
  15.8 2.9 %collective-permute-start.3 = (f32[72,256]{1,0:T(8,128)S(1)}, f32[72,256]{1,0:T(8,128)S(1)}, u32[]{:S(2)}, u32[]{:S(2)}) collective-permute-start(f32[72,256]{1,0:T(8,128)S(1)} %shard_map.150.a_ref), channel_id=1, source_target_pairs={{0,8},{1,9},{2,10},{3,11},{4,12},{5,13},{6,14},{7,15},{8,0},{9,1},... | collective-permute-start | bytes 221192 | tf_op jit(solution)/shard_map/ppermute | solution.py:560
  18.7 2.1 %shard_map.151 = (f32[512,256]{1,0:T(8,128)S(1)}, f32[256,768]{1,0:T(8,128)S(1)}, bf16[2048,256]{1,0:T(8,128)(2,1)S(1)}, bf16[768,256]{1,0:T(8,128)(2,1)S(1)}) custom-call(s32[3,6,16]{2,1,0:T(8,128)S(1)} %get-tuple-element.88.mask_ref, bf16[2048,768]{1,0:T(8,128)(2,1)S(1)} %get-tuple-element.95.ratings_ref, f32[2048,256]{1,0:T(8,128)S(1)} %get-tuple-element.96.r_ref, ...), custom_call_target="tpu_custom_call" | custom-call | flops 1000 | bytes 1000 | tf_op jit(solution)/shard_map/pallas_call | solution.py:64
  20.8 0.3 collective-permute-done.3.b_ref
  21.1 1.8 %collective-permute-start.4 = (f32[72,256]{1,0:T(8,128)S(1)}, f32[72,256]{1,0:T(8,128)S(1)}, u32[]{:S(2)}, u32[]{:S(2)}) collective-permute-start(f32[72,256]{1,0:T(8,128)S(1)} %shard_map.152.mine_ref), channel_id=1, source_target_pairs={{0,2},{1,3},{2,0},{3,1},{4,6},{5,7},{6,4},{7,5},{8,10},{9,11},{10,... | collective-permute-start | bytes 221192 | tf_op jit(solution)/shard_map/ppermute | solution.py:560
  23.0 1.8 %shard_map.153 = (f32[512,256]{1,0:T(8,128)S(1)}, f32[256,768]{1,0:T(8,128)S(1)}, f32[256,256]{1,0:T(8,128)S(1)}, f32[256,256]{1,0:T(8,128)S(1)}) custom-call(s32[3,6,16]{2,1,0:T(8,128)S(1)} %get-tuple-element.88.mask_ref, bf16[2048,768]{1,0:T(8,128)(2,1)S(1)} %get-tuple-element.95.ratings_ref, f32[2048,256]{1,0:T(8,128)S(1)} %get-tuple-element.96.r_ref, ...), custom_call_target="tpu_custom_call" | custom-call | flops 1000 | bytes 1000 | tf_op jit(solution)/shard_map/pallas_call | solution.py:64
  24.8 0.4 shard_map.154
  25.2 0.3 collective-permute-done.4.other_ref
  25.6 0.8 collective-permute-start.6
  26.3 10.5 %shard_map.155.mine_ref = f32[264,256]{1,0:T(8,128)S(1)} custom-call(f32[72,256]{1,0:T(8,128)S(1)} %shard_map.152.mine_ref, f32[72,256]{1,0:T(8,128)S(1)} %collective-permute-done.4.other_ref, f32[256,256]{1,0:T(8,128)S(1)} %get-tuple-element.126.wu_ref, f32[256,256]{1,0:T(8,128)S(1)} %get-tuple-element.127.wi_ref), custom_call_target="tpu_custom_call" | custom-call | flops 1000 | bytes 1000 | tf_op jit(solution)/shard_map/pallas_call | solution.py:64
  36.9 1.5 %collective-permute-done.5.other_ref = f32[264,256]{1,0:T(8,128)S(1)} collective-permute-done((f32[264,256]{1,0:T(8,128)S(1)}, f32[264,256]{1,0:T(8,128)S(1)}, u32[]{:S(2)}, u32[]{:S(2)}) %collective-permute-start.5) | collective-permute-done | bytes 270368 | tf_op jit(solution)/shard_map/ppermute | solution.py:560
  38.4 2.1 %shard_map.156 = (f32[2048,256]{1,0:T(8,128)S(1)}, f32[2048,256]{1,0:T(8,128)S(1)}) custom-call(f32[264,256]{1,0:T(8,128)S(1)} %shard_map.155.mine_ref, f32[264,256]{1,0:T(8,128)S(1)} %collective-permute-done.5.other_ref, f32[2048,256]{1,0:T(8,128)S(1)} %get-tuple-element.119.u_ref.x_ref, f32[512,256]{1,0:T(8,128)S(1)} %get-tuple-element.128.refs_0_, ...), custom_call_target="tpu_custom_call" | custom-call | flops 1000 | bytes 1000 | tf_op jit(solution)/shard_map/pallas_call | solution.py:64
  40.6 3.7 %collective-permute-done.6.pack_ref = f32[1536,256]{1,0:T(8,128)S(1)} collective-permute-done((f32[1536,256]{1,0:T(8,128)S(1)}, f32[1536,256]{1,0:T(8,128)S(1)}, u32[]{:S(2)}, u32[]{:S(2)}) %collective-permute-start.6) | collective-permute-done | bytes 1572896 | tf_op jit(solution)/shard_map/ppermute | solution.py:637
  44.3 0.8 shard_map.157
  45.1 4.9 %collective-permute-start.7 = (f32[768,256]{1,0:T(8,128)S(1)}, f32[768,256]{1,0:T(8,128)S(1)}, u32[]{:S(2)}, u32[]{:S(2)}) collective-permute-start(f32[768,256]{1,0:T(8,128)S(1)} %get-tuple-element.135.refs_3_.even_ref.odd_ref), channel_id=1, source_target_pairs={{0,15},{1,0},{2,1},{3,2},{4,3},{5,4},{6,5},{7,6},{8,7},{9,8},{10,9... | collective-permute-start | bytes 2359304 | tf_op jit(solution)/shard_map/ppermute | solution.py:637
  50.0 3.0 %shard_map.158 = (bf16[2048,768]{1,0:T(8,128)(2,1)S(1)}, f32[768,256]{1,0:T(8,128)S(1)}) custom-call(s32[3,6,16]{2,1,0:T(8,128)S(1)} %get-tuple-element.88.mask_ref, f32[264,256]{1,0:T(8,128)S(1)} %shard_map.155.mine_ref, f32[264,256]{1,0:T(8,128)S(1)} %collective-permute-done.5.other_ref, bf16[2048,768]{1,0:T(8,128)(2,1)S(1)} %get-tuple-element.136.refs_0_, ...), custom_call_target="tpu_custom_call" | custom-call | flops 1000 | bytes 1000 | tf_op jit(solution)/shard_map/pallas_call | solution.py:64
  53.0 4.1 %collective-permute-start.10 = (f32[768,256]{1,0:T(8,128)S(1)}, f32[768,256]{1,0:T(8,128)S(1)}, u32[]{:S(2)}, u32[]{:S(2)}) collective-permute-start(f32[768,256]{1,0:T(8,128)S(1)} %get-tuple-element.152), channel_id=1, source_target_pairs={{0,15},{2,1},{4,3},{6,5},{8,7},{10,9},{12,11},{14,13},{16,31},{18,... | collective-permute-start | bytes 2359304 | tf_op jit(solution)/shard_map/ppermute | solution.py:637
  57.1 3.3 %shard_map.159 = (f32[2048,256]{1,0:T(8,128)S(1)}, f32[2048,256]{1,0:T(8,128)S(1)}, bf16[2048,768]{1,0:T(8,128)(2,1)S(1)}, bf16[2048,256]{1,0:T(8,128)(2,1)S(1)}, bf16[768,256]{1,0:T(8,128)(2,1)S(1)}) custom-call(f32[264,256]{1,0:T(8,128)S(1)} %shard_map.155.mine_ref, f32[264,256]{1,0:T(8,128)S(1)} %collective-permute-done.5.other_ref, ...), custom_call_target="tpu_custom_call" | custom-call | flops 1000 | bytes 1000 | tf_op jit(solution)/shard_map/pallas_call | solution.py:64
  60.4 3.0 %shard_map.160 = (bf16[2048,768]{1,0:T(8,128)(2,1)S(1)}, f32[1536,256]{1,0:T(8,128)S(1)}) custom-call(s32[3,6,16]{2,1,0:T(8,128)S(1)} %get-tuple-element.88.mask_ref, f32[264,256]{1,0:T(8,128)S(1)} %shard_map.155.mine_ref, f32[264,256]{1,0:T(8,128)S(1)} %collective-permute-done.5.other_ref, bf16[2048,768]{1,0:T(8,128)(2,1)S(1)} %get-tuple-element.148.refs_0_, ...), custom_call_target="tpu_custom_call" | custom-call | flops 1000 | bytes 1000 | tf_op jit(solution)/shard_map/pallas_call | solution.py:64
  63.4 2.7 %collective-permute-start.9 = (f32[1536,256]{1,0:T(8,128)S(1)}, f32[1536,256]{1,0:T(8,128)S(1)}, u32[]{:S(2)}, u32[]{:S(2)}) collective-permute-start(f32[1536,256]{1,0:T(8,128)S(1)} %get-tuple-element.153.even_ref), channel_id=1, source_target_pairs={{0,15},{2,1},{4,3},{6,5},{8,7},{10,9},{12,11},{14,13},{16,31},{18,... | collective-permute-start | bytes 4718600 | tf_op jit(solution)/shard_map/ppermute | solution.py:637
  66.1 1.8 %collective-permute-done.10.refs_4_ = f32[768,256]{1,0:T(8,128)S(1)} collective-permute-done((f32[768,256]{1,0:T(8,128)S(1)}, f32[768,256]{1,0:T(8,128)S(1)}, u32[]{:S(2)}, u32[]{:S(2)}) %collective-permute-start.10) | collective-permute-done | bytes 786464 | tf_op jit(solution)/shard_map/ppermute | solution.py:637
  67.9 2.2 %collective-permute-start.11 = (f32[1536,256]{1,0:T(8,128)S(1)}, f32[1536,256]{1,0:T(8,128)S(1)}, u32[]{:S(2)}, u32[]{:S(2)}) collective-permute-start(f32[1536,256]{1,0:T(8,128)S(1)} %get-tuple-element.158.odd_ref), channel_id=1, source_target_pairs={{0,1},{1,0},{2,3},{3,2},{4,5},{5,4},{6,7},{7,6},{8,9},{9,8},{10,11... | collective-permute-start | bytes 4718600 | tf_op jit(solution)/shard_map/ppermute | solution.py:637
  70.1 5.3 %shard_map.162 = (f32[2048,256]{1,0:T(8,128)}, f32[2048,256]{1,0:T(8,128)}, f32[256,256]{1,0:T(8,128)}, f32[256,256]{1,0:T(8,128)}) custom-call(f32[264,256]{1,0:T(8,128)S(1)} %shard_map.155.mine_ref, f32[264,256]{1,0:T(8,128)S(1)} %collective-permute-done.5.other_ref, bf16[2048,768]{1,0:T(8,128)(2,1)S(1)} %get-tuple-element.155.res_ref, ...), custom_call_target="tpu_custom_call" | custom-call | flops 1000 | bytes 1000 | tf_op jit(solution)/shard_map/pallas_call | solution.py:64
  75.4 9.4 %collective-permute-done.9.odd_ref = f32[1536,256]{1,0:T(8,128)S(1)} collective-permute-done((f32[1536,256]{1,0:T(8,128)S(1)}, f32[1536,256]{1,0:T(8,128)S(1)}, u32[]{:S(2)}, u32[]{:S(2)}) %collective-permute-start.9) | collective-permute-done | bytes 1572896 | tf_op jit(solution)/shard_map/ppermute | solution.py:637
  84.8 1.2 %shard_map.163 = (f32[768,256]{1,0:T(8,128)}, f32[768,256]{1,0:T(8,128)}) custom-call(f32[1536,256]{1,0:T(8,128)S(1)} %collective-permute-done.11.even_ref, f32[1536,256]{1,0:T(8,128)S(1)} %collective-permute-done.9.odd_ref), custom_call_target="tpu_custom_call" | custom-call | flops 1000 | bytes 1000 | tf_op jit(solution)/shard_map/pallas_call | solution.py:548
  (11 shorter events, 0.5 us)
Async XLA Ops:
  4.3 1.5 %collective-permute-start = (f32[144,256]{1,0:T(8,128)S(1)}, f32[144,256]{1,0:T(8,128)S(1)}, u32[]{:S(2)}, u32[]{:S(2)}) collective-permute-start(f32[144,256]{1,0:T(8,128)S(1)} %get-tuple-element.90), channel_id=1, source_target_pairs={{0,1},{1,0},{2,3},{3,2},{4,5},{5,4},{6,7},{7,6},{8,9},{9,8},{10,11... | collective-permute-start | bytes 442376 | tf_op jit(solution)/shard_map/ppermute | solution.py:560
  5.8 5.5 %collective-permute-start.1 = (f32[72,256]{1,0:T(8,128)S(1)}, f32[72,256]{1,0:T(8,128)S(1)}, u32[]{:S(2)}, u32[]{:S(2)}) collective-permute-start(f32[72,256]{1,0:T(8,128)S(1)} %get-tuple-element.94), channel_id=1, source_target_pairs={{0,2},{1,3},{2,0},{3,1},{4,6},{5,7},{6,4},{7,5},{8,10},{9,11},{10,... | collective-permute-start | bytes 221192 | tf_op jit(solution)/shard_map/ppermute | solution.py:560
  11.4 4.4 %collective-permute-start.2 = (f32[72,256]{1,0:T(8,128)S(1)}, f32[72,256]{1,0:T(8,128)S(1)}, u32[]{:S(2)}, u32[]{:S(2)}) collective-permute-start(f32[72,256]{1,0:T(8,128)S(1)} %shard_map.148.a_ref), channel_id=1, source_target_pairs={{0,4},{1,5},{2,6},{3,7},{4,0},{5,1},{6,2},{7,3},{8,12},{9,13},{10,... | collective-permute-start | bytes 221192 | tf_op jit(solution)/shard_map/ppermute | solution.py:560
  15.8 5.3 %collective-permute-start.3 = (f32[72,256]{1,0:T(8,128)S(1)}, f32[72,256]{1,0:T(8,128)S(1)}, u32[]{:S(2)}, u32[]{:S(2)}) collective-permute-start(f32[72,256]{1,0:T(8,128)S(1)} %shard_map.150.a_ref), channel_id=1, source_target_pairs={{0,8},{1,9},{2,10},{3,11},{4,12},{5,13},{6,14},{7,15},{8,0},{9,1},... | collective-permute-start | bytes 221192 | tf_op jit(solution)/shard_map/ppermute | solution.py:560
  21.1 4.4 %collective-permute-start.4 = (f32[72,256]{1,0:T(8,128)S(1)}, f32[72,256]{1,0:T(8,128)S(1)}, u32[]{:S(2)}, u32[]{:S(2)}) collective-permute-start(f32[72,256]{1,0:T(8,128)S(1)} %shard_map.152.mine_ref), channel_id=1, source_target_pairs={{0,2},{1,3},{2,0},{3,1},{4,6},{5,7},{6,4},{7,5},{8,10},{9,11},{10,... | collective-permute-start | bytes 221192 | tf_op jit(solution)/shard_map/ppermute | solution.py:560
  25.6 18.7 %collective-permute-start.6 = (f32[1536,256]{1,0:T(8,128)S(1)}, f32[1536,256]{1,0:T(8,128)S(1)}, u32[]{:S(2)}, u32[]{:S(2)}) collective-permute-start(f32[1536,256]{1,0:T(8,128)S(1)} %shard_map.154), channel_id=1, source_target_pairs={{0,15},{1,0},{2,1},{3,2},{4,3},{5,4},{6,5},{7,6},{8,7},{9,8},{10,9... | collective-permute-start | bytes 4718600 | tf_op jit(solution)/shard_map/ppermute | solution.py:637
  36.8 1.6 %collective-permute-start.5 = (f32[264,256]{1,0:T(8,128)S(1)}, f32[264,256]{1,0:T(8,128)S(1)}, u32[]{:S(2)}, u32[]{:S(2)}) collective-permute-start(f32[264,256]{1,0:T(8,128)S(1)} %shard_map.155.mine_ref), channel_id=1, source_target_pairs={{0,1},{1,0},{2,3},{3,2},{4,5},{5,4},{6,7},{7,6},{8,9},{9,8},{10,11... | collective-permute-start | bytes 811016 | tf_op jit(solution)/shard_map/ppermute | solution.py:560
  45.1 15.3 %collective-permute-start.7 = (f32[768,256]{1,0:T(8,128)S(1)}, f32[768,256]{1,0:T(8,128)S(1)}, u32[]{:S(2)}, u32[]{:S(2)}) collective-permute-start(f32[768,256]{1,0:T(8,128)S(1)} %get-tuple-element.135.refs_3_.even_ref.odd_ref), channel_id=1, source_target_pairs={{0,15},{1,0},{2,1},{3,2},{4,3},{5,4},{6,5},{7,6},{8,7},{9,8},{10,9... | collective-permute-start | bytes 2359304 | tf_op jit(solution)/shard_map/ppermute | solution.py:637
  53.0 7.5 %collective-permute-start.8 = (f32[768,256]{1,0:T(8,128)S(1)}, f32[768,256]{1,0:T(8,128)S(1)}, u32[]{:S(2)}, u32[]{:S(2)}) collective-permute-start(f32[768,256]{1,0:T(8,128)S(1)} %get-tuple-element.152), channel_id=1, source_target_pairs={{0,1},{1,0},{2,3},{3,2},{4,5},{5,4},{6,7},{7,6},{8,9},{9,8},{10,11... | collective-permute-start | bytes 2359304 | tf_op jit(solution)/shard_map/ppermute | solution.py:637
  53.0 14.9 %collective-permute-start.10 = (f32[768,256]{1,0:T(8,128)S(1)}, f32[768,256]{1,0:T(8,128)S(1)}, u32[]{:S(2)}, u32[]{:S(2)}) collective-permute-start(f32[768,256]{1,0:T(8,128)S(1)} %get-tuple-element.152), channel_id=1, source_target_pairs={{0,15},{2,1},{4,3},{6,5},{8,7},{10,9},{12,11},{14,13},{16,31},{18,... | collective-permute-start | bytes 2359304 | tf_op jit(solution)/shard_map/ppermute | solution.py:637
  63.4 21.4 %collective-permute-start.9 = (f32[1536,256]{1,0:T(8,128)S(1)}, f32[1536,256]{1,0:T(8,128)S(1)}, u32[]{:S(2)}, u32[]{:S(2)}) collective-permute-start(f32[1536,256]{1,0:T(8,128)S(1)} %get-tuple-element.153.even_ref), channel_id=1, source_target_pairs={{0,15},{2,1},{4,3},{6,5},{8,7},{10,9},{12,11},{14,13},{16,31},{18,... | collective-permute-start | bytes 4718600 | tf_op jit(solution)/shard_map/ppermute | solution.py:637
  67.9 16.9 %collective-permute-start.11 = (f32[1536,256]{1,0:T(8,128)S(1)}, f32[1536,256]{1,0:T(8,128)S(1)}, u32[]{:S(2)}, u32[]{:S(2)}) collective-permute-start(f32[1536,256]{1,0:T(8,128)S(1)} %get-tuple-element.158.odd_ref), channel_id=1, source_target_pairs={{0,1},{1,0},{2,3},{3,2},{4,5},{5,4},{6,7},{7,6},{8,9},{9,8},{10,11... | collective-permute-start | bytes 4718600 | tf_op jit(solution)/shard_map/ppermute | solution.py:637

commit v5 on v4

--- a/solution.py
+++ b/solution.py
@@ -145,31 +145,28 @@
     others, (keep_ref, send_ref, u_ref, w_ref) = refs[:count], refs[count : count + 4]
     nears = refs[count + 4 : -1]
     first = parity() == 0
-    rows = u_ref.shape[0] // 2
-    copies = [pltpu.make_async_copy(w_hbm, w_ref, sems.at[0])]
-    for j in range(2):
-        part = pl.ds(j * rows, rows)
-        copies.append(pltpu.make_async_copy(u_hbm.at[part], u_ref.at[part], sems.at[j + 1]))
-    copies += fetches(slots, others, nears, sems.at[pl.ds(3, CHUNKS * count)])
+    copies = [
+        pltpu.make_async_copy(w_hbm, w_ref, sems.at[0]),
+        pltpu.make_async_copy(u_hbm, u_ref, sems.at[1]),
+    ]
+    copies += fetches(slots, others, nears, sems.at[pl.ds(2, CHUNKS * count)])
     for copy in copies:
         copy.start()
     copies[0].wait()
     item = w_ref[...]
     gram_i = gram_of(item)
     total_i = jnp.sum(item, 0, keepdims=True)
-    gram_u, total_u = 0.0, 0.0
-    for j in range(2):
-        copies[j + 1].wait()
-        user = u_ref[j * rows : (j + 1) * rows]
-        gram_u += gram_of(user)
-        total_u += jnp.sum(user, 0, keepdims=True)
+    copies[1].wait()
+    user = u_ref[...]
+    gram_u = gram_of(user)
+    total_u = jnp.sum(user, 0, keepdims=True)
     store_packed(
         keep_ref, jnp.where(first, gram_u, gram_i), jnp.where(first, total_u, total_i)
     )
     store_packed(
         send_ref, jnp.where(first, gram_i, gram_u), jnp.where(first, total_i, total_u)
     )
-    for copy in copies[3:]:
+    for copy in copies[2:]:
         copy.wait()
 
 
@@ -180,7 +177,7 @@
         functools.partial(gram_kernel, slots),
         (packed, packed, shape(*users.shape), shape(*items.shape), *near_shapes(later)),
         [ANY, ANY] + [ANY] * len(later),
-        [fetch_sems(later, 3)],
+        [fetch_sems(later, 2)],
     )(users, items, *fars)
 
 
@@ -240,7 +237,12 @@
     return jnp.concatenate(done, 0)
 
 
-def draw_kernel(counts, mine_ref, other_ref, wu_ref, wi_ref, out_ref):
+def draw_kernel(counts, slots, mine_ref, other_ref, wu_ref, wi_ref, *refs):
+    count = len(slots)
+    fars, out_ref, nears, sems = refs[:count], refs[count], refs[count + 1 : -1], refs[-1]
+    copies = fetches(slots, fars, nears, sems)
+    for copy in copies:
+        copy.start()
     first = parity() == 0
     lower = upper_half() == 0
     n = jnp.where(first, counts[0], counts[1])
@@ -275,14 +277,19 @@
     both = jnp.concatenate([top, low], 0)
     out_ref[0:RANK] = dot(both, both, 1, 1, HIGHEST)
     out_ref[RANK:] = n * mean / (2.0 + n)
-
-
-def draw(counts, mine, other, wishart_user, wishart_item):
-    return call(
-        functools.partial(draw_kernel, counts),
-        shape(RANK + 8, RANK),
-        [VMEM, VMEM, VMEM, VMEM],
-    )(mine, other, wishart_user, wishart_item)
+    for copy in copies:
+        copy.wait()
+
+
+def draw(counts, mine, other, wishart_user, wishart_item, later):
+    slots, fars = zip(*later)
+    drawn, *nears = call(
+        functools.partial(draw_kernel, counts, slots),
+        (shape(RANK + 8, RANK), *near_shapes(later)),
+        [VMEM] * 4 + [ANY] * len(later),
+        [fetch_sems(later)],
+    )(mine, other, wishart_user, wishart_item, *fars)
+    return drawn, nears
 
 
 def prior_of(users, mine_ref, other_ref):
@@ -377,7 +384,8 @@
 
 
 def finish_kernel(mine_ref, other_ref, x_ref, *refs):
-    parts, (x_out, m_out, rhs_ref) = refs[:-3], refs[-3:]
+    parts, (x_out, m_out, item_ref, rhs_ref) = refs[:-4], refs[-4:]
+    item_ref[...] = prior_of(False, mine_ref, other_ref)[0]
     rhs, center = prior_of(True, mine_ref, other_ref)
     rhs_ref[...] = rhs
     rows = 256
@@ -397,25 +405,26 @@
     n, k = x.shape
     return call(
         finish_kernel,
-        (shape(n, k), shape(n, k)),
+        (shape(n, k), shape(n, k), shape(6 * RANK, k, BF16)),
         [VMEM] * (3 + len(parts)),
         [pltpu.VMEM((6 * RANK, k), BF16)],
     )(mine, other, x, *parts)
 
 
-def first_items_kernel(mine_ref, other_ref, pack_ref, w_out, q_out):
-    rhs, center = prior_of(False, mine_ref, other_ref)
+def first_items_kernel(mine_ref, other_ref, rhs_ref, pack_ref, w_out, q_out):
+    row = slice(RANK, RANK + 1)
+    center = jnp.where(parity() == 1, mine_ref[row], other_ref[row])
     ni = w_out.shape[0]
     w = pack_ref[0:ni]
-    prior = dot(jnp.concatenate(split_columns(w - center), 1), rhs, 1, 0)
+    prior = dot(jnp.concatenate(split_columns(w - center), 1), rhs_ref[...], 1, 0)
     q = pack_ref[ni:] + RATE * prior
     q_out[...] = q
     w_out[...] = w + RATE * q
 
 
-def first_items(mine, other, pack):
+def first_items(mine, other, rhs, pack):
     ni, k = pack.shape[0] // 2, pack.shape[1]
-    return call(first_items_kernel, (shape(ni, k),) * 2, [VMEM] * 3)(mine, other, pack)
+    return call(first_items_kernel, (shape(ni, k),) * 2, [VMEM] * 4)(mine, other, rhs, pack)
 
 
 def items_kernel(weight, substep, turn, mask_ref, mine_ref, other_ref, *refs):
@@ -586,10 +595,10 @@
     rows = user_rows // parts
     rts, accs, loaded = [], [], []
     later = [
-        [(0, user_noise), (None, item_momentum), (0, item_noise)],
-        [(1, ratings)],
-        [(1, user_noise), (1, item_noise)],
+        [(0, user_noise)],
+        [(None, item_momentum), (0, item_noise)],
         [(None, wishart_user), (None, wishart_item)],
+        [],
     ]
 
     keep, send, near_u, near_w, near_ratings, near_r, mask = grams(
@@ -632,18 +641,18 @@
     other = swapped(send, 2, blocks)
     while len(rts) < parts:
         part()
-    item_part = item_start(weight, near_w, loaded[0][1], loaded[0][2], accs)
+    item_part = item_start(weight, near_w, *loaded[1], accs)
     other, item_part, *rts = fence((other, item_part, *rts))
     send = lambda array, pairs: lax.ppermute(array, "blk", pairs)
     early = send(item_part, ring)
-    wu, wi = loaded[3]
-    near = (loaded[1][0], *loaded[2])
+    wu, wi = loaded[2]
     counts = (1.0 * user_rows * blocks, 1.0 * item_rows * blocks)
-    drawn = draw(counts, mine, other, wu, wi)
+    later = [(1, x) for x in (ratings, user_noise, item_noise)]
+    drawn, near = draw(counts, mine, other, wu, wi, later)
     peer = swapped(drawn, 1, blocks)
-    users, user_mom = finish(drawn, peer, near_u, rts)
+    users, user_mom, split_item = finish(drawn, peer, near_u, rts)
     users, early = fence((users, early))
-    items, item_mom = first_items(drawn, peer, early)
+    items, item_mom = first_items(drawn, peer, split_item, early)
 
     before = send(items, ring)
     args = (mask, drawn, peer, near[0], users, near[2])

time: 86.4 us -> 86.2 us (level)
  Pallas kernels: 41.5 us -> 40.5 us
    ppermute x6, waiting for transfers between devices: 3.83 us -> 5.64 us  [swapped(): return lax.ppermute(array, 'blk', [(i, i ^ by) for i in range(size)])]
    ppermute x6, waiting for transfers between devices: 14.9 us -> 13.8 us  [local(): send = lambda array, pairs: lax.ppermute(array, 'blk', pairs)]
    pallas_call x18, Pallas kernels: 40.4 us -> 39.4 us  [placed(): run(*(pltpu.with_memory_space_constraint(a, spaces[id(s)]) if id(s) in sp...]
  transfers between devices with their start and end apart: 12 -> 12, of which waited for: 9 -> 9; matrix products, arithmetic and copies ran while one was open for 0% -> 0% of each run, Pallas kernels for 42% -> 41%
where the time goes in v5:
time: 86.2 us; the launch traced here: 85.9 us
  Pallas kernels  40.5 us (47%)
  starting transfers between devices  24.9 us (29%)
  waiting for transfers between devices  19.4 us (23%)
  between operations  0.99 us (1%)
    pallas_call x18, Pallas kernels, placed(): run(*(pltpu.with_memory_space_constraint(a, spaces[id(s)]) if id(s) in sp...  39.4 us
    ppermute x6, starting transfers between devices, local(): send = lambda array, pairs: lax.ppermute(array, 'blk', pairs)  14.8 us
    ppermute x6, waiting for transfers between devices, local(): send = lambda array, pairs: lax.ppermute(array, 'blk', pairs)  13.8 us
    ppermute x6, starting transfers between devices, swapped(): return lax.ppermute(array, 'blk', [(i, i ^ by) for i in range(size)])  10.2 us
    ppermute x6, waiting for transfers between devices, swapped(): return lax.ppermute(array, 'blk', [(i, i ^ by) for i in range(size)])  5.64 us
  transfers between devices with their start and end apart: 12, of which 9 were waited for; matrix products, arithmetic and copies ran while one was open for 0% of the time, Pallas kernels for 41%

profile of v5, /device:TPU:0, one launch (start us, length us, event | category | flops | bytes accessed | tf_op | source)
XLA Modules:
  0.0 85.9 jit_solution(13086798683612601319)
XLA Ops:
  0.6 3.4 %shard_map.145 = (f32[144,256]{1,0:T(8,128)S(1)}, f32[144,256]{1,0:T(8,128)S(1)}, f32[2048,256]{1,0:T(8,128)S(1)}, f32[768,256]{1,0:T(8,128)S(1)}, bf16[2048,768...) custom-call(f32[2048,256]{1,0:T(8,128)} %u_hbm.1, f32[768,256]{1,0:T(8,128)} %w_hbm.1, ...), custom_call_target="tpu_custom_call" | custom-call | flops 1000 | bytes 1000 | tf_op jit(solution)/shard_map/pallas_call | solution.py:64
  4.1 0.5 collective-permute-start
  4.6 1.0 %collective-permute-done.got_ref = f32[144,256]{1,0:T(8,128)S(1)} collective-permute-done((f32[144,256]{1,0:T(8,128)S(1)}, f32[144,256]{1,0:T(8,128)S(1)}, u32[]{:S(2)}, u32[]{:S(2)}) %collective-permute-start) | collective-permute-done | bytes 147488 | tf_op jit(solution)/shard_map/ppermute | solution.py:569
  5.6 2.9 %collective-permute-start.1 = (f32[72,256]{1,0:T(8,128)S(1)}, f32[72,256]{1,0:T(8,128)S(1)}, u32[]{:S(2)}, u32[]{:S(2)}) collective-permute-start(f32[72,256]{1,0:T(8,128)S(1)} %get-tuple-element.96), channel_id=1, source_target_pairs={{0,2},{1,3},{2,0},{3,1},{4,6},{5,7},{6,4},{7,5},{8,10},{9,11},{10,... | collective-permute-start | bytes 221192 | tf_op jit(solution)/shard_map/ppermute | solution.py:569
  8.6 1.8 %shard_map.147 = (f32[512,256]{1,0:T(8,128)S(1)}, f32[256,768]{1,0:T(8,128)S(1)}, bf16[2048,256]{1,0:T(8,128)(2,1)S(1)}) custom-call(s32[3,6,16]{2,1,0:T(8,128)S(1)} %get-tuple-element.90.mask_ref, bf16[2048,768]{1,0:T(8,128)(2,1)S(1)} %get-tuple-element.97.ratings_ref, f32[2048,256]{1,0:T(8,128)S(1)} %get-tuple-element.98.r_ref, ...), custom_call_target="tpu_custom_call" | custom-call | flops 1000 | bytes 1000 | tf_op jit(solution)/shard_map/pallas_call | solution.py:64
  10.3 0.8 collective-permute-done.1.b_ref
  11.2 1.9 %collective-permute-start.2 = (f32[72,256]{1,0:T(8,128)S(1)}, f32[72,256]{1,0:T(8,128)S(1)}, u32[]{:S(2)}, u32[]{:S(2)}) collective-permute-start(f32[72,256]{1,0:T(8,128)S(1)} %shard_map.148.a_ref), channel_id=1, source_target_pairs={{0,4},{1,5},{2,6},{3,7},{4,0},{5,1},{6,2},{7,3},{8,12},{9,13},{10,... | collective-permute-start | bytes 221192 | tf_op jit(solution)/shard_map/ppermute | solution.py:569
  13.1 2.0 %shard_map.149 = (f32[512,256]{1,0:T(8,128)S(1)}, f32[256,768]{1,0:T(8,128)S(1)}, f32[768,256]{1,0:T(8,128)S(1)}, bf16[768,256]{1,0:T(8,128)(2,1)S(1)}) custom-call(s32[3,6,16]{2,1,0:T(8,128)S(1)} %get-tuple-element.90.mask_ref, bf16[2048,768]{1,0:T(8,128)(2,1)S(1)} %get-tuple-element.97.ratings_ref, f32[2048,256]{1,0:T(8,128)S(1)} %get-tuple-element.98.r_ref, ...), custom_call_target="tpu_custom_call" | custom-call | flops 1000 | bytes 1000 | tf_op jit(solution)/shard_map/pallas_call | solution.py:64
  15.0 0.6 collective-permute-done.2.b_ref
  15.6 2.9 %collective-permute-start.3 = (f32[72,256]{1,0:T(8,128)S(1)}, f32[72,256]{1,0:T(8,128)S(1)}, u32[]{:S(2)}, u32[]{:S(2)}) collective-permute-start(f32[72,256]{1,0:T(8,128)S(1)} %shard_map.150.a_ref), channel_id=1, source_target_pairs={{0,8},{1,9},{2,10},{3,11},{4,12},{5,13},{6,14},{7,15},{8,0},{9,1},... | collective-permute-start | bytes 221192 | tf_op jit(solution)/shard_map/ppermute | solution.py:569
  18.5 1.8 %shard_map.151 = (f32[512,256]{1,0:T(8,128)S(1)}, f32[256,768]{1,0:T(8,128)S(1)}, f32[256,256]{1,0:T(8,128)S(1)}, f32[256,256]{1,0:T(8,128)S(1)}) custom-call(s32[3,6,16]{2,1,0:T(8,128)S(1)} %get-tuple-element.90.mask_ref, bf16[2048,768]{1,0:T(8,128)(2,1)S(1)} %get-tuple-element.97.ratings_ref, f32[2048,256]{1,0:T(8,128)S(1)} %get-tuple-element.98.r_ref, ...), custom_call_target="tpu_custom_call" | custom-call | flops 1000 | bytes 1000 | tf_op jit(solution)/shard_map/pallas_call | solution.py:64
  20.3 0.6 collective-permute-done.3.b_ref
  20.9 1.8 %collective-permute-start.4 = (f32[72,256]{1,0:T(8,128)S(1)}, f32[72,256]{1,0:T(8,128)S(1)}, u32[]{:S(2)}, u32[]{:S(2)}) collective-permute-start(f32[72,256]{1,0:T(8,128)S(1)} %shard_map.152.mine_ref), channel_id=1, source_target_pairs={{0,2},{1,3},{2,0},{3,1},{4,6},{5,7},{6,4},{7,5},{8,10},{9,11},{10,... | collective-permute-start | bytes 221192 | tf_op jit(solution)/shard_map/ppermute | solution.py:569
  22.8 1.0 %shard_map.153 = (f32[512,256]{1,0:T(8,128)S(1)}, f32[256,768]{1,0:T(8,128)S(1)}) custom-call(s32[3,6,16]{2,1,0:T(8,128)S(1)} %get-tuple-element.90.mask_ref, bf16[2048,768]{1,0:T(8,128)(2,1)S(1)} %get-tuple-element.97.ratings_ref, f32[2048,256]{1,0:T(8,128)S(1)} %get-tuple-element.98.r_ref, f32[2048,256]{1,0:T(8,128)S(1)} %get-tuple-element.121.u_ref.x_ref, ...), custom_call_target="tpu_custom_call" | custom-call | flops 1000 | bytes 1000 | tf_op jit(solution)/shard_map/pallas_call | solution.py:64
  24.2 1.2 %collective-permute-done.4.other_ref = f32[72,256]{1,0:T(8,128)S(1)} collective-permute-done((f32[72,256]{1,0:T(8,128)S(1)}, f32[72,256]{1,0:T(8,128)S(1)}, u32[]{:S(2)}, u32[]{:S(2)}) %collective-permute-start.4) | collective-permute-done | bytes 73760 | tf_op jit(solution)/shard_map/ppermute | solution.py:569
  25.3 0.8 collective-permute-start.6
  26.1 11.4 %shard_map.155 = (f32[264,256]{1,0:T(8,128)S(1)}, bf16[2048,768]{1,0:T(8,128)(2,1)S(1)}, bf16[2048,256]{1,0:T(8,128)(2,1)S(1)}, bf16[768,256]{1,0:T(8,128)(2,1)S(1)}) custom-call(f32[72,256]{1,0:T(8,128)S(1)} %shard_map.152.mine_ref, f32[72,256]{1,0:T(8,128)S(1)} %collective-permute-done.4.other_ref, f32[256,256]{1,0:T(8,128)S(1)} %get-tuple-element.128.wu_ref, ...), custom_call_target="tpu_custom_call" | custom-call | flops 1000 | bytes 1000 | tf_op jit(solution)/shard_map/pallas_call | solution.py:64
  37.6 1.5 %collective-permute-done.5.other_ref = f32[264,256]{1,0:T(8,128)S(1)} collective-permute-done((f32[264,256]{1,0:T(8,128)S(1)}, f32[264,256]{1,0:T(8,128)S(1)}, u32[]{:S(2)}, u32[]{:S(2)}) %collective-permute-start.5) | collective-permute-done | bytes 270368 | tf_op jit(solution)/shard_map/ppermute | solution.py:569
  39.2 2.3 %shard_map.156 = (f32[2048,256]{1,0:T(8,128)S(1)}, f32[2048,256]{1,0:T(8,128)S(1)}, bf16[1536,256]{1,0:T(8,128)(2,1)S(1)}) custom-call(f32[264,256]{1,0:T(8,128)S(1)} %get-tuple-element.130.mine_ref, f32[264,256]{1,0:T(8,128)S(1)} %collective-permute-done.5.other_ref, f32[2048,256]{1,0:T(8,128)S(1)} %get-tuple-element.121.u_ref.x_ref, ...), custom_call_target="tpu_custom_call" | custom-call | flops 1000 | bytes 1000 | tf_op jit(solution)/shard_map/pallas_call | solution.py:64
  41.5 2.6 %collective-permute-done.6.pack_ref = f32[1536,256]{1,0:T(8,128)S(1)} collective-permute-done((f32[1536,256]{1,0:T(8,128)S(1)}, f32[1536,256]{1,0:T(8,128)S(1)}, u32[]{:S(2)}, u32[]{:S(2)}) %collective-permute-start.6) | collective-permute-done | bytes 1572896 | tf_op jit(solution)/shard_map/ppermute | solution.py:646
  44.1 0.8 shard_map.157
  44.8 4.9 %collective-permute-start.7 = (f32[768,256]{1,0:T(8,128)S(1)}, f32[768,256]{1,0:T(8,128)S(1)}, u32[]{:S(2)}, u32[]{:S(2)}) collective-permute-start(f32[768,256]{1,0:T(8,128)S(1)} %get-tuple-element.139.refs_3_.even_ref.odd_ref), channel_id=1, source_target_pairs={{0,15},{1,0},{2,1},{3,2},{4,3},{5,4},{6,5},{7,6},{8,7},{9,8},{10,9... | collective-permute-start | bytes 2359304 | tf_op jit(solution)/shard_map/ppermute | solution.py:646
  49.7 3.0 %shard_map.158 = (bf16[2048,768]{1,0:T(8,128)(2,1)S(1)}, f32[768,256]{1,0:T(8,128)S(1)}) custom-call(s32[3,6,16]{2,1,0:T(8,128)S(1)} %get-tuple-element.90.mask_ref, f32[264,256]{1,0:T(8,128)S(1)} %get-tuple-element.130.mine_ref, f32[264,256]{1,0:T(8,128)S(1)} %collective-permute-done.5.other_ref, bf16[2048,768]{1,0:T(8,128)(2,1)S(1)} %get-tuple-element.140.refs_0_, ...), custom_call_target="tpu_custom_call" | custom-call | flops 1000 | bytes 1000 | tf_op jit(solution)/shard_map/pallas_call | solution.py:64
  52.8 4.1 %collective-permute-start.10 = (f32[768,256]{1,0:T(8,128)S(1)}, f32[768,256]{1,0:T(8,128)S(1)}, u32[]{:S(2)}, u32[]{:S(2)}) collective-permute-start(f32[768,256]{1,0:T(8,128)S(1)} %get-tuple-element.156), channel_id=1, source_target_pairs={{0,15},{2,1},{4,3},{6,5},{8,7},{10,9},{12,11},{14,13},{16,31},{18,... | collective-permute-start | bytes 2359304 | tf_op jit(solution)/shard_map/ppermute | solution.py:646
  56.9 3.2 %shard_map.159 = (f32[2048,256]{1,0:T(8,128)S(1)}, f32[2048,256]{1,0:T(8,128)S(1)}, bf16[2048,768]{1,0:T(8,128)(2,1)S(1)}, bf16[2048,256]{1,0:T(8,128)(2,1)S(1)}, bf16[768,256]{1,0:T(8,128)(2,1)S(1)}) custom-call(f32[264,256]{1,0:T(8,128)S(1)} %get-tuple-element.130.mine_ref, f32[264,256]{1,0:T(8,128)S(1)} %collective-permute-done.5.other_ref, ...), custom_call_target="tpu_custom_call" | custom-call | flops 1000 | bytes 1000 | tf_op jit(solution)/shard_map/pallas_call | solution.py:64
  60.1 3.0 %shard_map.160 = (bf16[2048,768]{1,0:T(8,128)(2,1)S(1)}, f32[1536,256]{1,0:T(8,128)S(1)}) custom-call(s32[3,6,16]{2,1,0:T(8,128)S(1)} %get-tuple-element.90.mask_ref, f32[264,256]{1,0:T(8,128)S(1)} %get-tuple-element.130.mine_ref, f32[264,256]{1,0:T(8,128)S(1)} %collective-permute-done.5.other_ref, bf16[2048,768]{1,0:T(8,128)(2,1)S(1)} %get-tuple-element.152.refs_0_, ...), custom_call_target="tpu_custom_call" | custom-call | flops 1000 | bytes 1000 | tf_op jit(solution)/shard_map/pallas_call | solution.py:64
  63.1 2.8 %collective-permute-start.9 = (f32[1536,256]{1,0:T(8,128)S(1)}, f32[1536,256]{1,0:T(8,128)S(1)}, u32[]{:S(2)}, u32[]{:S(2)}) collective-permute-start(f32[1536,256]{1,0:T(8,128)S(1)} %get-tuple-element.157.even_ref), channel_id=1, source_target_pairs={{0,15},{2,1},{4,3},{6,5},{8,7},{10,9},{12,11},{14,13},{16,31},{18,... | collective-permute-start | bytes 4718600 | tf_op jit(solution)/shard_map/ppermute | solution.py:646
  65.8 1.8 %collective-permute-done.10.refs_4_ = f32[768,256]{1,0:T(8,128)S(1)} collective-permute-done((f32[768,256]{1,0:T(8,128)S(1)}, f32[768,256]{1,0:T(8,128)S(1)}, u32[]{:S(2)}, u32[]{:S(2)}) %collective-permute-start.10) | collective-permute-done | bytes 786464 | tf_op jit(solution)/shard_map/ppermute | solution.py:646
  67.7 2.2 %collective-permute-start.11 = (f32[1536,256]{1,0:T(8,128)S(1)}, f32[1536,256]{1,0:T(8,128)S(1)}, u32[]{:S(2)}, u32[]{:S(2)}) collective-permute-start(f32[1536,256]{1,0:T(8,128)S(1)} %get-tuple-element.162.odd_ref), channel_id=1, source_target_pairs={{0,1},{1,0},{2,3},{3,2},{4,5},{5,4},{6,7},{7,6},{8,9},{9,8},{10,11... | collective-permute-start | bytes 4718600 | tf_op jit(solution)/shard_map/ppermute | solution.py:646
  69.9 5.2 %shard_map.162 = (f32[2048,256]{1,0:T(8,128)}, f32[2048,256]{1,0:T(8,128)}, f32[256,256]{1,0:T(8,128)}, f32[256,256]{1,0:T(8,128)}) custom-call(f32[264,256]{1,0:T(8,128)S(1)} %get-tuple-element.130.mine_ref, f32[264,256]{1,0:T(8,128)S(1)} %collective-permute-done.5.other_ref, bf16[2048,768]{1,0:T(8,128)(2,1)S(1)} %get-tuple-element.159.res_ref, ...), custom_call_target="tpu_custom_call" | custom-call | flops 1000 | bytes 1000 | tf_op jit(solution)/shard_map/pallas_call | solution.py:64
  75.1 9.4 %collective-permute-done.9.odd_ref = f32[1536,256]{1,0:T(8,128)S(1)} collective-permute-done((f32[1536,256]{1,0:T(8,128)S(1)}, f32[1536,256]{1,0:T(8,128)S(1)}, u32[]{:S(2)}, u32[]{:S(2)}) %collective-permute-start.9) | collective-permute-done | bytes 1572896 | tf_op jit(solution)/shard_map/ppermute | solution.py:646
  84.5 1.2 %shard_map.163 = (f32[768,256]{1,0:T(8,128)}, f32[768,256]{1,0:T(8,128)}) custom-call(f32[1536,256]{1,0:T(8,128)S(1)} %collective-permute-done.11.even_ref, f32[1536,256]{1,0:T(8,128)S(1)} %collective-permute-done.9.odd_ref), custom_call_target="tpu_custom_call" | custom-call | flops 1000 | bytes 1000 | tf_op jit(solution)/shard_map/pallas_call | solution.py:557
  (11 shorter events, 0.6 us)
Async XLA Ops:
  4.1 1.5 %collective-permute-start = (f32[144,256]{1,0:T(8,128)S(1)}, f32[144,256]{1,0:T(8,128)S(1)}, u32[]{:S(2)}, u32[]{:S(2)}) collective-permute-start(f32[144,256]{1,0:T(8,128)S(1)} %get-tuple-element.92), channel_id=1, source_target_pairs={{0,1},{1,0},{2,3},{3,2},{4,5},{5,4},{6,7},{7,6},{8,9},{9,8},{10,11... | collective-permute-start | bytes 442376 | tf_op jit(solution)/shard_map/ppermute | solution.py:569
  5.6 5.5 %collective-permute-start.1 = (f32[72,256]{1,0:T(8,128)S(1)}, f32[72,256]{1,0:T(8,128)S(1)}, u32[]{:S(2)}, u32[]{:S(2)}) collective-permute-start(f32[72,256]{1,0:T(8,128)S(1)} %get-tuple-element.96), channel_id=1, source_target_pairs={{0,2},{1,3},{2,0},{3,1},{4,6},{5,7},{6,4},{7,5},{8,10},{9,11},{10,... | collective-permute-start | bytes 221192 | tf_op jit(solution)/shard_map/ppermute | solution.py:569
  11.2 4.4 %collective-permute-start.2 = (f32[72,256]{1,0:T(8,128)S(1)}, f32[72,256]{1,0:T(8,128)S(1)}, u32[]{:S(2)}, u32[]{:S(2)}) collective-permute-start(f32[72,256]{1,0:T(8,128)S(1)} %shard_map.148.a_ref), channel_id=1, source_target_pairs={{0,4},{1,5},{2,6},{3,7},{4,0},{5,1},{6,2},{7,3},{8,12},{9,13},{10,... | collective-permute-start | bytes 221192 | tf_op jit(solution)/shard_map/ppermute | solution.py:569
  15.6 5.3 %collective-permute-start.3 = (f32[72,256]{1,0:T(8,128)S(1)}, f32[72,256]{1,0:T(8,128)S(1)}, u32[]{:S(2)}, u32[]{:S(2)}) collective-permute-start(f32[72,256]{1,0:T(8,128)S(1)} %shard_map.150.a_ref), channel_id=1, source_target_pairs={{0,8},{1,9},{2,10},{3,11},{4,12},{5,13},{6,14},{7,15},{8,0},{9,1},... | collective-permute-start | bytes 221192 | tf_op jit(solution)/shard_map/ppermute | solution.py:569
  20.9 4.4 %collective-permute-start.4 = (f32[72,256]{1,0:T(8,128)S(1)}, f32[72,256]{1,0:T(8,128)S(1)}, u32[]{:S(2)}, u32[]{:S(2)}) collective-permute-start(f32[72,256]{1,0:T(8,128)S(1)} %shard_map.152.mine_ref), channel_id=1, source_target_pairs={{0,2},{1,3},{2,0},{3,1},{4,6},{5,7},{6,4},{7,5},{8,10},{9,11},{10,... | collective-permute-start | bytes 221192 | tf_op jit(solution)/shard_map/ppermute | solution.py:569
  25.3 18.7 %collective-permute-start.6 = (f32[1536,256]{1,0:T(8,128)S(1)}, f32[1536,256]{1,0:T(8,128)S(1)}, u32[]{:S(2)}, u32[]{:S(2)}) collective-permute-start(f32[1536,256]{1,0:T(8,128)S(1)} %shard_map.154), channel_id=1, source_target_pairs={{0,15},{1,0},{2,1},{3,2},{4,3},{5,4},{6,5},{7,6},{8,7},{9,8},{10,9... | collective-permute-start | bytes 4718600 | tf_op jit(solution)/shard_map/ppermute | solution.py:646
  37.6 1.6 %collective-permute-start.5 = (f32[264,256]{1,0:T(8,128)S(1)}, f32[264,256]{1,0:T(8,128)S(1)}, u32[]{:S(2)}, u32[]{:S(2)}) collective-permute-start(f32[264,256]{1,0:T(8,128)S(1)} %get-tuple-element.130.mine_ref), channel_id=1, source_target_pairs={{0,1},{1,0},{2,3},{3,2},{4,5},{5,4},{6,7},{7,6},{8,9},{9,8},{10,11... | collective-permute-start | bytes 811016 | tf_op jit(solution)/shard_map/ppermute | solution.py:569
  44.8 15.2 %collective-permute-start.7 = (f32[768,256]{1,0:T(8,128)S(1)}, f32[768,256]{1,0:T(8,128)S(1)}, u32[]{:S(2)}, u32[]{:S(2)}) collective-permute-start(f32[768,256]{1,0:T(8,128)S(1)} %get-tuple-element.139.refs_3_.even_ref.odd_ref), channel_id=1, source_target_pairs={{0,15},{1,0},{2,1},{3,2},{4,3},{5,4},{6,5},{7,6},{8,7},{9,8},{10,9... | collective-permute-start | bytes 2359304 | tf_op jit(solution)/shard_map/ppermute | solution.py:646
  52.7 7.4 %collective-permute-start.8 = (f32[768,256]{1,0:T(8,128)S(1)}, f32[768,256]{1,0:T(8,128)S(1)}, u32[]{:S(2)}, u32[]{:S(2)}) collective-permute-start(f32[768,256]{1,0:T(8,128)S(1)} %get-tuple-element.156), channel_id=1, source_target_pairs={{0,1},{1,0},{2,3},{3,2},{4,5},{5,4},{6,7},{7,6},{8,9},{9,8},{10,11... | collective-permute-start | bytes 2359304 | tf_op jit(solution)/shard_map/ppermute | solution.py:646
  52.8 14.8 %collective-permute-start.10 = (f32[768,256]{1,0:T(8,128)S(1)}, f32[768,256]{1,0:T(8,128)S(1)}, u32[]{:S(2)}, u32[]{:S(2)}) collective-permute-start(f32[768,256]{1,0:T(8,128)S(1)} %get-tuple-element.156), channel_id=1, source_target_pairs={{0,15},{2,1},{4,3},{6,5},{8,7},{10,9},{12,11},{14,13},{16,31},{18,... | collective-permute-start | bytes 2359304 | tf_op jit(solution)/shard_map/ppermute | solution.py:646
  63.1 21.4 %collective-permute-start.9 = (f32[1536,256]{1,0:T(8,128)S(1)}, f32[1536,256]{1,0:T(8,128)S(1)}, u32[]{:S(2)}, u32[]{:S(2)}) collective-permute-start(f32[1536,256]{1,0:T(8,128)S(1)} %get-tuple-element.157.even_ref), channel_id=1, source_target_pairs={{0,15},{2,1},{4,3},{6,5},{8,7},{10,9},{12,11},{14,13},{16,31},{18,... | collective-permute-start | bytes 4718600 | tf_op jit(solution)/shard_map/ppermute | solution.py:646
  67.7 16.9 %collective-permute-start.11 = (f32[1536,256]{1,0:T(8,128)S(1)}, f32[1536,256]{1,0:T(8,128)S(1)}, u32[]{:S(2)}, u32[]{:S(2)}) collective-permute-start(f32[1536,256]{1,0:T(8,128)S(1)} %get-tuple-element.162.odd_ref), channel_id=1, source_target_pairs={{0,1},{1,0},{2,3},{3,2},{4,5},{5,4},{6,7},{7,6},{8,9},{9,8},{10,11... | collective-permute-start | bytes 4718600 | tf_op jit(solution)/shard_map/ppermute | solution.py:646
